TPU v7x, 32 devices: a whole 2x2x4 slice. The times are simulated.
32 devices in a mesh: seq: 8 (over z, x), section: 2 (over core), dp: 2 (over y).
Axes of the slice: x: 2, y: 2, z: 4, core: 2. Of those that a mesh axis runs over, the one named last changes fastest.
Arguments:
- queries: bfloat16 [2, 1024, 3584], P('section', 'seq', 'dp'), may hold values from -5 to 5
- key_vectors: bfloat16 [2, 1024, 3584], P('section', 'seq', 'dp'), may hold values from -5 to 5
- value_vectors: bfloat16 [2, 1024, 3584], P('section', 'seq', 'dp'), may hold values from -6 to 6
- out_grad: bfloat16 [2, 1024, 3584], P('section', 'seq', 'dp'), may hold values from -6 to 6
- doc_lengths: int32 [8], replicated, may hold values from 1 to 384, 1024 in all
Outputs:
- query_grad: bfloat16 [2, 1024, 3584], P('section', 'seq', 'dp')
- key_grad: bfloat16 [2, 1024, 3584], P('section', 'seq', 'dp')
- value_grad: bfloat16 [2, 1024, 3584], P('section', 'seq', 'dp')
Inputs may be any that keep to these rules, and one draw needn't show every extreme that they name: `doc_lengths`: the 8 lengths sum to 1024; the longest is exactly 384.
All inputs are finite; a program needn't handle non-finite values.
Results may differ from a plain program's by a relative error of at most 0.024.
Values may be sent and summed in bfloat16 or wider, within the bound.
No kernel may reach another device: no remote copies, remote signals or barrier semaphores. Data moves between devices by JAX's collectives and lax.ppermute only.
A program may use at most 192 MiB of HBM per device.

v0:
```python
import functools
import math
import jax
import jax.numpy as jnp
from jax import lax
from jax.experimental import pallas as pl
from jax.experimental.pallas import tpu as pltpu
from jax.sharding import PartitionSpec as P

HEAD = 224
LANES = 128
FLOOR = -1e30


def pick_slot(stacked, slot):
    return lax.dynamic_index_in_dim(stacked, slot, 0, keepdims=False)


def put_slot(stacked, update, slot):
    return lax.dynamic_update_index_in_dim(stacked, update, slot, 0)


def spread_shards(queries, key_vectors, value_vectors, out_grad, doc_lengths):
    local_rows = queries.shape[1]
    local_width = queries.shape[2]
    head_count = local_width // HEAD
    seq_size = lax.axis_size("seq")
    group = seq_size // head_count
    scaling = HEAD ** (-0.5)

    def spread(matrix):
        shaped = matrix.reshape(local_rows, head_count, 1, HEAD)
        copies = jnp.broadcast_to(shaped, (local_rows, head_count, group, HEAD))
        return copies.reshape(local_rows, seq_size * HEAD)

    query_head, key_head, value_head, cot_head = (
        lax.all_to_all(spread(queries), "seq", split_axis=1, concat_axis=0, tiled=True),
        lax.all_to_all(spread(key_vectors), "seq", split_axis=1, concat_axis=0, tiled=True),
        lax.all_to_all(spread(value_vectors), "seq", split_axis=1, concat_axis=0, tiled=True),
        lax.all_to_all(spread(out_grad), "seq", split_axis=1, concat_axis=0, tiled=True),
    )
    length = key_head.shape[0]
    member = lax.axis_index("seq") % group
    blocks = 2 * group
    block = length // blocks
    bounds = jnp.cumsum(doc_lengths)
    positions = jnp.arange(length, dtype=jnp.int32)
    doc_index = jnp.sum((positions[:, None] >= bounds[None, :]).astype(jnp.int32), axis=1)
    row_list = [member, blocks - 1 - member]
    query_list = []
    cot_list = []
    pos_list = []
    for which in range(2):
        offset = row_list[which] * block
        query_list.append(lax.dynamic_slice_in_dim(query_head, offset, block, 0))
        cot_list.append(lax.dynamic_slice_in_dim(cot_head, offset, block, 0))
        pos_list.append(offset + jnp.arange(block, dtype=jnp.int32))
    query_stack = jnp.stack(query_list)
    cot_stack = jnp.stack(cot_list)
    pos_stack = jnp.stack(pos_list)
    doc_stack = jnp.take(doc_index, pos_stack)
    plan = []
    for number in range(blocks + 1):
        first = number <= member
        slot = jnp.where(first, 0, 1).astype(jnp.int32)
        col_block = jnp.where(first, number, number - member - 1)
        flag = None
        plan.append((slot, col_block, flag))
    row_max = jnp.full((2, block), -jnp.inf, jnp.float32)
    row_sum = jnp.zeros((2, block), jnp.float32)
    stored = []
    for slot, col_block, flag in plan:

        def score_tile(carry, slot=slot, col_block=col_block):
            maxima, totals = carry
            query_rows = pick_slot(query_stack, slot)
            key_rows = lax.dynamic_slice_in_dim(key_head, col_block * block, block, 0)
            col_docs = lax.dynamic_slice_in_dim(doc_index, col_block * block, block, 0)
            col_positions = col_block * block + jnp.arange(block, dtype=jnp.int32)
            raw = jnp.dot(query_rows, key_rows.T, preferred_element_type=jnp.float32) * scaling
            allowed = (pick_slot(doc_stack, slot)[:, None] == col_docs[None, :]) & (
                pick_slot(pos_stack, slot)[:, None] >= col_positions[None, :]
            )
            scores = jnp.where(allowed, raw, -jnp.inf)
            before = pick_slot(maxima, slot)
            after = jnp.maximum(before, jnp.max(scores, axis=1))
            safe = jnp.where(jnp.isfinite(after), after, 0.0)
            total = pick_slot(totals, slot) * jnp.exp(before - safe) + jnp.sum(
                jnp.exp(scores - safe[:, None]), axis=1
            )
            return (scores, put_slot(maxima, after, slot), put_slot(totals, total, slot))

        scores, row_max, row_sum = score_tile((row_max, row_sum))
        stored.append(scores)

    def tile_weights(scores, slot):
        return (
            jnp.exp(scores - pick_slot(row_max, slot)[:, None]) / pick_slot(row_sum, slot)[:, None]
        )

    summed = jnp.zeros((2, block, HEAD), jnp.float32)
    for (slot, col_block, flag), scores in zip(plan, stored):

        def add_values(carry, slot=slot, col_block=col_block, scores=scores):
            rounded = tile_weights(scores, slot).astype(jnp.bfloat16)
            value_rows = lax.dynamic_slice_in_dim(value_head, col_block * block, block, 0)
            term = jnp.dot(rounded, value_rows, preferred_element_type=jnp.float32)
            return put_slot(carry, pick_slot(carry, slot) + term, slot)

        summed = add_values(summed)
    attended = summed.astype(jnp.bfloat16)
    row_dot = jnp.sum(cot_stack.astype(jnp.float32) * attended.astype(jnp.float32), axis=2)
    query_acc = jnp.zeros((2, block, HEAD), jnp.float32)
    key_acc = jnp.zeros((length, HEAD), jnp.float32)
    value_acc = jnp.zeros((length, HEAD), jnp.float32)
    for (slot, col_block, flag), scores in zip(plan, stored):

        def backward_tile(carry, slot=slot, col_block=col_block, scores=scores):
            query_sum, key_sum, value_sum = carry
            weights = tile_weights(scores, slot)
            rounded = weights.astype(jnp.bfloat16)
            query_rows = pick_slot(query_stack, slot)
            cot_rows = pick_slot(cot_stack, slot)
            start = col_block * block
            key_rows = lax.dynamic_slice_in_dim(key_head, start, block, 0)
            value_rows = lax.dynamic_slice_in_dim(value_head, start, block, 0)
            value_term = jnp.dot(rounded.T, cot_rows, preferred_element_type=jnp.float32)
            prob_grad = jnp.dot(cot_rows, value_rows.T, preferred_element_type=jnp.float32)
            score_grad = (
                weights * (prob_grad - pick_slot(row_dot, slot)[:, None]) * scaling
            ).astype(jnp.bfloat16)
            query_term = jnp.dot(score_grad, key_rows, preferred_element_type=jnp.float32)
            key_term = jnp.dot(score_grad.T, query_rows, preferred_element_type=jnp.float32)
            query_sum = put_slot(query_sum, pick_slot(query_sum, slot) + query_term, slot)
            key_sum = lax.dynamic_update_slice_in_dim(
                key_sum, lax.dynamic_slice_in_dim(key_sum, start, block, 0) + key_term, start, 0
            )
            value_sum = lax.dynamic_update_slice_in_dim(
                value_sum,
                lax.dynamic_slice_in_dim(value_sum, start, block, 0) + value_term,
                start,
                0,
            )
            return (query_sum, key_sum, value_sum)

        query_acc, key_acc, value_acc = backward_tile((query_acc, key_acc, value_acc))
    query_rounded = query_acc.astype(jnp.bfloat16)
    key_back, value_back = (
        lax.all_to_all(key_acc, "seq", split_axis=0, concat_axis=1, tiled=True),
        lax.all_to_all(value_acc, "seq", split_axis=0, concat_axis=1, tiled=True),
    )

    def settle(received):
        shaped = received.astype(jnp.float32).reshape(local_rows, head_count, group, HEAD)
        return jnp.sum(shaped, axis=2).reshape(1, local_rows, local_width).astype(jnp.bfloat16)

    query_full = jnp.zeros((length, HEAD), jnp.bfloat16)
    for which in range(2):
        query_full = lax.dynamic_update_slice_in_dim(
            query_full, query_rounded[which], row_list[which] * block, 0
        )
    query_back = lax.all_to_all(query_full, "seq", split_axis=0, concat_axis=1, tiled=True)
    query_out = settle(query_back)
    return (query_out, settle(key_back), settle(value_back))


NT = ((1,), (1,))
NN = ((1,), (0,))
TN = ((0,), (0,))
GROUP = 8


def head_span(head):
    low = head * HEAD // LANES * LANES
    high = -(-(head + 1) * HEAD // LANES) * LANES
    return low, high


def head_mask(head):
    low, high = head_span(head)
    lane = lax.broadcasted_iota(jnp.int32, (1, high - low), 1) + low
    inside = (lane >= head * HEAD) & (lane < (head + 1) * HEAD)
    return inside.astype(jnp.float32).astype(jnp.bfloat16)


def matmul(left, right, dims):
    return lax.dot_general(left, right, (dims, ((), ())), preferred_element_type=jnp.float32)


def stack(values, axis):
    return values[0] if len(values) == 1 else jnp.concatenate(values, axis=axis)


def allowed(lengths_ref, rows, query_block, key_block):
    shape = (rows, rows)
    position = query_block * rows + lax.broadcasted_iota(jnp.int32, shape, 1)
    keys = key_block * rows + lax.broadcasted_iota(jnp.int32, shape, 0)
    start = jnp.zeros_like(position)
    bound = jnp.int32(0)
    for doc in range(lengths_ref.shape[0]):
        bound = bound + lengths_ref[doc]
        start = jnp.where(position >= bound, bound, start)
    return (keys >= start) & (keys <= position)


def make_tile(lengths_ref, rows, queries, keys):
    mask = stack(
        [stack([allowed(lengths_ref, rows, q, k) for _, q in queries], 1) for _, k in keys], 0
    )
    return [slot for slot, _ in queries], [slot for slot, _ in keys], mask


def tile_values(plan, head, queries, keys, products):
    low, high = head_span(head)
    keep = head_mask(head)

    def gather(refs, number, slots):
        return stack([refs[slot][number][0, :, low:high] for slot in slots], 0)

    out = []
    for query_slots, key_slots, _ in plan:
        q = [gather(queries, number, query_slots) for number in range(products)]
        k = [gather(keys, number, key_slots) * keep for number in range(products)]
        out.append((q, k, [matmul(b, a, NT) for a, b in zip(q, k)]))
    return out, keep


def tiles_ahead(heads, plan, queries, keys, products):
    ready = tile_values(plan, 0, queries, keys, products)
    for head in range(heads):
        now = ready
        if head + 1 < heads:
            ready = tile_values(plan, head + 1, queries, keys, products)
        yield head, now


def pair_tile(lengths_ref, rows, me):
    mate = me + 1 - 2 * lax.rem(me, 2)
    return make_tile(lengths_ref, rows, ((0, me), (1, mate)), ((0, me), (1, me - 2)))


def third_tile(third, lengths_ref, rows, me):
    slots, keys, mask = make_tile(lengths_ref, rows, ((2, me + 1),), ((1, me - 2),))
    return slots, keys, mask & (me == third)


def tile_plan(third, lengths_ref, rows, me):
    plan = [pair_tile(lengths_ref, rows, me)]
    return plan if third is None else plan + [third_tile(third, lengths_ref, rows, me)]


def lane_cut(value, number, rows):
    return value[:, number * rows : (number + 1) * rows]


def row_of(group, kinds, kind, head):
    return pl.ds((group * kinds + kind) * GROUP + head, 1)


def per_query(slots, kinds, kind, head, ref):
    return stack([ref[row_of(slot, kinds, kind, head), :] for slot in slots], 1)


def collect_stats(heads, power, step, plan, queries, keys, rows, out_ref, groups):
    for head, (tiles, _) in tiles_ahead(heads, plan, queries, keys, 1):
        for (query_slots, _, mask), (_, _, (raw,)) in zip(plan, tiles):
            raw = jnp.where(mask, raw, FLOOR)
            top = jnp.max(raw, axis=0, keepdims=True)
            sums = jnp.sum(jnp.exp2((raw - top) * power), axis=0, keepdims=True)
            for number, slot in enumerate(query_slots):
                at = step * heads + head
                out_ref[row_of(groups[slot], 2, 0, at), :] = lane_cut(top, number, rows)
                out_ref[row_of(groups[slot], 2, 1, at), :] = lane_cut(sums, number, rows)


def stats_kernel(
    heads, power, place_ref, lengths_ref, q_own, q_mate, k_own, k_back, o_own, v_own, o_copy, v_copy, out_ref
):
    rows, me, step = k_own.shape[1], place_ref[0], pl.program_id(0)
    o_copy[...], v_copy[...] = o_own[...], v_own[...]
    plan = [pair_tile(lengths_ref, rows, me)]
    queries, keys = ((q_own,), (q_mate,)), ((k_own,), (k_back,))
    collect_stats(heads, power, step, plan, queries, keys, rows, out_ref, (0, 1))


def third_stats_kernel(third, heads, power, place_ref, lengths_ref, q_third, k_back, out_ref):
    rows, me, step = k_back.shape[1], place_ref[0], pl.program_id(0)
    plan = [third_tile(third, lengths_ref, rows, me)]
    queries, keys = (None, None, (q_third,)), (None, (k_back,))
    collect_stats(heads, power, step, plan, queries, keys, rows, out_ref, (None, None, 0))


def part_of(ref, kinds, number):
    size = kinds * GROUP
    return ref[number * size : (number + 1) * size, :]


def stats_parts(mine, sent, extra):
    own = [part_of(mine, 2, 0), part_of(sent, 2, 1)]
    mate = [part_of(mine, 2, 1), part_of(sent, 2, 0)]
    if not extra:
        return [own, mate]
    third, near, far, even, odd = extra
    return [own + [near[...]], mate + [far[...]], [third[...], part_of(even, 2, 0), part_of(odd, 2, 1)]]


def dots_parts(mine, sent, extra):
    own = [part_of(mine, 1, 0), part_of(sent, 1, 1)]
    mate = [part_of(mine, 1, 1), part_of(sent, 1, 0)]
    if not extra:
        return [own, mate]
    near, far = extra
    return [
        own + [part_of(near, 1, 2)],
        mate + [part_of(far, 1, 2)],
        [part_of(mine, 1, 2), part_of(near, 1, 0), part_of(far, 1, 1)],
    ]


def merge_stats(scaling, parts):
    split = [(jnp.where(p[GROUP:] > 0, p[:GROUP], FLOOR), p[GROUP:]) for p in parts]
    top = functools.reduce(jnp.maximum, [s[0] for s in split])
    total = sum(jnp.exp((s[0] - top) * scaling) * s[1] for s in split)
    return top + jnp.log(jnp.where(total > 0, total, 1.0)) / scaling


class Emitter:
    def __init__(self, outs):
        self.outs, self.carry = outs, {}

    def emit(self, head, name, value):
        ref = self.outs[name]
        low, high = head_span(head)
        first, last = head * HEAD % LANES == 0, (head + 1) * HEAD % LANES == 0
        start, stop = low, high
        if not first:
            shared = value[:, :LANES] + self.carry.pop(name)
            ref[0, :, low : low + LANES] = shared.astype(jnp.bfloat16)
            start = low + LANES
        if not last:
            self.carry[name] = value[:, high - LANES - low :]
            stop = high - LANES
        if stop > start:
            ref[0, :, start:stop] = value[:, start - low : stop - low].astype(jnp.bfloat16)


def add_rows(sums, kind, slots, value, rows):
    for number, slot in enumerate(slots):
        piece = value[number * rows : (number + 1) * rows]
        name = (kind, slot)
        sums[name] = sums[name] + piece if name in sums else piece


def split_refs(third, refs):
    count = 2 if third is None else 3
    queries = [(refs[2 * n], refs[2 * n + 1]) for n in range(count)]
    keys = [(refs[2 * n], refs[2 * n + 1]) for n in range(count, count + 2)]
    return queries, keys, refs[2 * count + 4 :]


def values_kernel(third, heads, scaling, power, place_ref, lengths_ref, *refs):
    count, last = (2, -3) if third is None else (3, -4)
    queries = [(refs[2 * n], refs[2 * n + 1]) for n in range(count)]
    refs, outs = refs[2 * count : last], refs[last:]
    keys, shift_ref = [(refs[0],), (refs[1],)], outs[-1]
    rows, me, step = keys[0][0].shape[1], place_ref[0], pl.program_id(0)
    plan = tile_plan(third, lengths_ref, rows, me)
    for number, parts in enumerate(stats_parts(refs[2], refs[3], refs[4:])):
        shift_ref[number * GROUP : (number + 1) * GROUP, :] = merge_stats(scaling, parts)
    out = Emitter(dict(zip((("v", 0), ("v", 1), ("b", 2)), outs[:-1])))
    for head, (tiles, keep) in tiles_ahead(heads, plan, queries, keys, 1):
        low, high = head_span(head)
        sums = {}
        for (query_slots, key_slots, mask), (_, (k,), (raw,)) in zip(plan, tiles):
            shift = per_query(query_slots, 1, 0, step * heads + head, shift_ref)
            weight = jnp.where(mask, jnp.exp2((raw - shift) * power), 0.0).astype(jnp.bfloat16)
            o = stack([queries[slot][1][0, :, low:high] for slot in query_slots], 0) * keep
            add_rows(sums, "v", key_slots, matmul(weight, o, NN), rows)
            if query_slots == [2]:
                add_rows(sums, "b", query_slots, matmul(weight, k, TN), rows)
        for name, value in sums.items():
            out.emit(head, name, value)


def dots_kernel(third, heads, power, place_ref, lengths_ref, *refs):
    queries, keys, (shift_ref, *outs) = split_refs(third, refs)
    dots_ref = outs[-1]
    rows, me, step = keys[0][0].shape[1], place_ref[0], pl.program_id(0)
    plan = tile_plan(third, lengths_ref, rows, me)
    out = Emitter(dict(zip((("a", 2),), outs[:-1])))
    for head, (tiles, _) in tiles_ahead(heads, plan, queries, keys, 2):
        at = step * heads + head
        for (query_slots, _, mask), (_, (k, _), (raw, grads)) in zip(plan, tiles):
            shift = per_query(query_slots, 1, 0, at, shift_ref)
            product = jnp.where(mask, jnp.exp2((raw - shift) * power), 0.0) * grads
            dots = jnp.sum(product, axis=0, keepdims=True)
            for number, slot in enumerate(query_slots):
                dots_ref[row_of(slot, 1, 0, at), :] = lane_cut(dots, number, rows)
            if query_slots == [2]:
                out.emit(head, ("a", 2), matmul(product.astype(jnp.bfloat16), k, TN))


def keys_kernel(third, heads, scaling, power, place_ref, lengths_ref, *refs):
    queries, keys, refs = split_refs(third, refs)
    (shift_ref, mine, sent, *extra), outs = refs[:-5], refs[-5:]
    total_ref = outs[-1]
    rows, me, step = keys[0][0].shape[1], place_ref[0], pl.program_id(0)
    plan = tile_plan(third, lengths_ref, rows, me)
    for number, parts in enumerate(dots_parts(mine, sent, extra)):
        total_ref[number * GROUP : (number + 1) * GROUP, :] = sum(parts)
    out = Emitter(dict(zip((("k", 0), ("k", 1), ("q", 0), ("q", 1)), outs[:-1])))
    for head, (tiles, keep) in tiles_ahead(heads, plan, queries, keys, 2):
        at = step * heads + head
        sums = {}
        for (query_slots, key_slots, mask), ((q, _), (k, _), (raw, grads)) in zip(plan, tiles):
            shift = per_query(query_slots, 1, 0, at, shift_ref)
            dots = per_query(query_slots, 1, 0, at, total_ref)
            weight = jnp.where(mask, jnp.exp2((raw - shift) * power), 0.0)
            slope = (weight * (grads - dots) * scaling).astype(jnp.bfloat16)
            add_rows(sums, "k", key_slots, matmul(slope, q * keep, NN), rows)
            if query_slots != [2]:
                add_rows(sums, "q", query_slots, matmul(slope, k, TN), rows)
        for name, value in sums.items():
            out.emit(head, name, value)


def add_refs(*refs):
    return sum(ref[...].astype(jnp.float32) for ref in refs)


def sums_kernel(key_part, key_sent, query_part, query_sent, key_out, query_out):
    key_out[...] = add_refs(key_part, key_sent).astype(jnp.bfloat16)
    query_out[...] = add_refs(query_part, query_sent).astype(jnp.bfloat16)


def third_sums_kernel(
    heads, scaling, key_part, key_sent, query_part, query_sent, a_sent, b_sent, total_ref, key_out, query_out
):
    key_out[...] = add_refs(key_part, key_sent).astype(jnp.bfloat16)
    step = pl.program_id(0)
    rows, part = query_out.shape[1:]
    spread = total_ref[pl.ds(pl.multiple_of(step * GROUP, GROUP), GROUP), :]
    columns = jnp.concatenate([spread, jnp.zeros((LANES - GROUP, rows), jnp.float32)], 0).T
    lane = lax.broadcasted_iota(jnp.int32, (rows, part), 1)
    dots = jnp.zeros((rows, part), jnp.float32)
    for head in range(heads):
        inside = (lane >= head * HEAD) & (lane < (head + 1) * HEAD)
        dots = jnp.where(inside, columns[:, head : head + 1], dots)
    extra = (a_sent[0].astype(jnp.float32) - dots * b_sent[0].astype(jnp.float32)) * scaling
    query_out[0] = (add_refs(query_part, query_sent)[0] + extra).astype(jnp.bfloat16)


def halo_program(third, queries, key_vectors, value_vectors, out_grad, doc_lengths):
    _, rows, width = queries.shape
    seq_size = lax.axis_size("seq")
    me = lax.axis_index("seq").astype(jnp.int32)
    scaling = HEAD ** (-0.5)
    power = scaling * math.log2(math.e)
    steps = width // HEAD // 4
    part = width // steps
    heads = part // HEAD
    count = 2 if third is None else 3
    devices = range(seq_size)
    mates = [(s, s ^ 1) for s in devices]
    ring = third is None
    chain = [(s, s + 2) for s in devices if s + 2 < seq_size]
    ahead = [(s, (s + 2) % seq_size) for s in devices] if ring else chain
    behind = [(s, s - 2) for s in devices if s >= 2]
    if not ring:
        relay, to_odd = [(third + 2, third)], [(third, third + 2)]
        from_even, to_even = [(third + 1, third)], [(third, third + 1)]
        near, far = from_even + to_even, relay + to_odd

    def send(value, pairs):
        return lax.ppermute(value, "seq", pairs)

    smem = pl.BlockSpec(memory_space=pltpu.SMEM)
    wide = pl.BlockSpec((1, rows, part), lambda step: (0, 0, step))
    wide_shape = jax.ShapeDtypeStruct((1, rows, width), jnp.bfloat16)

    def slim(groups, kinds):
        return pl.BlockSpec((groups * kinds * GROUP, rows), lambda step: (0, 0))

    def slim_shape(groups, kinds):
        return jax.ShapeDtypeStruct((groups * kinds * GROUP, rows), jnp.float32)

    def call(kernel, products, wides, slims, outs, slim_outs, plain=False):
        flops = 2 * products * 4 * rows * rows * width * 3 // 2
        lead = [] if plain else [me[None], doc_lengths]
        return pl.pallas_call(
            kernel,
            grid=(steps,),
            in_specs=[smem] * len(lead)
            + [wide] * len(wides)
            + [slim(groups, kinds) for groups, kinds, _ in slims],
            out_specs=[wide] * outs + [slim(*sizes) for sizes in slim_outs],
            out_shape=[wide_shape] * outs + [slim_shape(*sizes) for sizes in slim_outs],
            compiler_params=pltpu.CompilerParams(vmem_limit_bytes=20 * 1024 * 1024),
            cost_estimate=pl.CostEstimate(
                flops=flops, bytes_accessed=20 * rows * width, transcendentals=0
            ),
        )(*lead, *wides, *[value for _, _, value in slims])

    query_mate = send(queries, mates)
    key_back = send(key_vectors, chain)
    grad_mate = send(out_grad, mates)
    value_back = send(value_vectors, ahead)
    query_rows, grad_rows = [queries, query_mate], [out_grad, grad_mate]
    grad_own, value_own, stats = call(
        functools.partial(stats_kernel, heads, power), 1,
        [*query_rows, key_vectors, key_back, out_grad, value_vectors], [], 2, [(2, 2)],
    )
    stats_in = [(2, 2, stats), (2, 2, send(stats, mates))]
    grad_rows[0] = grad_own
    if not ring:
        query_rows.append(send(query_mate, relay))
        held, _ = lax.optimization_barrier((grad_mate, stats))
        grad_rows.append(send(held, relay))
        query_third, _ = lax.optimization_barrier((query_rows[2], value_back))
        (third_stats,) = call(
            functools.partial(third_stats_kernel, third, heads, power), 1,
            [query_third, key_back], [], 0, [(1, 2)],
        )
        stats_in += [(1, 2, third_stats), (1, 2, send(third_stats, to_even)), (1, 2, send(third_stats, to_odd))]
        stats_in += [(2, 2, send(stats, from_even)), (2, 2, send(stats, relay))]
    tensors = [t for two in zip(query_rows, grad_rows) for t in two]
    value_part, value_sent, *weighted, shift = call(
        functools.partial(values_kernel, third, heads, scaling, power), 2,
        tensors + [key_vectors, key_back], stats_in, count, [(count, 1)],
    )
    tensors += [key_vectors, value_own, key_back, value_back]
    *graded, dots = call(
        functools.partial(dots_kernel, third, heads, power), 2, tensors, [(count, 1, shift)],
        count - 2, [(count, 1)],
    )
    value_received = send(value_sent, behind)
    dots_in = [(count, 1, shift), (count, 1, dots), (count, 1, send(dots, mates))]
    if not ring:
        dots_in += [(count, 1, send(dots, pairs)) for pairs in (near, far)]
    key_part, key_sent, query_part, query_sent, totals = call(
        functools.partial(keys_kernel, third, heads, scaling, power), 4, tensors, dots_in,
        4, [(count, 1)],
    )
    key_received = send(key_sent, behind)
    query_received = send(query_sent, mates)
    value_ready = (value_part.astype(jnp.float32) + value_received.astype(jnp.float32)).astype(jnp.bfloat16)
    sums = [key_part, key_received, query_part, query_received]
    if ring:
        key_ready, query_ready = call(sums_kernel, 0, sums, [], 2, [], plain=True)
    else:
        sums += [send(graded[0], to_even), send(weighted[0], to_even)]
        by_step = totals[:GROUP].reshape(steps, heads, rows)
        by_step = jnp.pad(by_step, ((0, 0), (0, GROUP - heads), (0, 0))).reshape(steps * GROUP, rows)
        key_ready, query_ready = call(
            functools.partial(third_sums_kernel, heads, scaling), 0, sums, [(steps, 1, by_step)], 2, [],
            plain=True,
        )
    return query_ready, key_ready, value_ready


def program_index(rows, doc_lengths):
    count = doc_lengths.shape[0]
    ends = sum(lax.pad(doc_lengths[: count - n], jnp.int32(0), [(n, 0, 0)]) for n in range(count))
    shift = rows.bit_length() - 1
    first, last = (ends - doc_lengths) >> shift, (ends - 1) >> shift
    spans = (last - first >= 3) & (last & 1 == 0)
    return jnp.sum(jnp.where(spans, (last >> 1) - 1, 0))


def halo_shards(*arguments):
    rows, doc_lengths = arguments[0].shape[1], arguments[-1]
    thirds = range(3, lax.axis_size("seq") - 2, 2)
    programs = [functools.partial(halo_program, third) for third in (None, *thirds)]
    return lax.switch(program_index(rows, doc_lengths), programs, *arguments)


def shards(queries, key_vectors, value_vectors, out_grad, doc_lengths):
    _, rows, width = queries.shape
    seq_size = lax.axis_size("seq")
    longest = rows * seq_size * 3 // 8
    fits = longest <= 3 * rows and seq_size % 2 == 0 and seq_size > 4 and rows == LANES
    heads = width // HEAD
    plan = halo_shards if fits and heads % 4 == 0 and heads <= GROUP else spread_shards
    return plan(queries, key_vectors, value_vectors, out_grad, doc_lengths)


def solution(mesh):
    return jax.shard_map(
        shards,
        mesh=mesh,
        in_specs=(
            P("section", "seq", "dp"),
            P("section", "seq", "dp"),
            P("section", "seq", "dp"),
            P("section", "seq", "dp"),
            P(),
        ),
        out_specs=(P("section", "seq", "dp"), P("section", "seq", "dp"), P("section", "seq", "dp")),
        check_vma=False,
    )
```

profile of v0, /device:TPU:0, one launch (start us, length us, event | category | flops | bytes accessed | tf_op | source)
XLA Modules:
  0.0 53.9 jit_solution(10432559301071049049)
XLA Ops:
  0.6 0.6 %copy-done.6 = s32[8]{0:T(128)S(1)} copy-done((s32[8]{0:T(128)S(1)}, s32[8]{0:T(128)}, u32[]{:S(2)}) %copy-start.6) | copy-done | bytes 56
  1.3 0.7 %fusion = s32[]{:T(128)} fusion(s32[8]{0:T(128)S(1)} %copy-done.6, s32[1]{0:T(128)S(1)} %bitcast.16, s32[2]{0:T(128)S(1)} %bitcast.17, s32[3]{0:T(128)S(1)} %bitcast.18, s32[4]{0:T(128)S(1)} %bitcast.19, s32[5]{0:T(128)S(1)} %bitcast.20, s32[6]{0:T(128)S(1)} %bitcast.21, s32[7]{0:T(128)S(1)} %bitcast.22), kind=kLoop, calls=%fused_computation.6 | loop fusion | flops 159 | bytes 148 | tf_op jit(solution)/shard_map/reduce_sum | solution.py:567
  2.7 51.2 %conditional.4 = (bf16[1,128,1792]{2,1,0:T(8,128)(2,1)}, bf16[1,128,1792]{2,1,0:T(8,128)(2,1)}, bf16[1,128,1792]{2,1,0:T(8,128)(2,1)}) conditional(s32[]{:T(128)} %clamp.3, (bf16[1,128,1792]{2,1,0:T(8,128)(2,1)}, bf16[1,128,1792]{2,1,0:T(8,128)(2,1)}, s32[8]{0:T(128)S(1)}, bf16[1,128,1792]{2,1,0:T(8,128)(2,1)}, ...), branch_computations={%region_1.2_spmd, %region_2.3_spmd, %region_3.4_spmd} | conditional | flops 3524132864 | bytes 53187432
  2.7 3.0 %collective-permute-start = (bf16[1,128,1792]{2,1,0:T(8,128)(2,1)}, bf16[1,128,1792]{2,1,0:T(8,128)(2,1)S(1)}, u32[]{:S(2)}, u32[]{:S(2)}) collective-permute-start(bf16[1,128,1792]{2,1,0:T(8,128)(2,1)} %get-tuple-element.41.q_own.refs_0_), channel_id=1, source_target_pairs={{0,4},{4,0},{8,12},{12,8},{16,20},{20,16},{24,28},{28,24},{1,5},{5... | collective-permute-start | bytes 1376264 | tf_op jit(solution)/shard_map/cond/branch_0_fun/ppermute | solution.py:475
  5.7 3.5 %collective-permute-start.1 = (bf16[1,128,1792]{2,1,0:T(8,128)(2,1)}, bf16[1,128,1792]{2,1,0:T(8,128)(2,1)S(1)}, u32[]{:S(2)}, u32[]{:S(2)}) collective-permute-start(bf16[1,128,1792]{2,1,0:T(8,128)(2,1)} %get-tuple-element.42.k_own.refs_4_), channel_id=1, source_target_pairs={{0,8},{4,12},{8,16},{12,20},{16,24},{20,28},{1,9},{5,13},{9,17},{1... | collective-permute-start | bytes 1376264 | tf_op jit(solution)/shard_map/cond/branch_0_fun/ppermute | solution.py:475
  9.2 0.6 %collective-permute-start.2 = (bf16[1,128,1792]{2,1,0:T(8,128)(2,1)}, bf16[1,128,1792]{2,1,0:T(8,128)(2,1)S(1)}, u32[]{:S(2)}, u32[]{:S(2)}) collective-permute-start(bf16[1,128,1792]{2,1,0:T(8,128)(2,1)} %get-tuple-element.43.o_own), channel_id=1, source_target_pairs={{0,4},{4,0},{8,12},{12,8},{16,20},{20,16},{24,28},{28,24},{1,5},{5... | collective-permute-start | bytes 1376264 | tf_op jit(solution)/shard_map/cond/branch_0_fun/ppermute | solution.py:475
  9.8 1.6 %collective-permute-start.3 = (bf16[1,128,1792]{2,1,0:T(8,128)(2,1)}, bf16[1,128,1792]{2,1,0:T(8,128)(2,1)S(1)}, u32[]{:S(2)}, u32[]{:S(2)}) collective-permute-start(bf16[1,128,1792]{2,1,0:T(8,128)(2,1)} %get-tuple-element.44.v_own), channel_id=1, source_target_pairs={{0,8},{4,12},{8,16},{12,20},{16,24},{20,28},{24,0},{28,4},{1,9},{5... | collective-permute-start | bytes 1376264 | tf_op jit(solution)/shard_map/cond/branch_0_fun/ppermute | solution.py:475
  11.4 5.9 %collective-permute-done.q_mate.refs_2_ = bf16[1,128,1792]{2,1,0:T(8,128)(2,1)S(1)} collective-permute-done((bf16[1,128,1792]{2,1,0:T(8,128)(2,1)}, bf16[1,128,1792]{2,1,0:T(8,128)(2,1)S(1)}, u32[]{:S(2)}, u32[]{:S(2)}) %collective-permute-start) | collective-permute-done | bytes 458784 | tf_op jit(solution)/shard_map/cond/branch_0_fun/ppermute | solution.py:475
  17.3 3.2 %collective-permute-done.1.k_back.refs_5_.refs_6_ = bf16[1,128,1792]{2,1,0:T(8,128)(2,1)S(1)} collective-permute-done((bf16[1,128,1792]{2,1,0:T(8,128)(2,1)}, bf16[1,128,1792]{2,1,0:T(8,128)(2,1)S(1)}, u32[]{:S(2)}, u32[]{:S(2)}) %collective-permute-start.1) | collective-permute-done | bytes 458784 | tf_op jit(solution)/shard_map/cond/branch_0_fun/ppermute | solution.py:475
  20.4 2.6 %branch_0_fun.5 = (bf16[1,128,1792]{2,1,0:T(8,128)(2,1)S(1)}, bf16[1,128,1792]{2,1,0:T(8,128)(2,1)S(1)}, f32[32,128]{1,0:T(8,128)S(1)}) custom-call(s32[1]{0:T(128)} %bitcast.place_ref, s32[8]{0:T(128)S(1)} %get-tuple-element.40.lengths_ref, bf16[1,128,1792]{2,1,0:T(8,128)(2,1)} %get-tuple-element.41.q_own.refs_0_, ...), custom_call_target="tpu_custom_call" | custom-call | flops 352321536 | bytes 4587520 | tf_op jit(solution)/shard_map/cond/branch_0_fun/pallas_call | solution.py:490
  23.0 0.6 %collective-permute-start.4 = (f32[32,128]{1,0:T(8,128)S(1)}, f32[32,128]{1,0:T(8,128)S(1)}, u32[]{:S(2)}, u32[]{:S(2)}) collective-permute-start(f32[32,128]{1,0:T(8,128)S(1)} %get-tuple-element.47.refs_6_), channel_id=1, source_target_pairs={{0,4},{4,0},{8,12},{12,8},{16,20},{20,16},{24,28},{28,24},{1,5},{5... | collective-permute-start | bytes 49160 | tf_op jit(solution)/shard_map/cond/branch_0_fun/ppermute | solution.py:475
  23.6 2.8 %collective-permute-done.2.refs_3_ = bf16[1,128,1792]{2,1,0:T(8,128)(2,1)S(1)} collective-permute-done((bf16[1,128,1792]{2,1,0:T(8,128)(2,1)}, bf16[1,128,1792]{2,1,0:T(8,128)(2,1)S(1)}, u32[]{:S(2)}, u32[]{:S(2)}) %collective-permute-start.2) | collective-permute-done | bytes 458784 | tf_op jit(solution)/shard_map/cond/branch_0_fun/ppermute | solution.py:475
  26.4 0.4 collective-permute-done.4.refs_7_
  26.8 2.2 %branch_0_fun.6 = (bf16[1,128,1792]{2,1,0:T(8,128)(2,1)S(1)}, bf16[1,128,1792]{2,1,0:T(8,128)(2,1)S(1)}, f32[16,128]{1,0:T(8,128)S(1)}) custom-call(s32[1]{0:T(128)} %bitcast.place_ref, s32[8]{0:T(128)S(1)} %get-tuple-element.40.lengths_ref, bf16[1,128,1792]{2,1,0:T(8,128)(2,1)S(1)} %copy-done, bf16[1,128,1792]{2,1,0:T(8,128)(2,1)S(1)} %get-tuple-element.45.refs_1_, ...), custom_call_target="tpu_custom_call" | custom-call | flops 704643072 | bytes 4587520 | tf_op jit(solution)/shard_map/cond/branch_0_fun/pallas_call | solution.py:490
  29.1 1.3 %collective-permute-start.8 = (bf16[1,128,1792]{2,1,0:T(8,128)(2,1)S(1)}, bf16[1,128,1792]{2,1,0:T(8,128)(2,1)S(1)}, u32[]{:S(2)}, u32[]{:S(2)}) collective-permute-start(bf16[1,128,1792]{2,1,0:T(8,128)(2,1)S(1)} %get-tuple-element.56), channel_id=1, source_target_pairs={{8,0},{12,4},{16,8},{20,12},{24,16},{28,20},{9,1},{13,5},{17,9},{2... | collective-permute-start | bytes 1376264 | tf_op jit(solution)/shard_map/cond/branch_0_fun/ppermute | solution.py:475
  30.4 2.1 %branch_0_fun.7.refs_9_ = f32[16,128]{1,0:T(8,128)S(1)} custom-call(s32[1]{0:T(128)} %bitcast.place_ref, s32[8]{0:T(128)S(1)} %get-tuple-element.40.lengths_ref, bf16[1,128,1792]{2,1,0:T(8,128)(2,1)S(1)} %copy-done, bf16[1,128,1792]{2,1,0:T(8,128)(2,1)S(1)} %get-tuple-element.45.refs_1_, bf16[1,128,1792]{2,1,0:T(8,128)(2,1)S(1)} %collective-permute-done.q_mate.refs_2_, ...), custom_call_target="tpu_custom_call" | custom-call | flops 704643072 | bytes 4587520 | tf_op jit(solution)/shard_map/cond/branch_0_fun/pallas_call | solution.py:490
  32.5 1.6 %collective-permute-start.5 = (f32[16,128]{1,0:T(8,128)S(1)}, f32[16,128]{1,0:T(8,128)S(1)}, u32[]{:S(2)}, u32[]{:S(2)}) collective-permute-start(f32[16,128]{1,0:T(8,128)S(1)} %branch_0_fun.7.refs_9_), channel_id=1, source_target_pairs={{0,4},{4,0},{8,12},{12,8},{16,20},{20,16},{24,28},{28,24},{1,5},{5... | collective-permute-start | bytes 24584 | tf_op jit(solution)/shard_map/cond/branch_0_fun/ppermute | solution.py:475
  34.0 2.1 %collective-permute-done.5.refs_10_ = f32[16,128]{1,0:T(8,128)S(1)} collective-permute-done((f32[16,128]{1,0:T(8,128)S(1)}, f32[16,128]{1,0:T(8,128)S(1)}, u32[]{:S(2)}, u32[]{:S(2)}) %collective-permute-start.5) | collective-permute-done | bytes 8224 | tf_op jit(solution)/shard_map/cond/branch_0_fun/ppermute | solution.py:475
  36.2 3.7 %branch_0_fun.8 = (bf16[1,128,1792]{2,1,0:T(8,128)(2,1)S(1)}, bf16[1,128,1792]{2,1,0:T(8,128)(2,1)S(1)}, bf16[1,128,1792]{2,1,0:T(8,128)(2,1)S(1)}, bf16[1,128,1792]{2,1,0:T(8,128)(2,1)S(1)}, f32[16,128]{1,0:T(8,128)}) custom-call(s32[1]{0:T(128)} %bitcast.place_ref, s32[8]{0:T(128)S(1)} %get-tuple-element.40.lengths_ref, bf16[1,128,1792]{2,1,0:T(8,128)(2,1)S(1)} %copy-done, ...), custom_call_target="tpu_custom_call" | custom-call | flops 1409286144 | bytes 4587520 | tf_op jit(solution)/shard_map/cond/branch_0_fun/pallas_call | solution.py:490
  39.9 1.3 %collective-permute-start.6 = (bf16[1,128,1792]{2,1,0:T(8,128)(2,1)S(1)}, bf16[1,128,1792]{2,1,0:T(8,128)(2,1)S(1)}, u32[]{:S(2)}, u32[]{:S(2)}) collective-permute-start(bf16[1,128,1792]{2,1,0:T(8,128)(2,1)S(1)} %get-tuple-element.50), channel_id=1, source_target_pairs={{8,0},{12,4},{16,8},{20,12},{24,16},{28,20},{9,1},{13,5},{17,9},{2... | collective-permute-start | bytes 1376264 | tf_op jit(solution)/shard_map/cond/branch_0_fun/ppermute | solution.py:475
  41.2 1.6 %collective-permute-start.7 = (bf16[1,128,1792]{2,1,0:T(8,128)(2,1)S(1)}, bf16[1,128,1792]{2,1,0:T(8,128)(2,1)S(1)}, u32[]{:S(2)}, u32[]{:S(2)}) collective-permute-start(bf16[1,128,1792]{2,1,0:T(8,128)(2,1)S(1)} %get-tuple-element.52), channel_id=1, source_target_pairs={{0,4},{4,0},{8,12},{12,8},{16,20},{20,16},{24,28},{28,24},{1,5},{5... | collective-permute-start | bytes 1376264 | tf_op jit(solution)/shard_map/cond/branch_0_fun/ppermute | solution.py:475
  42.8 0.9 %convert_add_fusion = bf16[1,128,1792]{2,1,0:T(8,128)(2,1)} fusion(bf16[1,128,1792]{2,1,0:T(8,128)(2,1)S(1)} %collective-permute-done.8, bf16[1,128,1792]{2,1,0:T(8,128)(2,1)S(1)} %get-tuple-element.55), kind=kLoop, calls=%fused_computation | loop fusion | flops 917504 | bytes 1376256 | tf_op jit(solution)/shard_map/cond/branch_0_fun/add | solution.py:546
  43.6 9.1 %collective-permute-done.6.key_sent = bf16[1,128,1792]{2,1,0:T(8,128)(2,1)S(1)} collective-permute-done((bf16[1,128,1792]{2,1,0:T(8,128)(2,1)S(1)}, bf16[1,128,1792]{2,1,0:T(8,128)(2,1)S(1)}, u32[]{:S(2)}, u32[]{:S(2)}) %collective-permute-start.6) | collective-permute-done | bytes 458784 | tf_op jit(solution)/shard_map/cond/branch_0_fun/ppermute | solution.py:475
  52.8 1.2 %branch_0_fun.9 = (bf16[1,128,1792]{2,1,0:T(8,128)(2,1)}, bf16[1,128,1792]{2,1,0:T(8,128)(2,1)}) custom-call(bf16[1,128,1792]{2,1,0:T(8,128)(2,1)S(1)} %get-tuple-element.49.key_part, bf16[1,128,1792]{2,1,0:T(8,128)(2,1)S(1)} %collective-permute-done.6.key_sent, bf16[1,128,1792]{2,1,0:T(8,128)(2,1)S(1)} %get-tuple-element.51.query_part, ...), custom_call_target="tpu_custom_call" | custom-call | bytes 4587520 | tf_op jit(solution)/shard_map/cond/branch_0_fun/pallas_call | solution.py:490
  (8 shorter events, 0.0 us)
Async XLA Ops:
  0.6 0.7 %copy-start.6 = (s32[8]{0:T(128)S(1)}, s32[8]{0:T(128)}, u32[]{:S(2)}) copy-start(s32[8]{0:T(128)} %param.12) | copy-start | bytes 100
  2.7 14.6 %collective-permute-start = (bf16[1,128,1792]{2,1,0:T(8,128)(2,1)}, bf16[1,128,1792]{2,1,0:T(8,128)(2,1)S(1)}, u32[]{:S(2)}, u32[]{:S(2)}) collective-permute-start(bf16[1,128,1792]{2,1,0:T(8,128)(2,1)} %get-tuple-element.41.q_own.refs_0_), channel_id=1, source_target_pairs={{0,4},{4,0},{8,12},{12,8},{16,20},{20,16},{24,28},{28,24},{1,5},{5... | collective-permute-start | bytes 1376264 | tf_op jit(solution)/shard_map/cond/branch_0_fun/ppermute | solution.py:475
  5.7 14.7 %collective-permute-start.1 = (bf16[1,128,1792]{2,1,0:T(8,128)(2,1)}, bf16[1,128,1792]{2,1,0:T(8,128)(2,1)S(1)}, u32[]{:S(2)}, u32[]{:S(2)}) collective-permute-start(bf16[1,128,1792]{2,1,0:T(8,128)(2,1)} %get-tuple-element.42.k_own.refs_4_), channel_id=1, source_target_pairs={{0,8},{4,12},{8,16},{12,20},{16,24},{20,28},{1,9},{5,13},{9,17},{1... | collective-permute-start | bytes 1376264 | tf_op jit(solution)/shard_map/cond/branch_0_fun/ppermute | solution.py:475
  9.2 17.2 %collective-permute-start.2 = (bf16[1,128,1792]{2,1,0:T(8,128)(2,1)}, bf16[1,128,1792]{2,1,0:T(8,128)(2,1)S(1)}, u32[]{:S(2)}, u32[]{:S(2)}) collective-permute-start(bf16[1,128,1792]{2,1,0:T(8,128)(2,1)} %get-tuple-element.43.o_own), channel_id=1, source_target_pairs={{0,4},{4,0},{8,12},{12,8},{16,20},{20,16},{24,28},{28,24},{1,5},{5... | collective-permute-start | bytes 1376264 | tf_op jit(solution)/shard_map/cond/branch_0_fun/ppermute | solution.py:475
  9.8 20.6 %collective-permute-start.3 = (bf16[1,128,1792]{2,1,0:T(8,128)(2,1)}, bf16[1,128,1792]{2,1,0:T(8,128)(2,1)S(1)}, u32[]{:S(2)}, u32[]{:S(2)}) collective-permute-start(bf16[1,128,1792]{2,1,0:T(8,128)(2,1)} %get-tuple-element.44.v_own), channel_id=1, source_target_pairs={{0,8},{4,12},{8,16},{12,20},{16,24},{20,28},{24,0},{28,4},{1,9},{5... | collective-permute-start | bytes 1376264 | tf_op jit(solution)/shard_map/cond/branch_0_fun/ppermute | solution.py:475
  20.4 6.4 %copy-start = (bf16[1,128,1792]{2,1,0:T(8,128)(2,1)S(1)}, bf16[1,128,1792]{2,1,0:T(8,128)(2,1)}, u32[]{:S(2)}) copy-start(bf16[1,128,1792]{2,1,0:T(8,128)(2,1)} %get-tuple-element.41.q_own.refs_0_) | copy-start | bytes 1376260
  20.4 6.4 %copy-start.3 = (bf16[1,128,1792]{2,1,0:T(8,128)(2,1)S(1)}, bf16[1,128,1792]{2,1,0:T(8,128)(2,1)}, u32[]{:S(2)}) copy-start(bf16[1,128,1792]{2,1,0:T(8,128)(2,1)} %get-tuple-element.42.k_own.refs_4_) | copy-start | bytes 1376260
  23.0 3.8 %collective-permute-start.4 = (f32[32,128]{1,0:T(8,128)S(1)}, f32[32,128]{1,0:T(8,128)S(1)}, u32[]{:S(2)}, u32[]{:S(2)}) collective-permute-start(f32[32,128]{1,0:T(8,128)S(1)} %get-tuple-element.47.refs_6_), channel_id=1, source_target_pairs={{0,4},{4,0},{8,12},{12,8},{16,20},{20,16},{24,28},{28,24},{1,5},{5... | collective-permute-start | bytes 49160 | tf_op jit(solution)/shard_map/cond/branch_0_fun/ppermute | solution.py:475
  29.1 13.7 %collective-permute-start.8 = (bf16[1,128,1792]{2,1,0:T(8,128)(2,1)S(1)}, bf16[1,128,1792]{2,1,0:T(8,128)(2,1)S(1)}, u32[]{:S(2)}, u32[]{:S(2)}) collective-permute-start(bf16[1,128,1792]{2,1,0:T(8,128)(2,1)S(1)} %get-tuple-element.56), channel_id=1, source_target_pairs={{8,0},{12,4},{16,8},{20,12},{24,16},{28,20},{9,1},{13,5},{17,9},{2... | collective-permute-start | bytes 1376264 | tf_op jit(solution)/shard_map/cond/branch_0_fun/ppermute | solution.py:475
  32.5 3.7 %collective-permute-start.5 = (f32[16,128]{1,0:T(8,128)S(1)}, f32[16,128]{1,0:T(8,128)S(1)}, u32[]{:S(2)}, u32[]{:S(2)}) collective-permute-start(f32[16,128]{1,0:T(8,128)S(1)} %branch_0_fun.7.refs_9_), channel_id=1, source_target_pairs={{0,4},{4,0},{8,12},{12,8},{16,20},{20,16},{24,28},{28,24},{1,5},{5... | collective-permute-start | bytes 24584 | tf_op jit(solution)/shard_map/cond/branch_0_fun/ppermute | solution.py:475
  39.9 12.8 %collective-permute-start.6 = (bf16[1,128,1792]{2,1,0:T(8,128)(2,1)S(1)}, bf16[1,128,1792]{2,1,0:T(8,128)(2,1)S(1)}, u32[]{:S(2)}, u32[]{:S(2)}) collective-permute-start(bf16[1,128,1792]{2,1,0:T(8,128)(2,1)S(1)} %get-tuple-element.50), channel_id=1, source_target_pairs={{8,0},{12,4},{16,8},{20,12},{24,16},{28,20},{9,1},{13,5},{17,9},{2... | collective-permute-start | bytes 1376264 | tf_op jit(solution)/shard_map/cond/branch_0_fun/ppermute | solution.py:475
  41.2 11.6 %collective-permute-start.7 = (bf16[1,128,1792]{2,1,0:T(8,128)(2,1)S(1)}, bf16[1,128,1792]{2,1,0:T(8,128)(2,1)S(1)}, u32[]{:S(2)}, u32[]{:S(2)}) collective-permute-start(bf16[1,128,1792]{2,1,0:T(8,128)(2,1)S(1)} %get-tuple-element.52), channel_id=1, source_target_pairs={{0,4},{4,0},{8,12},{12,8},{16,20},{20,16},{24,28},{28,24},{1,5},{5... | collective-permute-start | bytes 1376264 | tf_op jit(solution)/shard_map/cond/branch_0_fun/ppermute | solution.py:475
where the time goes:
time: 54.1 us; the launch traced here: 53.9 us
  waiting for transfers between devices  23.5 us (43%)
  starting transfers between devices  15 us (28%)
  Pallas kernels  11.7 us (22%)
  other arithmetic  1.62 us (3%)
  between operations  1.29 us (2%)
  local copies, waits for them, and re-layouts  0.66 us (1%)
    ppermute x9, waiting for transfers between devices, send(): return lax.ppermute(value, 'seq', pairs)  23.5 us
    ppermute x9, starting transfers between devices, send(): return lax.ppermute(value, 'seq', pairs)  15 us
    pallas_call x5, Pallas kernels, call(): pl.pallas_call(kernel, grid=(steps,), in_specs=[smem] * len(lead) + [wide...  11.7 us
  transfers between devices with their start and end apart: 9, of which 6 were waited for; matrix products, arithmetic and copies ran while one was open for 2% of the time, Pallas kernels for 20%

commit v1 on v0

--- a/solution.py
+++ b/solution.py
@@ -484,7 +484,7 @@
     def slim_shape(groups, kinds):
         return jax.ShapeDtypeStruct((groups * kinds * GROUP, rows), jnp.float32)
 
-    def call(kernel, products, wides, slims, outs, slim_outs, plain=False):
+    def call(kernel, products, wides, slims, outs, slim_outs, plain=False, scratch=()):
         flops = 2 * products * 4 * rows * rows * width * 3 // 2
         lead = [] if plain else [me[None], doc_lengths]
         return pl.pallas_call(
@@ -495,6 +495,7 @@
             + [slim(groups, kinds) for groups, kinds, _ in slims],
             out_specs=[wide] * outs + [slim(*sizes) for sizes in slim_outs],
             out_shape=[wide_shape] * outs + [slim_shape(*sizes) for sizes in slim_outs],
+            scratch_shapes=[pltpu.VMEM((groups * GROUP, rows), jnp.float32) for groups in scratch],
             compiler_params=pltpu.CompilerParams(vmem_limit_bytes=20 * 1024 * 1024),
             cost_estimate=pl.CostEstimate(
                 flops=flops, bytes_accessed=20 * rows * width, transcendentals=0
@@ -537,9 +538,9 @@
     dots_in = [(count, 1, shift), (count, 1, dots), (count, 1, send(dots, mates))]
     if not ring:
         dots_in += [(count, 1, send(dots, pairs)) for pairs in (near, far)]
-    key_part, key_sent, query_part, query_sent, totals = call(
+    key_part, key_sent, query_part, query_sent, *totals = call(
         functools.partial(keys_kernel, third, heads, scaling, power), 4, tensors, dots_in,
-        4, [(count, 1)],
+        4, [] if ring else [(count, 1)], scratch=[count] if ring else [],
     )
     key_received = send(key_sent, behind)
     query_received = send(query_sent, mates)
@@ -549,7 +550,7 @@
         key_ready, query_ready = call(sums_kernel, 0, sums, [], 2, [], plain=True)
     else:
         sums += [send(graded[0], to_even), send(weighted[0], to_even)]
-        by_step = totals[:GROUP].reshape(steps, heads, rows)
+        by_step = totals[0][:GROUP].reshape(steps, heads, rows)
         by_step = jnp.pad(by_step, ((0, 0), (0, GROUP - heads), (0, 0))).reshape(steps * GROUP, rows)
         key_ready, query_ready = call(
             functools.partial(third_sums_kernel, heads, scaling), 0, sums, [(steps, 1, by_step)], 2, [],

time: 54.1 us -> 95.4 us (1.76)
  the two profiles are of different devices: /device:TPU:0 before, /device:TPU:24 now
where the time goes in v1:
time: 95.4 us; the launch traced here: 94.5 us
  waiting for transfers between devices  49.9 us (52%)
  starting transfers between devices  25 us (26%)
  Pallas kernels  15.6 us (16%)
  other arithmetic  1.63 us (2%)
  between operations  1.29 us (1%)
    ppermute x19, waiting for transfers between devices, send(): return lax.ppermute(value, 'seq', pairs)  49.9 us
    ppermute x19, starting transfers between devices, send(): return lax.ppermute(value, 'seq', pairs)  25 us
    pallas_call x6, Pallas kernels, call(): pl.pallas_call(kernel, grid=(steps,), in_specs=[smem] * len(lead) + [wide...  15.6 us
  transfers between devices with their start and end apart: 19, of which 8 were waited for; matrix products, arithmetic and copies ran while one was open for 1% of the time, Pallas kernels for 12%

profile of v1, /device:TPU:24, one launch (start us, length us, event | category | flops | bytes accessed | tf_op | source)
XLA Modules:
  0.0 94.5 jit_solution(3367971966387096785)
XLA Ops:
  2.7 91.8 %conditional.4 = (bf16[1,128,1792]{2,1,0:T(8,128)(2,1)}, bf16[1,128,1792]{2,1,0:T(8,128)(2,1)}, bf16[1,128,1792]{2,1,0:T(8,128)(2,1)}) conditional(s32[]{:T(128)} %clamp.3, (bf16[1,128,1792]{2,1,0:T(8,128)(2,1)}, bf16[1,128,1792]{2,1,0:T(8,128)(2,1)}, s32[8]{0:T(128)S(1)}, bf16[1,128,1792]{2,1,0:T(8,128)(2,1)}, ...), branch_computations={%region_1.2_spmd, %region_2.3_spmd, %region_3.4_spmd} | conditional | flops 3524132864 | bytes 53187432
  2.9 1.6 %collective-permute-start.28 = (bf16[1,128,1792]{2,1,0:T(8,128)(2,1)}, bf16[1,128,1792]{2,1,0:T(8,128)(2,1)S(1)}, u32[]{:S(2)}, u32[]{:S(2)}) collective-permute-start(bf16[1,128,1792]{2,1,0:T(8,128)(2,1)} %get-tuple-element.81.q_own.refs_0_), channel_id=1, source_target_pairs={{0,4},{4,0},{8,12},{12,8},{16,20},{20,16},{24,28},{28,24},{1,5},{5... | collective-permute-start | bytes 1376264 | tf_op jit(solution)/shard_map/cond/branch_2_fun/ppermute | solution.py:475
  4.5 1.3 %collective-permute-start.29 = (bf16[1,128,1792]{2,1,0:T(8,128)(2,1)}, bf16[1,128,1792]{2,1,0:T(8,128)(2,1)S(1)}, u32[]{:S(2)}, u32[]{:S(2)}) collective-permute-start(bf16[1,128,1792]{2,1,0:T(8,128)(2,1)} %get-tuple-element.82.k_own.refs_6_), channel_id=1, source_target_pairs={{0,8},{4,12},{8,16},{12,20},{16,24},{20,28},{1,9},{5,13},{9,17},{1... | collective-permute-start | bytes 1376264 | tf_op jit(solution)/shard_map/cond/branch_2_fun/ppermute | solution.py:475
  6.3 1.3 %collective-permute-start.33 = (bf16[1,128,1792]{2,1,0:T(8,128)(2,1)}, bf16[1,128,1792]{2,1,0:T(8,128)(2,1)S(1)}, u32[]{:S(2)}, u32[]{:S(2)}) collective-permute-start(bf16[1,128,1792]{2,1,0:T(8,128)(2,1)} %get-tuple-element.84.v_own), channel_id=1, source_target_pairs={{0,8},{4,12},{8,16},{12,20},{16,24},{20,28},{1,9},{5,13},{9,17},{1... | collective-permute-start | bytes 1376264 | tf_op jit(solution)/shard_map/cond/branch_2_fun/ppermute | solution.py:475
  7.6 8.9 %collective-permute-done.28.q_mate.refs_2_ = bf16[1,128,1792]{2,1,0:T(8,128)(2,1)S(1)} collective-permute-done((bf16[1,128,1792]{2,1,0:T(8,128)(2,1)}, bf16[1,128,1792]{2,1,0:T(8,128)(2,1)S(1)}, u32[]{:S(2)}, u32[]{:S(2)}) %collective-permute-start.28) | collective-permute-done | bytes 458784 | tf_op jit(solution)/shard_map/cond/branch_2_fun/ppermute | solution.py:475
  17.3 2.7 %collective-permute-done.29.k_back.refs_7_.refs_8_ = bf16[1,128,1792]{2,1,0:T(8,128)(2,1)S(1)} collective-permute-done((bf16[1,128,1792]{2,1,0:T(8,128)(2,1)}, bf16[1,128,1792]{2,1,0:T(8,128)(2,1)S(1)}, u32[]{:S(2)}, u32[]{:S(2)}) %collective-permute-start.29) | collective-permute-done | bytes 458784 | tf_op jit(solution)/shard_map/cond/branch_2_fun/ppermute | solution.py:475
  20.0 2.5 %branch_2_fun.6 = (bf16[1,128,1792]{2,1,0:T(8,128)(2,1)S(1)}, bf16[1,128,1792]{2,1,0:T(8,128)(2,1)S(1)}, f32[32,128]{1,0:T(8,128)S(1)}) custom-call(s32[1]{0:T(128)} %bitcast.4.place_ref, s32[8]{0:T(128)S(1)} %get-tuple-element.80.lengths_ref, bf16[1,128,1792]{2,1,0:T(8,128)(2,1)} %get-tuple-element.81.q_own.refs_0_, ...), custom_call_target="tpu_custom_call" | custom-call | flops 352321536 | bytes 4587520 | tf_op jit(solution)/shard_map/cond/branch_2_fun/pallas_call | solution.py:490
  22.5 2.7 %collective-permute-done.30.refs_3_ = bf16[1,128,1792]{2,1,0:T(8,128)(2,1)S(1)} collective-permute-done((bf16[1,128,1792]{2,1,0:T(8,128)(2,1)}, bf16[1,128,1792]{2,1,0:T(8,128)(2,1)S(1)}, u32[]{:S(2)}, u32[]{:S(2)}) %collective-permute-start.30) | collective-permute-done | bytes 458784 | tf_op jit(solution)/shard_map/cond/branch_2_fun/ppermute | solution.py:475
  26.8 4.5 %collective-permute-start.37 = (f32[32,128]{1,0:T(8,128)S(1)}, f32[32,128]{1,0:T(8,128)S(1)}, u32[]{:S(2)}, u32[]{:S(2)}) collective-permute-start(f32[32,128]{1,0:T(8,128)S(1)} %get-tuple-element.86.refs_8_), channel_id=1, source_target_pairs={{24,20},{25,21},{26,22},{27,23}} | collective-permute-start | bytes 49160 | tf_op jit(solution)/shard_map/cond/branch_2_fun/ppermute | solution.py:475
  31.4 1.2 %branch_2_fun.7.refs_10_ = f32[16,128]{1,0:T(8,128)S(1)} custom-call(s32[1]{0:T(128)} %bitcast.4.place_ref, s32[8]{0:T(128)S(1)} %get-tuple-element.80.lengths_ref, bf16[1,128,1792]{2,1,0:T(8,128)(2,1)S(1)} %collective-permute-done.31.q_third.refs_4_, bf16[1,128,1792]{2,1,0:T(8,128)(2,1)S(1)} %collective-permute-done.29.k_back.refs_7_.refs_8_), custom_call_target="tpu_custom_call" | custom-call | flops 352321536 | bytes 4587520 | tf_op jit(solution)/shard_map/cond/branch_2_fun/pallas_call | solution.py:490
  33.3 1.3 %collective-permute-start.35 = (f32[16,128]{1,0:T(8,128)S(1)}, f32[16,128]{1,0:T(8,128)S(1)}, u32[]{:S(2)}, u32[]{:S(2)}) collective-permute-start(f32[16,128]{1,0:T(8,128)S(1)} %branch_2_fun.7.refs_10_), channel_id=1, source_target_pairs={{20,24},{21,25},{22,26},{23,27}} | collective-permute-start | bytes 24584 | tf_op jit(solution)/shard_map/cond/branch_2_fun/ppermute | solution.py:475
  35.1 8.2 %collective-permute-done.35.refs_11_ = f32[16,128]{1,0:T(8,128)S(1)} collective-permute-done((f32[16,128]{1,0:T(8,128)S(1)}, f32[16,128]{1,0:T(8,128)S(1)}, u32[]{:S(2)}, u32[]{:S(2)}) %collective-permute-start.35) | collective-permute-done | bytes 8224 | tf_op jit(solution)/shard_map/cond/branch_2_fun/ppermute | solution.py:475
  43.3 2.8 %branch_2_fun.8 = (bf16[1,128,1792]{2,1,0:T(8,128)(2,1)S(1)}, bf16[1,128,1792]{2,1,0:T(8,128)(2,1)S(1)}, bf16[1,128,1792]{2,1,0:T(8,128)(2,1)S(1)}, f32[24,128]{1,0:T(8,128)S(1)}) custom-call(s32[1]{0:T(128)} %bitcast.4.place_ref, s32[8]{0:T(128)S(1)} %get-tuple-element.80.lengths_ref, bf16[1,128,1792]{2,1,0:T(8,128)(2,1)S(1)} %copy-done.2, ...), custom_call_target="tpu_custom_call" | custom-call | flops 704643072 | bytes 4587520 | tf_op jit(solution)/shard_map/cond/branch_2_fun/pallas_call | solution.py:490
  46.1 1.3 %collective-permute-start.46 = (bf16[1,128,1792]{2,1,0:T(8,128)(2,1)S(1)}, bf16[1,128,1792]{2,1,0:T(8,128)(2,1)S(1)}, u32[]{:S(2)}, u32[]{:S(2)}) collective-permute-start(bf16[1,128,1792]{2,1,0:T(8,128)(2,1)S(1)} %get-tuple-element.102), channel_id=1, source_target_pairs={{8,0},{12,4},{16,8},{20,12},{24,16},{28,20},{9,1},{13,5},{17,9},{2... | collective-permute-start | bytes 1376264 | tf_op jit(solution)/shard_map/cond/branch_2_fun/ppermute | solution.py:475
  47.5 3.4 %branch_2_fun.9 = (bf16[1,128,1792]{2,1,0:T(8,128)(2,1)S(1)}, f32[24,128]{1,0:T(8,128)S(1)}) custom-call(s32[1]{0:T(128)} %bitcast.4.place_ref, s32[8]{0:T(128)S(1)} %get-tuple-element.80.lengths_ref, bf16[1,128,1792]{2,1,0:T(8,128)(2,1)S(1)} %copy-done.2, bf16[1,128,1792]{2,1,0:T(8,128)(2,1)S(1)} %get-tuple-element.85.refs_1_, ...), custom_call_target="tpu_custom_call" | custom-call | flops 704643072 | bytes 4587520 | tf_op jit(solution)/shard_map/cond/branch_2_fun/pallas_call | solution.py:490
  51.5 5.5 %collective-permute-start.40 = (f32[24,128]{1,0:T(8,128)S(1)}, f32[24,128]{1,0:T(8,128)S(1)}, u32[]{:S(2)}, u32[]{:S(2)}) collective-permute-start(f32[24,128]{1,0:T(8,128)S(1)} %get-tuple-element.91.refs_11_), channel_id=1, source_target_pairs={{24,20},{20,24},{25,21},{21,25},{26,22},{22,26},{27,23},{23,27}} | collective-permute-start | bytes 36872 | tf_op jit(solution)/shard_map/cond/branch_2_fun/ppermute | solution.py:475
  57.1 1.3 %collective-permute-start.45 = (bf16[1,128,1792]{2,1,0:T(8,128)(2,1)S(1)}, bf16[1,128,1792]{2,1,0:T(8,128)(2,1)S(1)}, u32[]{:S(2)}, u32[]{:S(2)}) collective-permute-start(bf16[1,128,1792]{2,1,0:T(8,128)(2,1)S(1)} %get-tuple-element.97), channel_id=1, source_target_pairs={{20,24},{21,25},{22,26},{23,27}} | collective-permute-start | bytes 1376264 | tf_op jit(solution)/shard_map/cond/branch_2_fun/ppermute | solution.py:475
  58.4 1.3 %collective-permute-start.44 = (bf16[1,128,1792]{2,1,0:T(8,128)(2,1)S(1)}, bf16[1,128,1792]{2,1,0:T(8,128)(2,1)S(1)}, u32[]{:S(2)}, u32[]{:S(2)}) collective-permute-start(bf16[1,128,1792]{2,1,0:T(8,128)(2,1)S(1)} %get-tuple-element.96), channel_id=1, source_target_pairs={{20,24},{21,25},{22,26},{23,27}} | collective-permute-start | bytes 1376264 | tf_op jit(solution)/shard_map/cond/branch_2_fun/ppermute | solution.py:475
  59.7 19.2 %collective-permute-done.39.refs_12_ = f32[24,128]{1,0:T(8,128)S(1)} collective-permute-done((f32[24,128]{1,0:T(8,128)S(1)}, f32[24,128]{1,0:T(8,128)S(1)}, u32[]{:S(2)}, u32[]{:S(2)}) %collective-permute-start.39) | collective-permute-done | bytes 12320 | tf_op jit(solution)/shard_map/cond/branch_2_fun/ppermute | solution.py:475
  79.0 4.0 %branch_2_fun.10 = (bf16[1,128,1792]{2,1,0:T(8,128)(2,1)S(1)}, bf16[1,128,1792]{2,1,0:T(8,128)(2,1)S(1)}, bf16[1,128,1792]{2,1,0:T(8,128)(2,1)S(1)}, bf16[1,128,1792]{2,1,0:T(8,128)(2,1)S(1)}, f32[24,128]{1,0:T(8,128)S(1)}) custom-call(s32[1]{0:T(128)} %bitcast.4.place_ref, s32[8]{0:T(128)S(1)} %get-tuple-element.80.lengths_ref, ...), custom_call_target="tpu_custom_call" | custom-call | flops 1409286144 | bytes 4587520 | tf_op jit(solution)/shard_map/cond/branch_2_fun/pallas_call | solution.py:490
  82.9 1.3 %collective-permute-start.42 = (bf16[1,128,1792]{2,1,0:T(8,128)(2,1)S(1)}, bf16[1,128,1792]{2,1,0:T(8,128)(2,1)S(1)}, u32[]{:S(2)}, u32[]{:S(2)}) collective-permute-start(bf16[1,128,1792]{2,1,0:T(8,128)(2,1)S(1)} %get-tuple-element.93), channel_id=1, source_target_pairs={{8,0},{12,4},{16,8},{20,12},{24,16},{28,20},{9,1},{13,5},{17,9},{2... | collective-permute-start | bytes 1376264 | tf_op jit(solution)/shard_map/cond/branch_2_fun/ppermute | solution.py:475
  85.2 5.0 %collective-permute-done.42.key_sent = bf16[1,128,1792]{2,1,0:T(8,128)(2,1)S(1)} collective-permute-done((bf16[1,128,1792]{2,1,0:T(8,128)(2,1)S(1)}, bf16[1,128,1792]{2,1,0:T(8,128)(2,1)S(1)}, u32[]{:S(2)}, u32[]{:S(2)}) %collective-permute-start.42) | collective-permute-done | bytes 458784 | tf_op jit(solution)/shard_map/cond/branch_2_fun/ppermute | solution.py:475
  90.2 2.6 %collective-permute-done.43.query_sent = bf16[1,128,1792]{2,1,0:T(8,128)(2,1)S(1)} collective-permute-done((bf16[1,128,1792]{2,1,0:T(8,128)(2,1)S(1)}, bf16[1,128,1792]{2,1,0:T(8,128)(2,1)S(1)}, u32[]{:S(2)}, u32[]{:S(2)}) %collective-permute-start.43) | collective-permute-done | bytes 458784 | tf_op jit(solution)/shard_map/cond/branch_2_fun/ppermute | solution.py:475
  92.8 1.7 %branch_2_fun.11 = (bf16[1,128,1792]{2,1,0:T(8,128)(2,1)}, bf16[1,128,1792]{2,1,0:T(8,128)(2,1)}) custom-call(bf16[1,128,1792]{2,1,0:T(8,128)(2,1)S(1)} %get-tuple-element.92.key_part, bf16[1,128,1792]{2,1,0:T(8,128)(2,1)S(1)} %collective-permute-done.42.key_sent, bf16[1,128,1792]{2,1,0:T(8,128)(2,1)S(1)} %get-tuple-element.94.query_part, ...), custom_call_target="tpu_custom_call" | custom-call | bytes 4587520 | tf_op jit(solution)/shard_map/cond/branch_2_fun/pallas_call | solution.py:490
  (31 shorter events, 7.1 us)
Async XLA Ops:
  0.6 0.7 copy-start.6
  2.9 13.7 %collective-permute-start.28 = (bf16[1,128,1792]{2,1,0:T(8,128)(2,1)}, bf16[1,128,1792]{2,1,0:T(8,128)(2,1)S(1)}, u32[]{:S(2)}, u32[]{:S(2)}) collective-permute-start(bf16[1,128,1792]{2,1,0:T(8,128)(2,1)} %get-tuple-element.81.q_own.refs_0_), channel_id=1, source_target_pairs={{0,4},{4,0},{8,12},{12,8},{16,20},{20,16},{24,28},{28,24},{1,5},{5... | collective-permute-start | bytes 1376264 | tf_op jit(solution)/shard_map/cond/branch_2_fun/ppermute | solution.py:475
  4.5 15.5 %collective-permute-start.29 = (bf16[1,128,1792]{2,1,0:T(8,128)(2,1)}, bf16[1,128,1792]{2,1,0:T(8,128)(2,1)S(1)}, u32[]{:S(2)}, u32[]{:S(2)}) collective-permute-start(bf16[1,128,1792]{2,1,0:T(8,128)(2,1)} %get-tuple-element.82.k_own.refs_6_), channel_id=1, source_target_pairs={{0,8},{4,12},{8,16},{12,20},{16,24},{20,28},{1,9},{5,13},{9,17},{1... | collective-permute-start | bytes 1376264 | tf_op jit(solution)/shard_map/cond/branch_2_fun/ppermute | solution.py:475
  5.7 19.5 %collective-permute-start.30 = (bf16[1,128,1792]{2,1,0:T(8,128)(2,1)}, bf16[1,128,1792]{2,1,0:T(8,128)(2,1)S(1)}, u32[]{:S(2)}, u32[]{:S(2)}) collective-permute-start(bf16[1,128,1792]{2,1,0:T(8,128)(2,1)} %get-tuple-element.83.o_own), channel_id=1, source_target_pairs={{0,4},{4,0},{8,12},{12,8},{16,20},{20,16},{24,28},{28,24},{1,5},{5... | collective-permute-start | bytes 1376264 | tf_op jit(solution)/shard_map/cond/branch_2_fun/ppermute | solution.py:475
  6.3 24.9 %collective-permute-start.33 = (bf16[1,128,1792]{2,1,0:T(8,128)(2,1)}, bf16[1,128,1792]{2,1,0:T(8,128)(2,1)S(1)}, u32[]{:S(2)}, u32[]{:S(2)}) collective-permute-start(bf16[1,128,1792]{2,1,0:T(8,128)(2,1)} %get-tuple-element.84.v_own), channel_id=1, source_target_pairs={{0,8},{4,12},{8,16},{12,20},{16,24},{20,28},{1,9},{5,13},{9,17},{1... | collective-permute-start | bytes 1376264 | tf_op jit(solution)/shard_map/cond/branch_2_fun/ppermute | solution.py:475
  16.6 14.8 %collective-permute-start.31 = (bf16[1,128,1792]{2,1,0:T(8,128)(2,1)S(1)}, bf16[1,128,1792]{2,1,0:T(8,128)(2,1)S(1)}, u32[]{:S(2)}, u32[]{:S(2)}) collective-permute-start(bf16[1,128,1792]{2,1,0:T(8,128)(2,1)S(1)} %collective-permute-done.28.q_mate.refs_2_), channel_id=1, source_target_pairs={{28,20},{29,21},{30,22},{31,23}} | collective-permute-start | bytes 1376264 | tf_op jit(solution)/shard_map/cond/branch_2_fun/ppermute | solution.py:475
  25.3 18.0 %copy-start.2 = (bf16[1,128,1792]{2,1,0:T(8,128)(2,1)S(1)}, bf16[1,128,1792]{2,1,0:T(8,128)(2,1)}, u32[]{:S(2)}) copy-start(bf16[1,128,1792]{2,1,0:T(8,128)(2,1)} %get-tuple-element.81.q_own.refs_0_) | copy-start | bytes 1376260
  25.3 18.0 %copy-start.5 = (bf16[1,128,1792]{2,1,0:T(8,128)(2,1)S(1)}, bf16[1,128,1792]{2,1,0:T(8,128)(2,1)}, u32[]{:S(2)}) copy-start(bf16[1,128,1792]{2,1,0:T(8,128)(2,1)} %get-tuple-element.82.k_own.refs_6_) | copy-start | bytes 1376260
  25.3 9.8 %collective-permute-start.32 = (bf16[1,128,1792]{2,1,0:T(8,128)(2,1)S(1)}, bf16[1,128,1792]{2,1,0:T(8,128)(2,1)S(1)}, u32[]{:S(2)}, u32[]{:S(2)}) collective-permute-start(bf16[1,128,1792]{2,1,0:T(8,128)(2,1)S(1)} %collective-permute-done.30.refs_3_), channel_id=1, source_target_pairs={{28,20},{29,21},{30,22},{31,23}} | collective-permute-start | bytes 1376264 | tf_op jit(solution)/shard_map/cond/branch_2_fun/ppermute | solution.py:475
  26.1 7.2 %collective-permute-start.38 = (f32[32,128]{1,0:T(8,128)S(1)}, f32[32,128]{1,0:T(8,128)S(1)}, u32[]{:S(2)}, u32[]{:S(2)}) collective-permute-start(f32[32,128]{1,0:T(8,128)S(1)} %get-tuple-element.86.refs_8_), channel_id=1, source_target_pairs={{28,20},{29,21},{30,22},{31,23}} | collective-permute-start | bytes 49160 | tf_op jit(solution)/shard_map/cond/branch_2_fun/ppermute | solution.py:475
  26.8 7.9 %collective-permute-start.37 = (f32[32,128]{1,0:T(8,128)S(1)}, f32[32,128]{1,0:T(8,128)S(1)}, u32[]{:S(2)}, u32[]{:S(2)}) collective-permute-start(f32[32,128]{1,0:T(8,128)S(1)} %get-tuple-element.86.refs_8_), channel_id=1, source_target_pairs={{24,20},{25,21},{26,22},{27,23}} | collective-permute-start | bytes 49160 | tf_op jit(solution)/shard_map/cond/branch_2_fun/ppermute | solution.py:475
  31.3 3.8 %collective-permute-start.34 = (f32[32,128]{1,0:T(8,128)S(1)}, f32[32,128]{1,0:T(8,128)S(1)}, u32[]{:S(2)}, u32[]{:S(2)}) collective-permute-start(f32[32,128]{1,0:T(8,128)S(1)} %get-tuple-element.86.refs_8_), channel_id=1, source_target_pairs={{0,4},{4,0},{8,12},{12,8},{16,20},{20,16},{24,28},{28,24},{1,5},{5... | collective-permute-start | bytes 49160 | tf_op jit(solution)/shard_map/cond/branch_2_fun/ppermute | solution.py:475
  32.6 2.5 %collective-permute-start.36 = (f32[16,128]{1,0:T(8,128)S(1)}, f32[16,128]{1,0:T(8,128)S(1)}, u32[]{:S(2)}, u32[]{:S(2)}) collective-permute-start(f32[16,128]{1,0:T(8,128)S(1)} %branch_2_fun.7.refs_10_), channel_id=1, source_target_pairs={{20,28},{21,29},{22,30},{23,31}} | collective-permute-start | bytes 24584 | tf_op jit(solution)/shard_map/cond/branch_2_fun/ppermute | solution.py:475
  33.3 10.0 %collective-permute-start.35 = (f32[16,128]{1,0:T(8,128)S(1)}, f32[16,128]{1,0:T(8,128)S(1)}, u32[]{:S(2)}, u32[]{:S(2)}) collective-permute-start(f32[16,128]{1,0:T(8,128)S(1)} %branch_2_fun.7.refs_10_), channel_id=1, source_target_pairs={{20,24},{21,25},{22,26},{23,27}} | collective-permute-start | bytes 24584 | tf_op jit(solution)/shard_map/cond/branch_2_fun/ppermute | solution.py:475
  46.1 38.2 %collective-permute-start.46 = (bf16[1,128,1792]{2,1,0:T(8,128)(2,1)S(1)}, bf16[1,128,1792]{2,1,0:T(8,128)(2,1)S(1)}, u32[]{:S(2)}, u32[]{:S(2)}) collective-permute-start(bf16[1,128,1792]{2,1,0:T(8,128)(2,1)S(1)} %get-tuple-element.102), channel_id=1, source_target_pairs={{8,0},{12,4},{16,8},{20,12},{24,16},{28,20},{9,1},{13,5},{17,9},{2... | collective-permute-start | bytes 1376264 | tf_op jit(solution)/shard_map/cond/branch_2_fun/ppermute | solution.py:475
  50.8 7.6 %collective-permute-start.41 = (f32[24,128]{1,0:T(8,128)S(1)}, f32[24,128]{1,0:T(8,128)S(1)}, u32[]{:S(2)}, u32[]{:S(2)}) collective-permute-start(f32[24,128]{1,0:T(8,128)S(1)} %get-tuple-element.91.refs_11_), channel_id=1, source_target_pairs={{28,20},{20,28},{29,21},{21,29},{30,22},{22,30},{31,23},{23,31}} | collective-permute-start | bytes 36872 | tf_op jit(solution)/shard_map/cond/branch_2_fun/ppermute | solution.py:475
  51.5 8.2 %collective-permute-start.40 = (f32[24,128]{1,0:T(8,128)S(1)}, f32[24,128]{1,0:T(8,128)S(1)}, u32[]{:S(2)}, u32[]{:S(2)}) collective-permute-start(f32[24,128]{1,0:T(8,128)S(1)} %get-tuple-element.91.refs_11_), channel_id=1, source_target_pairs={{24,20},{20,24},{25,21},{21,25},{26,22},{22,26},{27,23},{23,27}} | collective-permute-start | bytes 36872 | tf_op jit(solution)/shard_map/cond/branch_2_fun/ppermute | solution.py:475
  57.0 21.9 %collective-permute-start.39 = (f32[24,128]{1,0:T(8,128)S(1)}, f32[24,128]{1,0:T(8,128)S(1)}, u32[]{:S(2)}, u32[]{:S(2)}) collective-permute-start(f32[24,128]{1,0:T(8,128)S(1)} %get-tuple-element.91.refs_11_), channel_id=1, source_target_pairs={{0,4},{4,0},{8,12},{12,8},{16,20},{20,16},{24,28},{28,24},{1,5},{5... | collective-permute-start | bytes 36872 | tf_op jit(solution)/shard_map/cond/branch_2_fun/ppermute | solution.py:475
  57.1 28.1 %collective-permute-start.45 = (bf16[1,128,1792]{2,1,0:T(8,128)(2,1)S(1)}, bf16[1,128,1792]{2,1,0:T(8,128)(2,1)S(1)}, u32[]{:S(2)}, u32[]{:S(2)}) collective-permute-start(bf16[1,128,1792]{2,1,0:T(8,128)(2,1)S(1)} %get-tuple-element.97), channel_id=1, source_target_pairs={{20,24},{21,25},{22,26},{23,27}} | collective-permute-start | bytes 1376264 | tf_op jit(solution)/shard_map/cond/branch_2_fun/ppermute | solution.py:475
  58.4 26.8 %collective-permute-start.44 = (bf16[1,128,1792]{2,1,0:T(8,128)(2,1)S(1)}, bf16[1,128,1792]{2,1,0:T(8,128)(2,1)S(1)}, u32[]{:S(2)}, u32[]{:S(2)}) collective-permute-start(bf16[1,128,1792]{2,1,0:T(8,128)(2,1)S(1)} %get-tuple-element.96), channel_id=1, source_target_pairs={{20,24},{21,25},{22,26},{23,27}} | collective-permute-start | bytes 1376264 | tf_op jit(solution)/shard_map/cond/branch_2_fun/ppermute | solution.py:475
  82.9 7.3 %collective-permute-start.42 = (bf16[1,128,1792]{2,1,0:T(8,128)(2,1)S(1)}, bf16[1,128,1792]{2,1,0:T(8,128)(2,1)S(1)}, u32[]{:S(2)}, u32[]{:S(2)}) collective-permute-start(bf16[1,128,1792]{2,1,0:T(8,128)(2,1)S(1)} %get-tuple-element.93), channel_id=1, source_target_pairs={{8,0},{12,4},{16,8},{20,12},{24,16},{28,20},{9,1},{13,5},{17,9},{2... | collective-permute-start | bytes 1376264 | tf_op jit(solution)/shard_map/cond/branch_2_fun/ppermute | solution.py:475
  84.3 8.5 %collective-permute-start.43 = (bf16[1,128,1792]{2,1,0:T(8,128)(2,1)S(1)}, bf16[1,128,1792]{2,1,0:T(8,128)(2,1)S(1)}, u32[]{:S(2)}, u32[]{:S(2)}) collective-permute-start(bf16[1,128,1792]{2,1,0:T(8,128)(2,1)S(1)} %get-tuple-element.95), channel_id=1, source_target_pairs={{0,4},{4,0},{8,12},{12,8},{16,20},{20,16},{24,28},{28,24},{1,5},{5... | collective-permute-start | bytes 1376264 | tf_op jit(solution)/shard_map/cond/branch_2_fun/ppermute | solution.py:475

commit v2 on v1

--- a/solution.py
+++ b/solution.py
@@ -197,7 +197,7 @@
     keys = key_block * rows + lax.broadcasted_iota(jnp.int32, shape, 0)
     start = jnp.zeros_like(position)
     bound = jnp.int32(0)
-    for doc in range(lengths_ref.shape[0]):
+    for doc in range(1, lengths_ref.shape[0]):
         bound = bound + lengths_ref[doc]
         start = jnp.where(position >= bound, bound, start)
     return (keys >= start) & (keys <= position)
@@ -450,7 +450,7 @@
     query_out[0] = (add_refs(query_part, query_sent)[0] + extra).astype(jnp.bfloat16)
 
 
-def halo_program(third, queries, key_vectors, value_vectors, out_grad, doc_lengths):
+def halo_program(third, queries, key_vectors, value_vectors, out_grad, facts):
     _, rows, width = queries.shape
     seq_size = lax.axis_size("seq")
     me = lax.axis_index("seq").astype(jnp.int32)
@@ -486,7 +486,7 @@
 
     def call(kernel, products, wides, slims, outs, slim_outs, plain=False, scratch=()):
         flops = 2 * products * 4 * rows * rows * width * 3 // 2
-        lead = [] if plain else [me[None], doc_lengths]
+        lead = [] if plain else [me[None], facts]
         return pl.pallas_call(
             kernel,
             grid=(steps,),
@@ -559,20 +559,34 @@
     return query_ready, key_ready, value_ready
 
 
-def program_index(rows, doc_lengths):
-    count = doc_lengths.shape[0]
-    ends = sum(lax.pad(doc_lengths[: count - n], jnp.int32(0), [(n, 0, 0)]) for n in range(count))
-    shift = rows.bit_length() - 1
-    first, last = (ends - doc_lengths) >> shift, (ends - 1) >> shift
-    spans = (last - first >= 3) & (last & 1 == 0)
-    return jnp.sum(jnp.where(spans, (last >> 1) - 1, 0))
+def program_kernel(shift, lengths_ref, out_ref):
+    start, found = jnp.int32(0), jnp.int32(0)
+    for doc in range(lengths_ref.shape[0]):
+        end = start + lengths_ref[doc]
+        last = (end - 1) >> shift
+        spans = (last - (start >> shift) >= 3) & (last & 1 == 0)
+        found = jnp.where(spans, (last >> 1) - 1, found)
+        out_ref[doc + 1] = lengths_ref[doc]
+        start = end
+    out_ref[0] = found
+
+
+def program_facts(rows, doc_lengths):
+    smem = pl.BlockSpec(memory_space=pltpu.SMEM)
+    return pl.pallas_call(
+        functools.partial(program_kernel, rows.bit_length() - 1),
+        in_specs=[smem],
+        out_specs=smem,
+        out_shape=jax.ShapeDtypeStruct((doc_lengths.shape[0] + 1,), jnp.int32),
+    )(doc_lengths)
 
 
 def halo_shards(*arguments):
-    rows, doc_lengths = arguments[0].shape[1], arguments[-1]
+    *tensors, doc_lengths = arguments
+    facts = program_facts(tensors[0].shape[1], doc_lengths)
     thirds = range(3, lax.axis_size("seq") - 2, 2)
     programs = [functools.partial(halo_program, third) for third in (None, *thirds)]
-    return lax.switch(program_index(rows, doc_lengths), programs, *arguments)
+    return lax.switch(facts[0], programs, *tensors, facts)
 
 
 def shards(queries, key_vectors, value_vectors, out_grad, doc_lengths):

time: 95.4 us -> 52.9 us (0.55)
  the two profiles are of different devices: /device:TPU:24 before, /device:TPU:0 now
where the time goes in v2:
time: 52.9 us; the launch traced here: 52.7 us
  waiting for transfers between devices  23.6 us (45%)
  starting transfers between devices  15 us (28%)
  Pallas kernels  12.4 us (23%)
  other arithmetic  0.87 us (2%)
  between operations  0.67 us (1%)
    ppermute x9, waiting for transfers between devices, send(): return lax.ppermute(value, 'seq', pairs)  23.6 us
    ppermute x9, starting transfers between devices, send(): return lax.ppermute(value, 'seq', pairs)  15 us
    pallas_call x5, Pallas kernels, call(): pl.pallas_call(kernel, grid=(steps,), in_specs=[smem] * len(lead) + [wide...  11.2 us
    pallas_call x1, Pallas kernels, program_facts(): pl.pallas_call(functools.partial(program_kernel, rows.bit_length() - 1),...  1.29 us
  transfers between devices with their start and end apart: 9, of which 7 were waited for; matrix products, arithmetic and copies ran while one was open for 2% of the time, Pallas kernels for 19%

profile of v2, /device:TPU:0, one launch (start us, length us, event | category | flops | bytes accessed | tf_op | source)
XLA Modules:
  0.0 52.7 jit_solution(4111138388704428438)
XLA Ops:
  0.6 1.3 %shard_map.91 = s32[9]{0:T(128)S(1)} custom-call(s32[8]{0:T(128)} %lengths_ref.1), custom_call_target="tpu_custom_call" | custom-call | tf_op jit(solution)/shard_map/pallas_call | solution.py:576
  2.0 50.8 %conditional.4 = (bf16[1,128,1792]{2,1,0:T(8,128)(2,1)}, bf16[1,128,1792]{2,1,0:T(8,128)(2,1)}, bf16[1,128,1792]{2,1,0:T(8,128)(2,1)}) conditional(s32[]{:T(128)} %bitcast.7, (bf16[1,128,1792]{2,1,0:T(8,128)(2,1)}, bf16[1,128,1792]{2,1,0:T(8,128)(2,1)}, s32[9]{0:T(128)S(1)}, bf16[1,128,1792]{2,1,0:T(8,128)(2,1)}, ...), branch_computations={%region_0.0_spmd, %region_1.2_spmd, %region_2.3_spmd} | conditional | flops 3524132864 | bytes 53187432
  2.0 3.0 %collective-permute-start = (bf16[1,128,1792]{2,1,0:T(8,128)(2,1)}, bf16[1,128,1792]{2,1,0:T(8,128)(2,1)S(1)}, u32[]{:S(2)}, u32[]{:S(2)}) collective-permute-start(bf16[1,128,1792]{2,1,0:T(8,128)(2,1)} %get-tuple-element.119.q_own.refs_0_), channel_id=1, source_target_pairs={{0,4},{4,0},{8,12},{12,8},{16,20},{20,16},{24,28},{28,24},{1,5},{5... | collective-permute-start | bytes 1376264 | tf_op jit(solution)/shard_map/cond/branch_0_fun/ppermute | solution.py:475
  5.0 3.5 %collective-permute-start.1 = (bf16[1,128,1792]{2,1,0:T(8,128)(2,1)}, bf16[1,128,1792]{2,1,0:T(8,128)(2,1)S(1)}, u32[]{:S(2)}, u32[]{:S(2)}) collective-permute-start(bf16[1,128,1792]{2,1,0:T(8,128)(2,1)} %get-tuple-element.122.k_own.refs_4_), channel_id=1, source_target_pairs={{0,8},{4,12},{8,16},{12,20},{16,24},{20,28},{1,9},{5,13},{9,17},{1... | collective-permute-start | bytes 1376264 | tf_op jit(solution)/shard_map/cond/branch_0_fun/ppermute | solution.py:475
  8.5 0.6 %collective-permute-start.2 = (bf16[1,128,1792]{2,1,0:T(8,128)(2,1)}, bf16[1,128,1792]{2,1,0:T(8,128)(2,1)S(1)}, u32[]{:S(2)}, u32[]{:S(2)}) collective-permute-start(bf16[1,128,1792]{2,1,0:T(8,128)(2,1)} %get-tuple-element.125.o_own), channel_id=1, source_target_pairs={{0,4},{4,0},{8,12},{12,8},{16,20},{20,16},{24,28},{28,24},{1,5},{5... | collective-permute-start | bytes 1376264 | tf_op jit(solution)/shard_map/cond/branch_0_fun/ppermute | solution.py:475
  9.1 1.6 %collective-permute-start.3 = (bf16[1,128,1792]{2,1,0:T(8,128)(2,1)}, bf16[1,128,1792]{2,1,0:T(8,128)(2,1)S(1)}, u32[]{:S(2)}, u32[]{:S(2)}) collective-permute-start(bf16[1,128,1792]{2,1,0:T(8,128)(2,1)} %get-tuple-element.128.v_own), channel_id=1, source_target_pairs={{0,8},{4,12},{8,16},{12,20},{16,24},{20,28},{24,0},{28,4},{1,9},{5... | collective-permute-start | bytes 1376264 | tf_op jit(solution)/shard_map/cond/branch_0_fun/ppermute | solution.py:475
  10.6 5.9 %collective-permute-done.q_mate.refs_2_ = bf16[1,128,1792]{2,1,0:T(8,128)(2,1)S(1)} collective-permute-done((bf16[1,128,1792]{2,1,0:T(8,128)(2,1)}, bf16[1,128,1792]{2,1,0:T(8,128)(2,1)S(1)}, u32[]{:S(2)}, u32[]{:S(2)}) %collective-permute-start) | collective-permute-done | bytes 458784 | tf_op jit(solution)/shard_map/cond/branch_0_fun/ppermute | solution.py:475
  16.5 3.2 %collective-permute-done.1.k_back.refs_5_.refs_6_ = bf16[1,128,1792]{2,1,0:T(8,128)(2,1)S(1)} collective-permute-done((bf16[1,128,1792]{2,1,0:T(8,128)(2,1)}, bf16[1,128,1792]{2,1,0:T(8,128)(2,1)S(1)}, u32[]{:S(2)}, u32[]{:S(2)}) %collective-permute-start.1) | collective-permute-done | bytes 458784 | tf_op jit(solution)/shard_map/cond/branch_0_fun/ppermute | solution.py:475
  19.7 2.6 %branch_0_fun.5 = (bf16[1,128,1792]{2,1,0:T(8,128)(2,1)S(1)}, bf16[1,128,1792]{2,1,0:T(8,128)(2,1)S(1)}, f32[32,128]{1,0:T(8,128)S(1)}) custom-call(s32[1]{0:T(128)} %bitcast.place_ref, s32[9]{0:T(128)S(1)} %get-tuple-element.40.lengths_ref, bf16[1,128,1792]{2,1,0:T(8,128)(2,1)} %get-tuple-element.119.q_own.refs_0_, ...), custom_call_target="tpu_custom_call" | custom-call | flops 352321536 | bytes 4587520 | tf_op jit(solution)/shard_map/cond/branch_0_fun/pallas_call | solution.py:490
  22.3 0.6 %collective-permute-start.4 = (f32[32,128]{1,0:T(8,128)S(1)}, f32[32,128]{1,0:T(8,128)S(1)}, u32[]{:S(2)}, u32[]{:S(2)}) collective-permute-start(f32[32,128]{1,0:T(8,128)S(1)} %get-tuple-element.47.refs_6_), channel_id=1, source_target_pairs={{0,4},{4,0},{8,12},{12,8},{16,20},{20,16},{24,28},{28,24},{1,5},{5... | collective-permute-start | bytes 49160 | tf_op jit(solution)/shard_map/cond/branch_0_fun/ppermute | solution.py:475
  22.9 2.8 %collective-permute-done.2.refs_3_ = bf16[1,128,1792]{2,1,0:T(8,128)(2,1)S(1)} collective-permute-done((bf16[1,128,1792]{2,1,0:T(8,128)(2,1)}, bf16[1,128,1792]{2,1,0:T(8,128)(2,1)S(1)}, u32[]{:S(2)}, u32[]{:S(2)}) %collective-permute-start.2) | collective-permute-done | bytes 458784 | tf_op jit(solution)/shard_map/cond/branch_0_fun/ppermute | solution.py:475
  25.7 0.4 collective-permute-done.4.refs_7_
  26.1 2.2 %branch_0_fun.6 = (bf16[1,128,1792]{2,1,0:T(8,128)(2,1)S(1)}, bf16[1,128,1792]{2,1,0:T(8,128)(2,1)S(1)}, f32[16,128]{1,0:T(8,128)S(1)}) custom-call(s32[1]{0:T(128)} %bitcast.place_ref, s32[9]{0:T(128)S(1)} %get-tuple-element.40.lengths_ref, bf16[1,128,1792]{2,1,0:T(8,128)(2,1)S(1)} %copy-done, bf16[1,128,1792]{2,1,0:T(8,128)(2,1)S(1)} %get-tuple-element.45.refs_1_, ...), custom_call_target="tpu_custom_call" | custom-call | flops 704643072 | bytes 4587520 | tf_op jit(solution)/shard_map/cond/branch_0_fun/pallas_call | solution.py:490
  28.3 1.3 %collective-permute-start.8 = (bf16[1,128,1792]{2,1,0:T(8,128)(2,1)S(1)}, bf16[1,128,1792]{2,1,0:T(8,128)(2,1)S(1)}, u32[]{:S(2)}, u32[]{:S(2)}) collective-permute-start(bf16[1,128,1792]{2,1,0:T(8,128)(2,1)S(1)} %get-tuple-element.56), channel_id=1, source_target_pairs={{8,0},{12,4},{16,8},{20,12},{24,16},{28,20},{9,1},{13,5},{17,9},{2... | collective-permute-start | bytes 1376264 | tf_op jit(solution)/shard_map/cond/branch_0_fun/ppermute | solution.py:475
  29.7 2.1 %branch_0_fun.7.refs_9_ = f32[16,128]{1,0:T(8,128)S(1)} custom-call(s32[1]{0:T(128)} %bitcast.place_ref, s32[9]{0:T(128)S(1)} %get-tuple-element.40.lengths_ref, bf16[1,128,1792]{2,1,0:T(8,128)(2,1)S(1)} %copy-done, bf16[1,128,1792]{2,1,0:T(8,128)(2,1)S(1)} %get-tuple-element.45.refs_1_, bf16[1,128,1792]{2,1,0:T(8,128)(2,1)S(1)} %collective-permute-done.q_mate.refs_2_, ...), custom_call_target="tpu_custom_call" | custom-call | flops 704643072 | bytes 4587520 | tf_op jit(solution)/shard_map/cond/branch_0_fun/pallas_call | solution.py:490
  31.7 1.6 %collective-permute-start.5 = (f32[16,128]{1,0:T(8,128)S(1)}, f32[16,128]{1,0:T(8,128)S(1)}, u32[]{:S(2)}, u32[]{:S(2)}) collective-permute-start(f32[16,128]{1,0:T(8,128)S(1)} %branch_0_fun.7.refs_9_), channel_id=1, source_target_pairs={{0,4},{4,0},{8,12},{12,8},{16,20},{20,16},{24,28},{28,24},{1,5},{5... | collective-permute-start | bytes 24584 | tf_op jit(solution)/shard_map/cond/branch_0_fun/ppermute | solution.py:475
  33.3 2.1 %collective-permute-done.5.refs_10_ = f32[16,128]{1,0:T(8,128)S(1)} collective-permute-done((f32[16,128]{1,0:T(8,128)S(1)}, f32[16,128]{1,0:T(8,128)S(1)}, u32[]{:S(2)}, u32[]{:S(2)}) %collective-permute-start.5) | collective-permute-done | bytes 8224 | tf_op jit(solution)/shard_map/cond/branch_0_fun/ppermute | solution.py:475
  35.5 3.1 %branch_0_fun.8 = (bf16[1,128,1792]{2,1,0:T(8,128)(2,1)S(1)}, bf16[1,128,1792]{2,1,0:T(8,128)(2,1)S(1)}, bf16[1,128,1792]{2,1,0:T(8,128)(2,1)S(1)}, bf16[1,128,1792]{2,1,0:T(8,128)(2,1)S(1)}) custom-call(s32[1]{0:T(128)} %bitcast.place_ref, s32[9]{0:T(128)S(1)} %get-tuple-element.40.lengths_ref, bf16[1,128,1792]{2,1,0:T(8,128)(2,1)S(1)} %copy-done, ...), custom_call_target="tpu_custom_call" | custom-call | flops 1409286144 | bytes 4587520 | tf_op jit(solution)/shard_map/cond/branch_0_fun/pallas_call | solution.py:490
  38.6 1.3 %collective-permute-start.6 = (bf16[1,128,1792]{2,1,0:T(8,128)(2,1)S(1)}, bf16[1,128,1792]{2,1,0:T(8,128)(2,1)S(1)}, u32[]{:S(2)}, u32[]{:S(2)}) collective-permute-start(bf16[1,128,1792]{2,1,0:T(8,128)(2,1)S(1)} %get-tuple-element.50), channel_id=1, source_target_pairs={{8,0},{12,4},{16,8},{20,12},{24,16},{28,20},{9,1},{13,5},{17,9},{2... | collective-permute-start | bytes 1376264 | tf_op jit(solution)/shard_map/cond/branch_0_fun/ppermute | solution.py:475
  39.9 1.6 %collective-permute-start.7 = (bf16[1,128,1792]{2,1,0:T(8,128)(2,1)S(1)}, bf16[1,128,1792]{2,1,0:T(8,128)(2,1)S(1)}, u32[]{:S(2)}, u32[]{:S(2)}) collective-permute-start(bf16[1,128,1792]{2,1,0:T(8,128)(2,1)S(1)} %get-tuple-element.52), channel_id=1, source_target_pairs={{0,4},{4,0},{8,12},{12,8},{16,20},{20,16},{24,28},{28,24},{1,5},{5... | collective-permute-start | bytes 1376264 | tf_op jit(solution)/shard_map/cond/branch_0_fun/ppermute | solution.py:475
  41.5 0.3 collective-permute-done.8
  41.8 0.9 %convert_add_fusion = bf16[1,128,1792]{2,1,0:T(8,128)(2,1)} fusion(bf16[1,128,1792]{2,1,0:T(8,128)(2,1)S(1)} %collective-permute-done.8, bf16[1,128,1792]{2,1,0:T(8,128)(2,1)S(1)} %get-tuple-element.55), kind=kLoop, calls=%fused_computation | loop fusion | flops 917504 | bytes 1376256 | tf_op jit(solution)/shard_map/cond/branch_0_fun/add | solution.py:547
  42.7 8.9 %collective-permute-done.6.key_sent = bf16[1,128,1792]{2,1,0:T(8,128)(2,1)S(1)} collective-permute-done((bf16[1,128,1792]{2,1,0:T(8,128)(2,1)S(1)}, bf16[1,128,1792]{2,1,0:T(8,128)(2,1)S(1)}, u32[]{:S(2)}, u32[]{:S(2)}) %collective-permute-start.6) | collective-permute-done | bytes 458784 | tf_op jit(solution)/shard_map/cond/branch_0_fun/ppermute | solution.py:475
  51.6 1.2 %branch_0_fun.9 = (bf16[1,128,1792]{2,1,0:T(8,128)(2,1)}, bf16[1,128,1792]{2,1,0:T(8,128)(2,1)}) custom-call(bf16[1,128,1792]{2,1,0:T(8,128)(2,1)S(1)} %get-tuple-element.49.key_part, bf16[1,128,1792]{2,1,0:T(8,128)(2,1)S(1)} %collective-permute-done.6.key_sent, bf16[1,128,1792]{2,1,0:T(8,128)(2,1)S(1)} %get-tuple-element.51.query_part, ...), custom_call_target="tpu_custom_call" | custom-call | bytes 4587520 | tf_op jit(solution)/shard_map/cond/branch_0_fun/pallas_call | solution.py:490
  (6 shorter events, 0.0 us)
Async XLA Ops:
  2.0 14.6 %collective-permute-start = (bf16[1,128,1792]{2,1,0:T(8,128)(2,1)}, bf16[1,128,1792]{2,1,0:T(8,128)(2,1)S(1)}, u32[]{:S(2)}, u32[]{:S(2)}) collective-permute-start(bf16[1,128,1792]{2,1,0:T(8,128)(2,1)} %get-tuple-element.119.q_own.refs_0_), channel_id=1, source_target_pairs={{0,4},{4,0},{8,12},{12,8},{16,20},{20,16},{24,28},{28,24},{1,5},{5... | collective-permute-start | bytes 1376264 | tf_op jit(solution)/shard_map/cond/branch_0_fun/ppermute | solution.py:475
  5.0 14.7 %collective-permute-start.1 = (bf16[1,128,1792]{2,1,0:T(8,128)(2,1)}, bf16[1,128,1792]{2,1,0:T(8,128)(2,1)S(1)}, u32[]{:S(2)}, u32[]{:S(2)}) collective-permute-start(bf16[1,128,1792]{2,1,0:T(8,128)(2,1)} %get-tuple-element.122.k_own.refs_4_), channel_id=1, source_target_pairs={{0,8},{4,12},{8,16},{12,20},{16,24},{20,28},{1,9},{5,13},{9,17},{1... | collective-permute-start | bytes 1376264 | tf_op jit(solution)/shard_map/cond/branch_0_fun/ppermute | solution.py:475
  8.5 17.2 %collective-permute-start.2 = (bf16[1,128,1792]{2,1,0:T(8,128)(2,1)}, bf16[1,128,1792]{2,1,0:T(8,128)(2,1)S(1)}, u32[]{:S(2)}, u32[]{:S(2)}) collective-permute-start(bf16[1,128,1792]{2,1,0:T(8,128)(2,1)} %get-tuple-element.125.o_own), channel_id=1, source_target_pairs={{0,4},{4,0},{8,12},{12,8},{16,20},{20,16},{24,28},{28,24},{1,5},{5... | collective-permute-start | bytes 1376264 | tf_op jit(solution)/shard_map/cond/branch_0_fun/ppermute | solution.py:475
  9.1 20.6 %collective-permute-start.3 = (bf16[1,128,1792]{2,1,0:T(8,128)(2,1)}, bf16[1,128,1792]{2,1,0:T(8,128)(2,1)S(1)}, u32[]{:S(2)}, u32[]{:S(2)}) collective-permute-start(bf16[1,128,1792]{2,1,0:T(8,128)(2,1)} %get-tuple-element.128.v_own), channel_id=1, source_target_pairs={{0,8},{4,12},{8,16},{12,20},{16,24},{20,28},{24,0},{28,4},{1,9},{5... | collective-permute-start | bytes 1376264 | tf_op jit(solution)/shard_map/cond/branch_0_fun/ppermute | solution.py:475
  19.7 6.4 %copy-start = (bf16[1,128,1792]{2,1,0:T(8,128)(2,1)S(1)}, bf16[1,128,1792]{2,1,0:T(8,128)(2,1)}, u32[]{:S(2)}) copy-start(bf16[1,128,1792]{2,1,0:T(8,128)(2,1)} %get-tuple-element.119.q_own.refs_0_) | copy-start | bytes 1376260
  19.7 6.4 %copy-start.3 = (bf16[1,128,1792]{2,1,0:T(8,128)(2,1)S(1)}, bf16[1,128,1792]{2,1,0:T(8,128)(2,1)}, u32[]{:S(2)}) copy-start(bf16[1,128,1792]{2,1,0:T(8,128)(2,1)} %get-tuple-element.122.k_own.refs_4_) | copy-start | bytes 1376260
  22.3 3.8 %collective-permute-start.4 = (f32[32,128]{1,0:T(8,128)S(1)}, f32[32,128]{1,0:T(8,128)S(1)}, u32[]{:S(2)}, u32[]{:S(2)}) collective-permute-start(f32[32,128]{1,0:T(8,128)S(1)} %get-tuple-element.47.refs_6_), channel_id=1, source_target_pairs={{0,4},{4,0},{8,12},{12,8},{16,20},{20,16},{24,28},{28,24},{1,5},{5... | collective-permute-start | bytes 49160 | tf_op jit(solution)/shard_map/cond/branch_0_fun/ppermute | solution.py:475
  28.3 13.4 %collective-permute-start.8 = (bf16[1,128,1792]{2,1,0:T(8,128)(2,1)S(1)}, bf16[1,128,1792]{2,1,0:T(8,128)(2,1)S(1)}, u32[]{:S(2)}, u32[]{:S(2)}) collective-permute-start(bf16[1,128,1792]{2,1,0:T(8,128)(2,1)S(1)} %get-tuple-element.56), channel_id=1, source_target_pairs={{8,0},{12,4},{16,8},{20,12},{24,16},{28,20},{9,1},{13,5},{17,9},{2... | collective-permute-start | bytes 1376264 | tf_op jit(solution)/shard_map/cond/branch_0_fun/ppermute | solution.py:475
  31.7 3.7 %collective-permute-start.5 = (f32[16,128]{1,0:T(8,128)S(1)}, f32[16,128]{1,0:T(8,128)S(1)}, u32[]{:S(2)}, u32[]{:S(2)}) collective-permute-start(f32[16,128]{1,0:T(8,128)S(1)} %branch_0_fun.7.refs_9_), channel_id=1, source_target_pairs={{0,4},{4,0},{8,12},{12,8},{16,20},{20,16},{24,28},{28,24},{1,5},{5... | collective-permute-start | bytes 24584 | tf_op jit(solution)/shard_map/cond/branch_0_fun/ppermute | solution.py:475
  38.6 13.0 %collective-permute-start.6 = (bf16[1,128,1792]{2,1,0:T(8,128)(2,1)S(1)}, bf16[1,128,1792]{2,1,0:T(8,128)(2,1)S(1)}, u32[]{:S(2)}, u32[]{:S(2)}) collective-permute-start(bf16[1,128,1792]{2,1,0:T(8,128)(2,1)S(1)} %get-tuple-element.50), channel_id=1, source_target_pairs={{8,0},{12,4},{16,8},{20,12},{24,16},{28,20},{9,1},{13,5},{17,9},{2... | collective-permute-start | bytes 1376264 | tf_op jit(solution)/shard_map/cond/branch_0_fun/ppermute | solution.py:475
  39.9 11.7 %collective-permute-start.7 = (bf16[1,128,1792]{2,1,0:T(8,128)(2,1)S(1)}, bf16[1,128,1792]{2,1,0:T(8,128)(2,1)S(1)}, u32[]{:S(2)}, u32[]{:S(2)}) collective-permute-start(bf16[1,128,1792]{2,1,0:T(8,128)(2,1)S(1)} %get-tuple-element.52), channel_id=1, source_target_pairs={{0,4},{4,0},{8,12},{12,8},{16,20},{20,16},{24,28},{28,24},{1,5},{5... | collective-permute-start | bytes 1376264 | tf_op jit(solution)/shard_map/cond/branch_0_fun/ppermute | solution.py:475

commit v3 on v2

--- a/solution.py
+++ b/solution.py
@@ -244,11 +244,6 @@
     return slots, keys, mask & (me == third)
 
 
-def tile_plan(third, lengths_ref, rows, me):
-    plan = [pair_tile(lengths_ref, rows, me)]
-    return plan if third is None else plan + [third_tile(third, lengths_ref, rows, me)]
-
-
 def lane_cut(value, number, rows):
     return value[:, number * rows : (number + 1) * rows]
 
@@ -295,26 +290,19 @@
     return ref[number * size : (number + 1) * size, :]
 
 
-def stats_parts(mine, sent, extra):
-    own = [part_of(mine, 2, 0), part_of(sent, 2, 1)]
-    mate = [part_of(mine, 2, 1), part_of(sent, 2, 0)]
-    if not extra:
-        return [own, mate]
-    third, near, far, even, odd = extra
-    return [own + [near[...]], mate + [far[...]], [third[...], part_of(even, 2, 0), part_of(odd, 2, 1)]]
-
-
-def dots_parts(mine, sent, extra):
-    own = [part_of(mine, 1, 0), part_of(sent, 1, 1)]
-    mate = [part_of(mine, 1, 1), part_of(sent, 1, 0)]
-    if not extra:
-        return [own, mate]
-    near, far = extra
-    return [
-        own + [part_of(near, 1, 2)],
-        mate + [part_of(far, 1, 2)],
-        [part_of(mine, 1, 2), part_of(near, 1, 0), part_of(far, 1, 1)],
-    ]
+def group_parts(kinds, mine, sent, extra):
+    own = [part_of(mine, kinds, 0), part_of(sent, kinds, 1)]
+    mate = [part_of(mine, kinds, 1), part_of(sent, kinds, 0)]
+    if extra:
+        near, far = extra
+        own, mate = own + [near[...]], mate + [far[...]]
+    return [own, mate]
+
+
+def merge_groups(scaling, shift_ref, refs):
+    mine, sent, *extra = refs
+    for number, parts in enumerate(group_parts(2, mine, sent, extra)):
+        shift_ref[number * GROUP : (number + 1) * GROUP, :] = merge_stats(scaling, parts)
 
 
 def merge_stats(scaling, parts):
@@ -325,23 +313,26 @@
 
 
 class Emitter:
-    def __init__(self, outs):
-        self.outs, self.carry = outs, {}
+    def __init__(self, outs, base={}):
+        self.outs, self.base, self.carry = outs, base, {}
+
+    def put(self, name, start, stop, value):
+        if name in self.base:
+            value = value + self.base[name][0, :, start:stop].astype(jnp.float32)
+        self.outs[name][0, :, start:stop] = value.astype(jnp.bfloat16)
 
     def emit(self, head, name, value):
-        ref = self.outs[name]
         low, high = head_span(head)
         first, last = head * HEAD % LANES == 0, (head + 1) * HEAD % LANES == 0
         start, stop = low, high
         if not first:
-            shared = value[:, :LANES] + self.carry.pop(name)
-            ref[0, :, low : low + LANES] = shared.astype(jnp.bfloat16)
+            self.put(name, low, low + LANES, value[:, :LANES] + self.carry.pop(name))
             start = low + LANES
         if not last:
             self.carry[name] = value[:, high - LANES - low :]
             stop = high - LANES
         if stop > start:
-            ref[0, :, start:stop] = value[:, start - low : stop - low].astype(jnp.bfloat16)
+            self.put(name, start, stop, value[:, start - low : stop - low])
 
 
 def add_rows(sums, kind, slots, value, rows):
@@ -351,64 +342,61 @@
         sums[name] = sums[name] + piece if name in sums else piece
 
 
-def split_refs(third, refs):
-    count = 2 if third is None else 3
-    queries = [(refs[2 * n], refs[2 * n + 1]) for n in range(count)]
-    keys = [(refs[2 * n], refs[2 * n + 1]) for n in range(count, count + 2)]
-    return queries, keys, refs[2 * count + 4 :]
-
-
-def values_kernel(third, heads, scaling, power, place_ref, lengths_ref, *refs):
-    count, last = (2, -3) if third is None else (3, -4)
-    queries = [(refs[2 * n], refs[2 * n + 1]) for n in range(count)]
-    refs, outs = refs[2 * count : last], refs[last:]
-    keys, shift_ref = [(refs[0],), (refs[1],)], outs[-1]
-    rows, me, step = keys[0][0].shape[1], place_ref[0], pl.program_id(0)
-    plan = tile_plan(third, lengths_ref, rows, me)
-    for number, parts in enumerate(stats_parts(refs[2], refs[3], refs[4:])):
-        shift_ref[number * GROUP : (number + 1) * GROUP, :] = merge_stats(scaling, parts)
-    out = Emitter(dict(zip((("v", 0), ("v", 1), ("b", 2)), outs[:-1])))
+def split_refs(refs):
+    return ((refs[0:2], refs[2:4]), (refs[4:6], refs[6:8]), refs[8:])
+
+
+def values_kernel(merge, heads, scaling, power, place_ref, lengths_ref, q0, o0, q1, o1, k0, k1, *refs):
+    queries, keys = ((q0, o0), (q1, o1)), ((k0,), (k1,))
+    if merge:
+        *stats, value_own, value_back, shift_ref = refs
+        merge_groups(scaling, shift_ref, stats)
+    else:
+        shift_ref, value_own, value_back = refs
+    rows, me, step = k0.shape[1], place_ref[0], pl.program_id(0)
+    plan = [pair_tile(lengths_ref, rows, me)]
+    out = Emitter({("v", 0): value_own, ("v", 1): value_back})
     for head, (tiles, keep) in tiles_ahead(heads, plan, queries, keys, 1):
         low, high = head_span(head)
         sums = {}
-        for (query_slots, key_slots, mask), (_, (k,), (raw,)) in zip(plan, tiles):
+        for (query_slots, key_slots, mask), (_, _, (raw,)) in zip(plan, tiles):
             shift = per_query(query_slots, 1, 0, step * heads + head, shift_ref)
             weight = jnp.where(mask, jnp.exp2((raw - shift) * power), 0.0).astype(jnp.bfloat16)
             o = stack([queries[slot][1][0, :, low:high] for slot in query_slots], 0) * keep
             add_rows(sums, "v", key_slots, matmul(weight, o, NN), rows)
-            if query_slots == [2]:
-                add_rows(sums, "b", query_slots, matmul(weight, k, TN), rows)
         for name, value in sums.items():
             out.emit(head, name, value)
 
 
-def dots_kernel(third, heads, power, place_ref, lengths_ref, *refs):
-    queries, keys, (shift_ref, *outs) = split_refs(third, refs)
-    dots_ref = outs[-1]
+def dots_kernel(merge, heads, scaling, power, place_ref, lengths_ref, *refs):
+    queries, keys, refs = split_refs(refs)
+    if merge:
+        *stats, dots_ref, shift_ref = refs
+        merge_groups(scaling, shift_ref, stats)
+    else:
+        shift_ref, dots_ref = refs
     rows, me, step = keys[0][0].shape[1], place_ref[0], pl.program_id(0)
-    plan = tile_plan(third, lengths_ref, rows, me)
-    out = Emitter(dict(zip((("a", 2),), outs[:-1])))
+    plan = [pair_tile(lengths_ref, rows, me)]
     for head, (tiles, _) in tiles_ahead(heads, plan, queries, keys, 2):
         at = step * heads + head
-        for (query_slots, _, mask), (_, (k, _), (raw, grads)) in zip(plan, tiles):
+        for (query_slots, _, mask), (_, _, (raw, grads)) in zip(plan, tiles):
             shift = per_query(query_slots, 1, 0, at, shift_ref)
-            product = jnp.where(mask, jnp.exp2((raw - shift) * power), 0.0) * grads
-            dots = jnp.sum(product, axis=0, keepdims=True)
+            weight = jnp.where(mask, jnp.exp2((raw - shift) * power), 0.0)
+            dots = jnp.sum(weight * grads, axis=0, keepdims=True)
             for number, slot in enumerate(query_slots):
                 dots_ref[row_of(slot, 1, 0, at), :] = lane_cut(dots, number, rows)
-            if query_slots == [2]:
-                out.emit(head, ("a", 2), matmul(product.astype(jnp.bfloat16), k, TN))
 
 
 def keys_kernel(third, heads, scaling, power, place_ref, lengths_ref, *refs):
-    queries, keys, refs = split_refs(third, refs)
-    (shift_ref, mine, sent, *extra), outs = refs[:-5], refs[-5:]
-    total_ref = outs[-1]
+    queries, keys, refs = split_refs(refs)
+    (*base, shift_ref, mine, sent), refs = (refs[:3], refs[3:]) if third is None else (refs[:4], refs[4:])
+    *extra, key_own, key_back, query_own, query_mate, total_ref = refs
     rows, me, step = keys[0][0].shape[1], place_ref[0], pl.program_id(0)
-    plan = tile_plan(third, lengths_ref, rows, me)
-    for number, parts in enumerate(dots_parts(mine, sent, extra)):
+    plan = [pair_tile(lengths_ref, rows, me)]
+    for number, parts in enumerate(group_parts(1, mine, sent, extra)):
         total_ref[number * GROUP : (number + 1) * GROUP, :] = sum(parts)
-    out = Emitter(dict(zip((("k", 0), ("k", 1), ("q", 0), ("q", 1)), outs[:-1])))
+    outs = {("k", 0): key_own, ("k", 1): key_back, ("q", 0): query_own, ("q", 1): query_mate}
+    out = Emitter(outs, {("k", 1): ref for ref in base})
     for head, (tiles, keep) in tiles_ahead(heads, plan, queries, keys, 2):
         at = step * heads + head
         sums = {}
@@ -418,36 +406,43 @@
             weight = jnp.where(mask, jnp.exp2((raw - shift) * power), 0.0)
             slope = (weight * (grads - dots) * scaling).astype(jnp.bfloat16)
             add_rows(sums, "k", key_slots, matmul(slope, q * keep, NN), rows)
-            if query_slots != [2]:
-                add_rows(sums, "q", query_slots, matmul(slope, k, TN), rows)
+            add_rows(sums, "q", query_slots, matmul(slope, k, TN), rows)
         for name, value in sums.items():
             out.emit(head, name, value)
 
 
+def third_kernel(
+    third, heads, scaling, power, place_ref, lengths_ref, q_third, o_third, k_back, v_back, value_part,
+    stats, even_stats, odd_stats, even_dots, odd_dots, value_out, key_out, query_out, dots_ref, shift_ref,
+):
+    rows, me, step = k_back.shape[1], place_ref[0], pl.program_id(0)
+    parts = [stats[...], part_of(even_stats, 2, 0), part_of(odd_stats, 2, 1)]
+    shift_ref[...] = merge_stats(scaling, parts)
+    slots, keys, mask = third_tile(third, lengths_ref, rows, me)
+    queries, keys = (None, None, (q_third, o_third)), (None, (k_back, v_back))
+    plan = [(slots, [1], mask)]
+    out = Emitter({"v": value_out, "k": key_out, "q": query_out}, {"v": value_part})
+    for head, (tiles, keep) in tiles_ahead(heads, plan, queries, keys, 2):
+        (q, o), (k, _), (raw, grads) = tiles[0]
+        at = step * heads + head
+        weight = jnp.where(mask, jnp.exp2((raw - shift_ref[pl.ds(at, 1), :]) * power), 0.0)
+        dots = jnp.sum(weight * grads, axis=0, keepdims=True)
+        dots_ref[pl.ds(at, 1), :] = dots
+        total = dots + even_dots[row_of(0, 1, 0, at), :] + odd_dots[row_of(1, 1, 0, at), :]
+        slope = (weight * (grads - total) * scaling).astype(jnp.bfloat16)
+        out.emit(head, "v", matmul(weight.astype(jnp.bfloat16), o * keep, NN))
+        out.emit(head, "k", matmul(slope, q * keep, NN))
+        out.emit(head, "q", matmul(slope, k, TN))
+
+
 def add_refs(*refs):
     return sum(ref[...].astype(jnp.float32) for ref in refs)
 
 
-def sums_kernel(key_part, key_sent, query_part, query_sent, key_out, query_out):
+def sums_kernel(key_part, key_sent, *refs):
+    *query_parts, key_out, query_out = refs
     key_out[...] = add_refs(key_part, key_sent).astype(jnp.bfloat16)
-    query_out[...] = add_refs(query_part, query_sent).astype(jnp.bfloat16)
-
-
-def third_sums_kernel(
-    heads, scaling, key_part, key_sent, query_part, query_sent, a_sent, b_sent, total_ref, key_out, query_out
-):
-    key_out[...] = add_refs(key_part, key_sent).astype(jnp.bfloat16)
-    step = pl.program_id(0)
-    rows, part = query_out.shape[1:]
-    spread = total_ref[pl.ds(pl.multiple_of(step * GROUP, GROUP), GROUP), :]
-    columns = jnp.concatenate([spread, jnp.zeros((LANES - GROUP, rows), jnp.float32)], 0).T
-    lane = lax.broadcasted_iota(jnp.int32, (rows, part), 1)
-    dots = jnp.zeros((rows, part), jnp.float32)
-    for head in range(heads):
-        inside = (lane >= head * HEAD) & (lane < (head + 1) * HEAD)
-        dots = jnp.where(inside, columns[:, head : head + 1], dots)
-    extra = (a_sent[0].astype(jnp.float32) - dots * b_sent[0].astype(jnp.float32)) * scaling
-    query_out[0] = (add_refs(query_part, query_sent)[0] + extra).astype(jnp.bfloat16)
+    query_out[...] = add_refs(*query_parts).astype(jnp.bfloat16)
 
 
 def halo_program(third, queries, key_vectors, value_vectors, out_grad, facts):
@@ -459,7 +454,6 @@
     steps = width // HEAD // 4
     part = width // steps
     heads = part // HEAD
-    count = 2 if third is None else 3
     devices = range(seq_size)
     mates = [(s, s ^ 1) for s in devices]
     ring = third is None
@@ -469,7 +463,6 @@
     if not ring:
         relay, to_odd = [(third + 2, third)], [(third, third + 2)]
         from_even, to_even = [(third + 1, third)], [(third, third + 1)]
-        near, far = from_even + to_even, relay + to_odd
 
     def send(value, pairs):
         return lax.ppermute(value, "seq", pairs)
@@ -506,56 +499,62 @@
     key_back = send(key_vectors, chain)
     grad_mate = send(out_grad, mates)
     value_back = send(value_vectors, ahead)
-    query_rows, grad_rows = [queries, query_mate], [out_grad, grad_mate]
     grad_own, value_own, stats = call(
         functools.partial(stats_kernel, heads, power), 1,
-        [*query_rows, key_vectors, key_back, out_grad, value_vectors], [], 2, [(2, 2)],
+        [queries, query_mate, key_vectors, key_back, out_grad, value_vectors], [], 2, [(2, 2)],
     )
     stats_in = [(2, 2, stats), (2, 2, send(stats, mates))]
-    grad_rows[0] = grad_own
-    if not ring:
-        query_rows.append(send(query_mate, relay))
-        held, _ = lax.optimization_barrier((grad_mate, stats))
-        grad_rows.append(send(held, relay))
-        query_third, _ = lax.optimization_barrier((query_rows[2], value_back))
+    rows_in = [queries, grad_own, query_mate, grad_mate]
+    tensors = rows_in + [key_vectors, value_own, key_back, value_back]
+    constants = (heads, scaling, power)
+    if ring:
+        value_part, value_sent, shift = call(
+            functools.partial(values_kernel, True, *constants), 2, rows_in + [key_vectors, key_back],
+            stats_in, 2, [(2, 1)],
+        )
+        (dots,) = call(
+            functools.partial(dots_kernel, False, *constants), 2, tensors, [(2, 1, shift)], 0, [(2, 1)]
+        )
+        dots_in = [(2, 1, shift), (2, 1, dots), (2, 1, send(dots, mates))]
+        base = []
+    else:
+        query_third = send(query_mate, relay)
+        even_stats, odd_stats = send(stats, from_even), send(stats, relay)
+        held, even_stats, odd_stats = lax.optimization_barrier((grad_mate, even_stats, odd_stats))
+        grad_third = send(held, relay)
+        query_third, _ = lax.optimization_barrier((query_third, value_back))
         (third_stats,) = call(
-            functools.partial(third_stats_kernel, third, heads, power), 1,
-            [query_third, key_back], [], 0, [(1, 2)],
-        )
-        stats_in += [(1, 2, third_stats), (1, 2, send(third_stats, to_even)), (1, 2, send(third_stats, to_odd))]
-        stats_in += [(2, 2, send(stats, from_even)), (2, 2, send(stats, relay))]
-    tensors = [t for two in zip(query_rows, grad_rows) for t in two]
-    value_part, value_sent, *weighted, shift = call(
-        functools.partial(values_kernel, third, heads, scaling, power), 2,
-        tensors + [key_vectors, key_back], stats_in, count, [(count, 1)],
-    )
-    tensors += [key_vectors, value_own, key_back, value_back]
-    *graded, dots = call(
-        functools.partial(dots_kernel, third, heads, power), 2, tensors, [(count, 1, shift)],
-        count - 2, [(count, 1)],
-    )
+            functools.partial(third_stats_kernel, third, heads, power), 1, [query_third, key_back], [],
+            0, [(1, 2)],
+        )
+        stats_in += [(1, 2, send(third_stats, to_even)), (1, 2, send(third_stats, to_odd))]
+        dots, shift = call(
+            functools.partial(dots_kernel, True, *constants), 2, tensors, stats_in, 0, [(2, 1), (2, 1)]
+        )
+        even_dots, odd_dots = send(dots, from_even), send(dots, relay)
+        value_part, value_back_part = call(
+            functools.partial(values_kernel, False, *constants), 2, rows_in + [key_vectors, key_back],
+            [(2, 1, shift)], 2, [],
+        )
+        value_sent, key_third, query_extra, third_dots = call(
+            functools.partial(third_kernel, third, *constants), 2,
+            [query_third, grad_third, key_back, value_back, value_back_part],
+            [(1, 2, third_stats), (2, 2, even_stats), (2, 2, odd_stats), (2, 1, even_dots), (2, 1, odd_dots)],
+            3, [(1, 1)], scratch=[1],
+        )
+        dots_in = [(2, 1, shift), (2, 1, dots), (2, 1, send(dots, mates))]
+        dots_in += [(1, 1, send(third_dots, to_even)), (1, 1, send(third_dots, to_odd))]
+        base = [key_third]
     value_received = send(value_sent, behind)
-    dots_in = [(count, 1, shift), (count, 1, dots), (count, 1, send(dots, mates))]
-    if not ring:
-        dots_in += [(count, 1, send(dots, pairs)) for pairs in (near, far)]
-    key_part, key_sent, query_part, query_sent, *totals = call(
-        functools.partial(keys_kernel, third, heads, scaling, power), 4, tensors, dots_in,
-        4, [] if ring else [(count, 1)], scratch=[count] if ring else [],
+    key_part, key_sent, query_part, query_sent = call(
+        functools.partial(keys_kernel, third, *constants), 4, tensors + base, dots_in, 4, [], scratch=[2],
     )
     key_received = send(key_sent, behind)
-    query_received = send(query_sent, mates)
+    query_received = [send(query_sent, mates)] + ([] if ring else [send(query_extra, to_even)])
     value_ready = (value_part.astype(jnp.float32) + value_received.astype(jnp.float32)).astype(jnp.bfloat16)
-    sums = [key_part, key_received, query_part, query_received]
-    if ring:
-        key_ready, query_ready = call(sums_kernel, 0, sums, [], 2, [], plain=True)
-    else:
-        sums += [send(graded[0], to_even), send(weighted[0], to_even)]
-        by_step = totals[0][:GROUP].reshape(steps, heads, rows)
-        by_step = jnp.pad(by_step, ((0, 0), (0, GROUP - heads), (0, 0))).reshape(steps * GROUP, rows)
-        key_ready, query_ready = call(
-            functools.partial(third_sums_kernel, heads, scaling), 0, sums, [(steps, 1, by_step)], 2, [],
-            plain=True,
-        )
+    key_ready, query_ready = call(
+        sums_kernel, 0, [key_part, key_received, query_part, *query_received], [], 2, [], plain=True
+    )
     return query_ready, key_ready, value_ready
 
 

time: 52.9 us -> 52.9 us (level)
  no operation moved by 1% of the time
where the time goes in v3:
time: 52.9 us; the launch traced here: 52.7 us
  waiting for transfers between devices  23.6 us (45%)
  starting transfers between devices  15 us (28%)
  Pallas kernels  12.4 us (23%)
  other arithmetic  0.87 us (2%)
  between operations  0.67 us (1%)
    ppermute x9, waiting for transfers between devices, send(): return lax.ppermute(value, 'seq', pairs)  23.6 us
    ppermute x9, starting transfers between devices, send(): return lax.ppermute(value, 'seq', pairs)  15 us
    pallas_call x5, Pallas kernels, call(): pl.pallas_call(kernel, grid=(steps,), in_specs=[smem] * len(lead) + [wide...  11.2 us
    pallas_call x1, Pallas kernels, program_facts(): pl.pallas_call(functools.partial(program_kernel, rows.bit_length() - 1),...  1.29 us
  transfers between devices with their start and end apart: 9, of which 7 were waited for; matrix products, arithmetic and copies ran while one was open for 2% of the time, Pallas kernels for 19%

profile of v3, /device:TPU:0, one launch (start us, length us, event | category | flops | bytes accessed | tf_op | source)
XLA Modules:
  0.0 52.7 jit_solution(143004047934101219)
XLA Ops:
  0.6 1.3 %shard_map.91 = s32[9]{0:T(128)S(1)} custom-call(s32[8]{0:T(128)} %lengths_ref.1), custom_call_target="tpu_custom_call" | custom-call | tf_op jit(solution)/shard_map/pallas_call | solution.py:575
  2.0 50.8 %conditional.4 = (bf16[1,128,1792]{2,1,0:T(8,128)(2,1)}, bf16[1,128,1792]{2,1,0:T(8,128)(2,1)}, bf16[1,128,1792]{2,1,0:T(8,128)(2,1)}) conditional(s32[]{:T(128)} %bitcast.3, (bf16[1,128,1792]{2,1,0:T(8,128)(2,1)}, bf16[1,128,1792]{2,1,0:T(8,128)(2,1)}, s32[9]{0:T(128)S(1)}, bf16[1,128,1792]{2,1,0:T(8,128)(2,1)}, ...), branch_computations={%region_0.0_spmd, %region_1.0_spmd, %region_2.0_spmd} | conditional | flops 4228775936 | bytes 55903120
  2.0 3.0 %collective-permute-start = (bf16[1,128,1792]{2,1,0:T(8,128)(2,1)}, bf16[1,128,1792]{2,1,0:T(8,128)(2,1)S(1)}, u32[]{:S(2)}, u32[]{:S(2)}) collective-permute-start(bf16[1,128,1792]{2,1,0:T(8,128)(2,1)} %get-tuple-element.125.q_own.q0.refs_0_), channel_id=1, source_target_pairs={{0,4},{4,0},{8,12},{12,8},{16,20},{20,16},{24,28},{28,24},{1,5},{5... | collective-permute-start | bytes 1376264 | tf_op jit(solution)/shard_map/cond/branch_0_fun/ppermute | solution.py:468
  5.0 3.5 %collective-permute-start.1 = (bf16[1,128,1792]{2,1,0:T(8,128)(2,1)}, bf16[1,128,1792]{2,1,0:T(8,128)(2,1)S(1)}, u32[]{:S(2)}, u32[]{:S(2)}) collective-permute-start(bf16[1,128,1792]{2,1,0:T(8,128)(2,1)} %get-tuple-element.128.k_own.k0.refs_4_), channel_id=1, source_target_pairs={{0,8},{4,12},{8,16},{12,20},{16,24},{20,28},{1,9},{5,13},{9,17},{1... | collective-permute-start | bytes 1376264 | tf_op jit(solution)/shard_map/cond/branch_0_fun/ppermute | solution.py:468
  8.5 0.6 %collective-permute-start.2 = (bf16[1,128,1792]{2,1,0:T(8,128)(2,1)}, bf16[1,128,1792]{2,1,0:T(8,128)(2,1)S(1)}, u32[]{:S(2)}, u32[]{:S(2)}) collective-permute-start(bf16[1,128,1792]{2,1,0:T(8,128)(2,1)} %get-tuple-element.131.o_own), channel_id=1, source_target_pairs={{0,4},{4,0},{8,12},{12,8},{16,20},{20,16},{24,28},{28,24},{1,5},{5... | collective-permute-start | bytes 1376264 | tf_op jit(solution)/shard_map/cond/branch_0_fun/ppermute | solution.py:468
  9.1 1.6 %collective-permute-start.3 = (bf16[1,128,1792]{2,1,0:T(8,128)(2,1)}, bf16[1,128,1792]{2,1,0:T(8,128)(2,1)S(1)}, u32[]{:S(2)}, u32[]{:S(2)}) collective-permute-start(bf16[1,128,1792]{2,1,0:T(8,128)(2,1)} %get-tuple-element.134.v_own), channel_id=1, source_target_pairs={{0,8},{4,12},{8,16},{12,20},{16,24},{20,28},{24,0},{28,4},{1,9},{5... | collective-permute-start | bytes 1376264 | tf_op jit(solution)/shard_map/cond/branch_0_fun/ppermute | solution.py:468
  10.6 5.9 %collective-permute-done.q_mate.q1.refs_2_ = bf16[1,128,1792]{2,1,0:T(8,128)(2,1)S(1)} collective-permute-done((bf16[1,128,1792]{2,1,0:T(8,128)(2,1)}, bf16[1,128,1792]{2,1,0:T(8,128)(2,1)S(1)}, u32[]{:S(2)}, u32[]{:S(2)}) %collective-permute-start) | collective-permute-done | bytes 458784 | tf_op jit(solution)/shard_map/cond/branch_0_fun/ppermute | solution.py:468
  16.5 3.2 %collective-permute-done.1.k_back.k1.refs_6_ = bf16[1,128,1792]{2,1,0:T(8,128)(2,1)S(1)} collective-permute-done((bf16[1,128,1792]{2,1,0:T(8,128)(2,1)}, bf16[1,128,1792]{2,1,0:T(8,128)(2,1)S(1)}, u32[]{:S(2)}, u32[]{:S(2)}) %collective-permute-start.1) | collective-permute-done | bytes 458784 | tf_op jit(solution)/shard_map/cond/branch_0_fun/ppermute | solution.py:468
  19.7 2.6 %branch_0_fun.5 = (bf16[1,128,1792]{2,1,0:T(8,128)(2,1)S(1)}, bf16[1,128,1792]{2,1,0:T(8,128)(2,1)S(1)}, f32[32,128]{1,0:T(8,128)S(1)}) custom-call(s32[1]{0:T(128)} %bitcast.place_ref, s32[9]{0:T(128)S(1)} %get-tuple-element.40.lengths_ref, bf16[1,128,1792]{2,1,0:T(8,128)(2,1)} %get-tuple-element.125.q_own.q0.refs_0_, ...), custom_call_target="tpu_custom_call" | custom-call | flops 352321536 | bytes 4587520 | tf_op jit(solution)/shard_map/cond/branch_0_fun/pallas_call | solution.py:483
  22.3 0.6 %collective-permute-start.4 = (f32[32,128]{1,0:T(8,128)S(1)}, f32[32,128]{1,0:T(8,128)S(1)}, u32[]{:S(2)}, u32[]{:S(2)}) collective-permute-start(f32[32,128]{1,0:T(8,128)S(1)} %get-tuple-element.47.refs_0_), channel_id=1, source_target_pairs={{0,4},{4,0},{8,12},{12,8},{16,20},{20,16},{24,28},{28,24},{1,5},{5... | collective-permute-start | bytes 49160 | tf_op jit(solution)/shard_map/cond/branch_0_fun/ppermute | solution.py:468
  22.9 2.8 %collective-permute-done.2.o1.refs_3_ = bf16[1,128,1792]{2,1,0:T(8,128)(2,1)S(1)} collective-permute-done((bf16[1,128,1792]{2,1,0:T(8,128)(2,1)}, bf16[1,128,1792]{2,1,0:T(8,128)(2,1)S(1)}, u32[]{:S(2)}, u32[]{:S(2)}) %collective-permute-start.2) | collective-permute-done | bytes 458784 | tf_op jit(solution)/shard_map/cond/branch_0_fun/ppermute | solution.py:468
  25.7 0.4 collective-permute-done.4.refs_1_
  26.1 2.2 %branch_0_fun.6 = (bf16[1,128,1792]{2,1,0:T(8,128)(2,1)S(1)}, bf16[1,128,1792]{2,1,0:T(8,128)(2,1)S(1)}, f32[16,128]{1,0:T(8,128)S(1)}) custom-call(s32[1]{0:T(128)} %bitcast.place_ref, s32[9]{0:T(128)S(1)} %get-tuple-element.40.lengths_ref, bf16[1,128,1792]{2,1,0:T(8,128)(2,1)S(1)} %copy-done, bf16[1,128,1792]{2,1,0:T(8,128)(2,1)S(1)} %get-tuple-element.45.o0.refs_1_, ...), custom_call_target="tpu_custom_call" | custom-call | flops 704643072 | bytes 4587520 | tf_op jit(solution)/shard_map/cond/branch_0_fun/pallas_call | solution.py:483
  28.3 1.3 %collective-permute-start.8 = (bf16[1,128,1792]{2,1,0:T(8,128)(2,1)S(1)}, bf16[1,128,1792]{2,1,0:T(8,128)(2,1)S(1)}, u32[]{:S(2)}, u32[]{:S(2)}) collective-permute-start(bf16[1,128,1792]{2,1,0:T(8,128)(2,1)S(1)} %get-tuple-element.56), channel_id=1, source_target_pairs={{8,0},{12,4},{16,8},{20,12},{24,16},{28,20},{9,1},{13,5},{17,9},{2... | collective-permute-start | bytes 1376264 | tf_op jit(solution)/shard_map/cond/branch_0_fun/ppermute | solution.py:468
  29.7 2.1 %branch_0_fun.7.refs_9_ = f32[16,128]{1,0:T(8,128)S(1)} custom-call(s32[1]{0:T(128)} %bitcast.place_ref, s32[9]{0:T(128)S(1)} %get-tuple-element.40.lengths_ref, bf16[1,128,1792]{2,1,0:T(8,128)(2,1)S(1)} %copy-done, bf16[1,128,1792]{2,1,0:T(8,128)(2,1)S(1)} %get-tuple-element.45.o0.refs_1_, bf16[1,128,1792]{2,1,0:T(8,128)(2,1)S(1)} %collective-permute-done.q_mate.q1.refs_2_, ...), custom_call_target="tpu_custom_call" | custom-call | flops 704643072 | bytes 4587520 | tf_op jit(solution)/shard_map/cond/branch_0_fun/pallas_call | solution.py:483
  31.7 1.6 %collective-permute-start.5 = (f32[16,128]{1,0:T(8,128)S(1)}, f32[16,128]{1,0:T(8,128)S(1)}, u32[]{:S(2)}, u32[]{:S(2)}) collective-permute-start(f32[16,128]{1,0:T(8,128)S(1)} %branch_0_fun.7.refs_9_), channel_id=1, source_target_pairs={{0,4},{4,0},{8,12},{12,8},{16,20},{20,16},{24,28},{28,24},{1,5},{5... | collective-permute-start | bytes 24584 | tf_op jit(solution)/shard_map/cond/branch_0_fun/ppermute | solution.py:468
  33.3 2.1 %collective-permute-done.5.refs_10_ = f32[16,128]{1,0:T(8,128)S(1)} collective-permute-done((f32[16,128]{1,0:T(8,128)S(1)}, f32[16,128]{1,0:T(8,128)S(1)}, u32[]{:S(2)}, u32[]{:S(2)}) %collective-permute-start.5) | collective-permute-done | bytes 8224 | tf_op jit(solution)/shard_map/cond/branch_0_fun/ppermute | solution.py:468
  35.5 3.1 %branch_0_fun.8 = (bf16[1,128,1792]{2,1,0:T(8,128)(2,1)S(1)}, bf16[1,128,1792]{2,1,0:T(8,128)(2,1)S(1)}, bf16[1,128,1792]{2,1,0:T(8,128)(2,1)S(1)}, bf16[1,128,1792]{2,1,0:T(8,128)(2,1)S(1)}) custom-call(s32[1]{0:T(128)} %bitcast.place_ref, s32[9]{0:T(128)S(1)} %get-tuple-element.40.lengths_ref, bf16[1,128,1792]{2,1,0:T(8,128)(2,1)S(1)} %copy-done, ...), custom_call_target="tpu_custom_call" | custom-call | flops 1409286144 | bytes 4587520 | tf_op jit(solution)/shard_map/cond/branch_0_fun/pallas_call | solution.py:483
  38.6 1.3 %collective-permute-start.6 = (bf16[1,128,1792]{2,1,0:T(8,128)(2,1)S(1)}, bf16[1,128,1792]{2,1,0:T(8,128)(2,1)S(1)}, u32[]{:S(2)}, u32[]{:S(2)}) collective-permute-start(bf16[1,128,1792]{2,1,0:T(8,128)(2,1)S(1)} %get-tuple-element.50), channel_id=1, source_target_pairs={{8,0},{12,4},{16,8},{20,12},{24,16},{28,20},{9,1},{13,5},{17,9},{2... | collective-permute-start | bytes 1376264 | tf_op jit(solution)/shard_map/cond/branch_0_fun/ppermute | solution.py:468
  39.9 1.6 %collective-permute-start.7 = (bf16[1,128,1792]{2,1,0:T(8,128)(2,1)S(1)}, bf16[1,128,1792]{2,1,0:T(8,128)(2,1)S(1)}, u32[]{:S(2)}, u32[]{:S(2)}) collective-permute-start(bf16[1,128,1792]{2,1,0:T(8,128)(2,1)S(1)} %get-tuple-element.52), channel_id=1, source_target_pairs={{0,4},{4,0},{8,12},{12,8},{16,20},{20,16},{24,28},{28,24},{1,5},{5... | collective-permute-start | bytes 1376264 | tf_op jit(solution)/shard_map/cond/branch_0_fun/ppermute | solution.py:468
  41.5 0.3 collective-permute-done.8
  41.8 0.9 %convert_add_fusion = bf16[1,128,1792]{2,1,0:T(8,128)(2,1)} fusion(bf16[1,128,1792]{2,1,0:T(8,128)(2,1)S(1)} %collective-permute-done.8, bf16[1,128,1792]{2,1,0:T(8,128)(2,1)S(1)} %get-tuple-element.55), kind=kLoop, calls=%fused_computation | loop fusion | flops 917504 | bytes 1376256 | tf_op jit(solution)/shard_map/cond/branch_0_fun/add | solution.py:554
  42.7 8.9 %collective-permute-done.6.key_sent = bf16[1,128,1792]{2,1,0:T(8,128)(2,1)S(1)} collective-permute-done((bf16[1,128,1792]{2,1,0:T(8,128)(2,1)S(1)}, bf16[1,128,1792]{2,1,0:T(8,128)(2,1)S(1)}, u32[]{:S(2)}, u32[]{:S(2)}) %collective-permute-start.6) | collective-permute-done | bytes 458784 | tf_op jit(solution)/shard_map/cond/branch_0_fun/ppermute | solution.py:468
  51.6 1.2 %branch_0_fun.9 = (bf16[1,128,1792]{2,1,0:T(8,128)(2,1)}, bf16[1,128,1792]{2,1,0:T(8,128)(2,1)}) custom-call(bf16[1,128,1792]{2,1,0:T(8,128)(2,1)S(1)} %get-tuple-element.49.key_part, bf16[1,128,1792]{2,1,0:T(8,128)(2,1)S(1)} %collective-permute-done.6.key_sent, bf16[1,128,1792]{2,1,0:T(8,128)(2,1)S(1)} %get-tuple-element.51.refs_0_, ...), custom_call_target="tpu_custom_call" | custom-call | bytes 4587520 | tf_op jit(solution)/shard_map/cond/branch_0_fun/pallas_call | solution.py:483
  (6 shorter events, 0.0 us)
Async XLA Ops:
  2.0 14.6 %collective-permute-start = (bf16[1,128,1792]{2,1,0:T(8,128)(2,1)}, bf16[1,128,1792]{2,1,0:T(8,128)(2,1)S(1)}, u32[]{:S(2)}, u32[]{:S(2)}) collective-permute-start(bf16[1,128,1792]{2,1,0:T(8,128)(2,1)} %get-tuple-element.125.q_own.q0.refs_0_), channel_id=1, source_target_pairs={{0,4},{4,0},{8,12},{12,8},{16,20},{20,16},{24,28},{28,24},{1,5},{5... | collective-permute-start | bytes 1376264 | tf_op jit(solution)/shard_map/cond/branch_0_fun/ppermute | solution.py:468
  5.0 14.7 %collective-permute-start.1 = (bf16[1,128,1792]{2,1,0:T(8,128)(2,1)}, bf16[1,128,1792]{2,1,0:T(8,128)(2,1)S(1)}, u32[]{:S(2)}, u32[]{:S(2)}) collective-permute-start(bf16[1,128,1792]{2,1,0:T(8,128)(2,1)} %get-tuple-element.128.k_own.k0.refs_4_), channel_id=1, source_target_pairs={{0,8},{4,12},{8,16},{12,20},{16,24},{20,28},{1,9},{5,13},{9,17},{1... | collective-permute-start | bytes 1376264 | tf_op jit(solution)/shard_map/cond/branch_0_fun/ppermute | solution.py:468
  8.5 17.2 %collective-permute-start.2 = (bf16[1,128,1792]{2,1,0:T(8,128)(2,1)}, bf16[1,128,1792]{2,1,0:T(8,128)(2,1)S(1)}, u32[]{:S(2)}, u32[]{:S(2)}) collective-permute-start(bf16[1,128,1792]{2,1,0:T(8,128)(2,1)} %get-tuple-element.131.o_own), channel_id=1, source_target_pairs={{0,4},{4,0},{8,12},{12,8},{16,20},{20,16},{24,28},{28,24},{1,5},{5... | collective-permute-start | bytes 1376264 | tf_op jit(solution)/shard_map/cond/branch_0_fun/ppermute | solution.py:468
  9.1 20.6 %collective-permute-start.3 = (bf16[1,128,1792]{2,1,0:T(8,128)(2,1)}, bf16[1,128,1792]{2,1,0:T(8,128)(2,1)S(1)}, u32[]{:S(2)}, u32[]{:S(2)}) collective-permute-start(bf16[1,128,1792]{2,1,0:T(8,128)(2,1)} %get-tuple-element.134.v_own), channel_id=1, source_target_pairs={{0,8},{4,12},{8,16},{12,20},{16,24},{20,28},{24,0},{28,4},{1,9},{5... | collective-permute-start | bytes 1376264 | tf_op jit(solution)/shard_map/cond/branch_0_fun/ppermute | solution.py:468
  19.7 6.4 %copy-start = (bf16[1,128,1792]{2,1,0:T(8,128)(2,1)S(1)}, bf16[1,128,1792]{2,1,0:T(8,128)(2,1)}, u32[]{:S(2)}) copy-start(bf16[1,128,1792]{2,1,0:T(8,128)(2,1)} %get-tuple-element.125.q_own.q0.refs_0_) | copy-start | bytes 1376260
  19.7 6.4 %copy-start.3 = (bf16[1,128,1792]{2,1,0:T(8,128)(2,1)S(1)}, bf16[1,128,1792]{2,1,0:T(8,128)(2,1)}, u32[]{:S(2)}) copy-start(bf16[1,128,1792]{2,1,0:T(8,128)(2,1)} %get-tuple-element.128.k_own.k0.refs_4_) | copy-start | bytes 1376260
  22.3 3.8 %collective-permute-start.4 = (f32[32,128]{1,0:T(8,128)S(1)}, f32[32,128]{1,0:T(8,128)S(1)}, u32[]{:S(2)}, u32[]{:S(2)}) collective-permute-start(f32[32,128]{1,0:T(8,128)S(1)} %get-tuple-element.47.refs_0_), channel_id=1, source_target_pairs={{0,4},{4,0},{8,12},{12,8},{16,20},{20,16},{24,28},{28,24},{1,5},{5... | collective-permute-start | bytes 49160 | tf_op jit(solution)/shard_map/cond/branch_0_fun/ppermute | solution.py:468
  28.3 13.4 %collective-permute-start.8 = (bf16[1,128,1792]{2,1,0:T(8,128)(2,1)S(1)}, bf16[1,128,1792]{2,1,0:T(8,128)(2,1)S(1)}, u32[]{:S(2)}, u32[]{:S(2)}) collective-permute-start(bf16[1,128,1792]{2,1,0:T(8,128)(2,1)S(1)} %get-tuple-element.56), channel_id=1, source_target_pairs={{8,0},{12,4},{16,8},{20,12},{24,16},{28,20},{9,1},{13,5},{17,9},{2... | collective-permute-start | bytes 1376264 | tf_op jit(solution)/shard_map/cond/branch_0_fun/ppermute | solution.py:468
  31.7 3.7 %collective-permute-start.5 = (f32[16,128]{1,0:T(8,128)S(1)}, f32[16,128]{1,0:T(8,128)S(1)}, u32[]{:S(2)}, u32[]{:S(2)}) collective-permute-start(f32[16,128]{1,0:T(8,128)S(1)} %branch_0_fun.7.refs_9_), channel_id=1, source_target_pairs={{0,4},{4,0},{8,12},{12,8},{16,20},{20,16},{24,28},{28,24},{1,5},{5... | collective-permute-start | bytes 24584 | tf_op jit(solution)/shard_map/cond/branch_0_fun/ppermute | solution.py:468
  38.6 13.0 %collective-permute-start.6 = (bf16[1,128,1792]{2,1,0:T(8,128)(2,1)S(1)}, bf16[1,128,1792]{2,1,0:T(8,128)(2,1)S(1)}, u32[]{:S(2)}, u32[]{:S(2)}) collective-permute-start(bf16[1,128,1792]{2,1,0:T(8,128)(2,1)S(1)} %get-tuple-element.50), channel_id=1, source_target_pairs={{8,0},{12,4},{16,8},{20,12},{24,16},{28,20},{9,1},{13,5},{17,9},{2... | collective-permute-start | bytes 1376264 | tf_op jit(solution)/shard_map/cond/branch_0_fun/ppermute | solution.py:468
  39.9 11.7 %collective-permute-start.7 = (bf16[1,128,1792]{2,1,0:T(8,128)(2,1)S(1)}, bf16[1,128,1792]{2,1,0:T(8,128)(2,1)S(1)}, u32[]{:S(2)}, u32[]{:S(2)}) collective-permute-start(bf16[1,128,1792]{2,1,0:T(8,128)(2,1)S(1)} %get-tuple-element.52), channel_id=1, source_target_pairs={{0,4},{4,0},{8,12},{12,8},{16,20},{20,16},{24,28},{28,24},{1,5},{5... | collective-permute-start | bytes 1376264 | tf_op jit(solution)/shard_map/cond/branch_0_fun/ppermute | solution.py:468

commit v4 on v3

--- a/solution.py
+++ b/solution.py
@@ -503,14 +503,14 @@
         functools.partial(stats_kernel, heads, power), 1,
         [queries, query_mate, key_vectors, key_back, out_grad, value_vectors], [], 2, [(2, 2)],
     )
-    stats_in = [(2, 2, stats), (2, 2, send(stats, mates))]
+    stats_mate = send(stats, mates)
     rows_in = [queries, grad_own, query_mate, grad_mate]
     tensors = rows_in + [key_vectors, value_own, key_back, value_back]
     constants = (heads, scaling, power)
     if ring:
         value_part, value_sent, shift = call(
             functools.partial(values_kernel, True, *constants), 2, rows_in + [key_vectors, key_back],
-            stats_in, 2, [(2, 1)],
+            [(2, 2, stats), (2, 2, stats_mate)], 2, [(2, 1)],
         )
         (dots,) = call(
             functools.partial(dots_kernel, False, *constants), 2, tensors, [(2, 1, shift)], 0, [(2, 1)]
@@ -520,29 +520,31 @@
     else:
         query_third = send(query_mate, relay)
         even_stats, odd_stats = send(stats, from_even), send(stats, relay)
-        held, even_stats, odd_stats = lax.optimization_barrier((grad_mate, even_stats, odd_stats))
+        held, odd_stats, stats_mate = lax.optimization_barrier((grad_mate, odd_stats, stats_mate))
         grad_third = send(held, relay)
-        query_third, _ = lax.optimization_barrier((query_third, value_back))
+        query_third, even_stats, _ = lax.optimization_barrier((query_third, even_stats, value_back))
         (third_stats,) = call(
             functools.partial(third_stats_kernel, third, heads, power), 1, [query_third, key_back], [],
             0, [(1, 2)],
         )
+        stats_in = [(2, 2, stats), (2, 2, stats_mate)]
         stats_in += [(1, 2, send(third_stats, to_even)), (1, 2, send(third_stats, to_odd))]
         dots, shift = call(
             functools.partial(dots_kernel, True, *constants), 2, tensors, stats_in, 0, [(2, 1), (2, 1)]
         )
-        even_dots, odd_dots = send(dots, from_even), send(dots, relay)
+        even_dots, odd_dots, dots_mate = (send(dots, pairs) for pairs in (from_even, relay, mates))
         value_part, value_back_part = call(
             functools.partial(values_kernel, False, *constants), 2, rows_in + [key_vectors, key_back],
             [(2, 1, shift)], 2, [],
         )
+        value_back_part, dots_mate = lax.optimization_barrier((value_back_part, dots_mate))
         value_sent, key_third, query_extra, third_dots = call(
             functools.partial(third_kernel, third, *constants), 2,
             [query_third, grad_third, key_back, value_back, value_back_part],
             [(1, 2, third_stats), (2, 2, even_stats), (2, 2, odd_stats), (2, 1, even_dots), (2, 1, odd_dots)],
             3, [(1, 1)], scratch=[1],
         )
-        dots_in = [(2, 1, shift), (2, 1, dots), (2, 1, send(dots, mates))]
+        dots_in = [(2, 1, shift), (2, 1, dots), (2, 1, dots_mate)]
         dots_in += [(1, 1, send(third_dots, to_even)), (1, 1, send(third_dots, to_odd))]
         base = [key_third]
     value_received = send(value_sent, behind)

time: 52.9 us -> 52.9 us (level)
  no operation moved by 1% of the time
where the time goes in v4:
time: 52.9 us; the launch traced here: 52.7 us
  waiting for transfers between devices  23.6 us (45%)
  starting transfers between devices  15 us (28%)
  Pallas kernels  12.4 us (23%)
  other arithmetic  0.87 us (2%)
  between operations  0.67 us (1%)
    ppermute x9, waiting for transfers between devices, send(): return lax.ppermute(value, 'seq', pairs)  23.6 us
    ppermute x9, starting transfers between devices, send(): return lax.ppermute(value, 'seq', pairs)  15 us
    pallas_call x5, Pallas kernels, call(): pl.pallas_call(kernel, grid=(steps,), in_specs=[smem] * len(lead) + [wide...  11.2 us
    pallas_call x1, Pallas kernels, program_facts(): pl.pallas_call(functools.partial(program_kernel, rows.bit_length() - 1),...  1.29 us
  transfers between devices with their start and end apart: 9, of which 7 were waited for; matrix products, arithmetic and copies ran while one was open for 2% of the time, Pallas kernels for 19%

profile of v4, /device:TPU:0, one launch (start us, length us, event | category | flops | bytes accessed | tf_op | source)
XLA Modules:
  0.0 52.7 jit_solution(4557705034003906545)
XLA Ops:
  0.6 1.3 %shard_map.91 = s32[9]{0:T(128)S(1)} custom-call(s32[8]{0:T(128)} %lengths_ref.1), custom_call_target="tpu_custom_call" | custom-call | tf_op jit(solution)/shard_map/pallas_call | solution.py:577
  2.0 50.8 %conditional.4 = (bf16[1,128,1792]{2,1,0:T(8,128)(2,1)}, bf16[1,128,1792]{2,1,0:T(8,128)(2,1)}, bf16[1,128,1792]{2,1,0:T(8,128)(2,1)}) conditional(s32[]{:T(128)} %bitcast.3, (bf16[1,128,1792]{2,1,0:T(8,128)(2,1)}, bf16[1,128,1792]{2,1,0:T(8,128)(2,1)}, s32[9]{0:T(128)S(1)}, bf16[1,128,1792]{2,1,0:T(8,128)(2,1)}, ...), branch_computations={%region_0.0_spmd, %region_1.0_spmd, %region_2.0_spmd} | conditional | flops 4228775936 | bytes 55903120
  2.0 3.0 %collective-permute-start = (bf16[1,128,1792]{2,1,0:T(8,128)(2,1)}, bf16[1,128,1792]{2,1,0:T(8,128)(2,1)S(1)}, u32[]{:S(2)}, u32[]{:S(2)}) collective-permute-start(bf16[1,128,1792]{2,1,0:T(8,128)(2,1)} %get-tuple-element.131.q_own.q0.refs_0_), channel_id=1, source_target_pairs={{0,4},{4,0},{8,12},{12,8},{16,20},{20,16},{24,28},{28,24},{1,5},{5... | collective-permute-start | bytes 1376264 | tf_op jit(solution)/shard_map/cond/branch_0_fun/ppermute | solution.py:468
  5.0 3.5 %collective-permute-start.1 = (bf16[1,128,1792]{2,1,0:T(8,128)(2,1)}, bf16[1,128,1792]{2,1,0:T(8,128)(2,1)S(1)}, u32[]{:S(2)}, u32[]{:S(2)}) collective-permute-start(bf16[1,128,1792]{2,1,0:T(8,128)(2,1)} %get-tuple-element.134.k_own.k0.refs_4_), channel_id=1, source_target_pairs={{0,8},{4,12},{8,16},{12,20},{16,24},{20,28},{1,9},{5,13},{9,17},{1... | collective-permute-start | bytes 1376264 | tf_op jit(solution)/shard_map/cond/branch_0_fun/ppermute | solution.py:468
  8.5 0.6 %collective-permute-start.2 = (bf16[1,128,1792]{2,1,0:T(8,128)(2,1)}, bf16[1,128,1792]{2,1,0:T(8,128)(2,1)S(1)}, u32[]{:S(2)}, u32[]{:S(2)}) collective-permute-start(bf16[1,128,1792]{2,1,0:T(8,128)(2,1)} %get-tuple-element.137.o_own), channel_id=1, source_target_pairs={{0,4},{4,0},{8,12},{12,8},{16,20},{20,16},{24,28},{28,24},{1,5},{5... | collective-permute-start | bytes 1376264 | tf_op jit(solution)/shard_map/cond/branch_0_fun/ppermute | solution.py:468
  9.1 1.6 %collective-permute-start.3 = (bf16[1,128,1792]{2,1,0:T(8,128)(2,1)}, bf16[1,128,1792]{2,1,0:T(8,128)(2,1)S(1)}, u32[]{:S(2)}, u32[]{:S(2)}) collective-permute-start(bf16[1,128,1792]{2,1,0:T(8,128)(2,1)} %get-tuple-element.140.v_own), channel_id=1, source_target_pairs={{0,8},{4,12},{8,16},{12,20},{16,24},{20,28},{24,0},{28,4},{1,9},{5... | collective-permute-start | bytes 1376264 | tf_op jit(solution)/shard_map/cond/branch_0_fun/ppermute | solution.py:468
  10.6 5.9 %collective-permute-done.q_mate.q1.refs_2_ = bf16[1,128,1792]{2,1,0:T(8,128)(2,1)S(1)} collective-permute-done((bf16[1,128,1792]{2,1,0:T(8,128)(2,1)}, bf16[1,128,1792]{2,1,0:T(8,128)(2,1)S(1)}, u32[]{:S(2)}, u32[]{:S(2)}) %collective-permute-start) | collective-permute-done | bytes 458784 | tf_op jit(solution)/shard_map/cond/branch_0_fun/ppermute | solution.py:468
  16.5 3.2 %collective-permute-done.1.k_back.k1.refs_6_ = bf16[1,128,1792]{2,1,0:T(8,128)(2,1)S(1)} collective-permute-done((bf16[1,128,1792]{2,1,0:T(8,128)(2,1)}, bf16[1,128,1792]{2,1,0:T(8,128)(2,1)S(1)}, u32[]{:S(2)}, u32[]{:S(2)}) %collective-permute-start.1) | collective-permute-done | bytes 458784 | tf_op jit(solution)/shard_map/cond/branch_0_fun/ppermute | solution.py:468
  19.7 2.6 %branch_0_fun.5 = (bf16[1,128,1792]{2,1,0:T(8,128)(2,1)S(1)}, bf16[1,128,1792]{2,1,0:T(8,128)(2,1)S(1)}, f32[32,128]{1,0:T(8,128)S(1)}) custom-call(s32[1]{0:T(128)} %bitcast.place_ref, s32[9]{0:T(128)S(1)} %get-tuple-element.40.lengths_ref, bf16[1,128,1792]{2,1,0:T(8,128)(2,1)} %get-tuple-element.131.q_own.q0.refs_0_, ...), custom_call_target="tpu_custom_call" | custom-call | flops 352321536 | bytes 4587520 | tf_op jit(solution)/shard_map/cond/branch_0_fun/pallas_call | solution.py:483
  22.3 0.6 %collective-permute-start.4 = (f32[32,128]{1,0:T(8,128)S(1)}, f32[32,128]{1,0:T(8,128)S(1)}, u32[]{:S(2)}, u32[]{:S(2)}) collective-permute-start(f32[32,128]{1,0:T(8,128)S(1)} %get-tuple-element.47.refs_0_), channel_id=1, source_target_pairs={{0,4},{4,0},{8,12},{12,8},{16,20},{20,16},{24,28},{28,24},{1,5},{5... | collective-permute-start | bytes 49160 | tf_op jit(solution)/shard_map/cond/branch_0_fun/ppermute | solution.py:468
  22.9 2.8 %collective-permute-done.2.o1.refs_3_ = bf16[1,128,1792]{2,1,0:T(8,128)(2,1)S(1)} collective-permute-done((bf16[1,128,1792]{2,1,0:T(8,128)(2,1)}, bf16[1,128,1792]{2,1,0:T(8,128)(2,1)S(1)}, u32[]{:S(2)}, u32[]{:S(2)}) %collective-permute-start.2) | collective-permute-done | bytes 458784 | tf_op jit(solution)/shard_map/cond/branch_0_fun/ppermute | solution.py:468
  25.7 0.4 collective-permute-done.4.refs_1_
  26.1 2.2 %branch_0_fun.6 = (bf16[1,128,1792]{2,1,0:T(8,128)(2,1)S(1)}, bf16[1,128,1792]{2,1,0:T(8,128)(2,1)S(1)}, f32[16,128]{1,0:T(8,128)S(1)}) custom-call(s32[1]{0:T(128)} %bitcast.place_ref, s32[9]{0:T(128)S(1)} %get-tuple-element.40.lengths_ref, bf16[1,128,1792]{2,1,0:T(8,128)(2,1)S(1)} %copy-done, bf16[1,128,1792]{2,1,0:T(8,128)(2,1)S(1)} %get-tuple-element.45.o0.refs_1_, ...), custom_call_target="tpu_custom_call" | custom-call | flops 704643072 | bytes 4587520 | tf_op jit(solution)/shard_map/cond/branch_0_fun/pallas_call | solution.py:483
  28.3 1.3 %collective-permute-start.8 = (bf16[1,128,1792]{2,1,0:T(8,128)(2,1)S(1)}, bf16[1,128,1792]{2,1,0:T(8,128)(2,1)S(1)}, u32[]{:S(2)}, u32[]{:S(2)}) collective-permute-start(bf16[1,128,1792]{2,1,0:T(8,128)(2,1)S(1)} %get-tuple-element.56), channel_id=1, source_target_pairs={{8,0},{12,4},{16,8},{20,12},{24,16},{28,20},{9,1},{13,5},{17,9},{2... | collective-permute-start | bytes 1376264 | tf_op jit(solution)/shard_map/cond/branch_0_fun/ppermute | solution.py:468
  29.7 2.1 %branch_0_fun.7.refs_9_ = f32[16,128]{1,0:T(8,128)S(1)} custom-call(s32[1]{0:T(128)} %bitcast.place_ref, s32[9]{0:T(128)S(1)} %get-tuple-element.40.lengths_ref, bf16[1,128,1792]{2,1,0:T(8,128)(2,1)S(1)} %copy-done, bf16[1,128,1792]{2,1,0:T(8,128)(2,1)S(1)} %get-tuple-element.45.o0.refs_1_, bf16[1,128,1792]{2,1,0:T(8,128)(2,1)S(1)} %collective-permute-done.q_mate.q1.refs_2_, ...), custom_call_target="tpu_custom_call" | custom-call | flops 704643072 | bytes 4587520 | tf_op jit(solution)/shard_map/cond/branch_0_fun/pallas_call | solution.py:483
  31.7 1.6 %collective-permute-start.5 = (f32[16,128]{1,0:T(8,128)S(1)}, f32[16,128]{1,0:T(8,128)S(1)}, u32[]{:S(2)}, u32[]{:S(2)}) collective-permute-start(f32[16,128]{1,0:T(8,128)S(1)} %branch_0_fun.7.refs_9_), channel_id=1, source_target_pairs={{0,4},{4,0},{8,12},{12,8},{16,20},{20,16},{24,28},{28,24},{1,5},{5... | collective-permute-start | bytes 24584 | tf_op jit(solution)/shard_map/cond/branch_0_fun/ppermute | solution.py:468
  33.3 2.1 %collective-permute-done.5.refs_10_ = f32[16,128]{1,0:T(8,128)S(1)} collective-permute-done((f32[16,128]{1,0:T(8,128)S(1)}, f32[16,128]{1,0:T(8,128)S(1)}, u32[]{:S(2)}, u32[]{:S(2)}) %collective-permute-start.5) | collective-permute-done | bytes 8224 | tf_op jit(solution)/shard_map/cond/branch_0_fun/ppermute | solution.py:468
  35.5 3.1 %branch_0_fun.8 = (bf16[1,128,1792]{2,1,0:T(8,128)(2,1)S(1)}, bf16[1,128,1792]{2,1,0:T(8,128)(2,1)S(1)}, bf16[1,128,1792]{2,1,0:T(8,128)(2,1)S(1)}, bf16[1,128,1792]{2,1,0:T(8,128)(2,1)S(1)}) custom-call(s32[1]{0:T(128)} %bitcast.place_ref, s32[9]{0:T(128)S(1)} %get-tuple-element.40.lengths_ref, bf16[1,128,1792]{2,1,0:T(8,128)(2,1)S(1)} %copy-done, ...), custom_call_target="tpu_custom_call" | custom-call | flops 1409286144 | bytes 4587520 | tf_op jit(solution)/shard_map/cond/branch_0_fun/pallas_call | solution.py:483
  38.6 1.3 %collective-permute-start.6 = (bf16[1,128,1792]{2,1,0:T(8,128)(2,1)S(1)}, bf16[1,128,1792]{2,1,0:T(8,128)(2,1)S(1)}, u32[]{:S(2)}, u32[]{:S(2)}) collective-permute-start(bf16[1,128,1792]{2,1,0:T(8,128)(2,1)S(1)} %get-tuple-element.50), channel_id=1, source_target_pairs={{8,0},{12,4},{16,8},{20,12},{24,16},{28,20},{9,1},{13,5},{17,9},{2... | collective-permute-start | bytes 1376264 | tf_op jit(solution)/shard_map/cond/branch_0_fun/ppermute | solution.py:468
  39.9 1.6 %collective-permute-start.7 = (bf16[1,128,1792]{2,1,0:T(8,128)(2,1)S(1)}, bf16[1,128,1792]{2,1,0:T(8,128)(2,1)S(1)}, u32[]{:S(2)}, u32[]{:S(2)}) collective-permute-start(bf16[1,128,1792]{2,1,0:T(8,128)(2,1)S(1)} %get-tuple-element.52), channel_id=1, source_target_pairs={{0,4},{4,0},{8,12},{12,8},{16,20},{20,16},{24,28},{28,24},{1,5},{5... | collective-permute-start | bytes 1376264 | tf_op jit(solution)/shard_map/cond/branch_0_fun/ppermute | solution.py:468
  41.5 0.3 collective-permute-done.8
  41.8 0.9 %convert_add_fusion = bf16[1,128,1792]{2,1,0:T(8,128)(2,1)} fusion(bf16[1,128,1792]{2,1,0:T(8,128)(2,1)S(1)} %collective-permute-done.8, bf16[1,128,1792]{2,1,0:T(8,128)(2,1)S(1)} %get-tuple-element.55), kind=kLoop, calls=%fused_computation | loop fusion | flops 917504 | bytes 1376256 | tf_op jit(solution)/shard_map/cond/branch_0_fun/add | solution.py:556
  42.7 8.9 %collective-permute-done.6.key_sent = bf16[1,128,1792]{2,1,0:T(8,128)(2,1)S(1)} collective-permute-done((bf16[1,128,1792]{2,1,0:T(8,128)(2,1)S(1)}, bf16[1,128,1792]{2,1,0:T(8,128)(2,1)S(1)}, u32[]{:S(2)}, u32[]{:S(2)}) %collective-permute-start.6) | collective-permute-done | bytes 458784 | tf_op jit(solution)/shard_map/cond/branch_0_fun/ppermute | solution.py:468
  51.6 1.2 %branch_0_fun.9 = (bf16[1,128,1792]{2,1,0:T(8,128)(2,1)}, bf16[1,128,1792]{2,1,0:T(8,128)(2,1)}) custom-call(bf16[1,128,1792]{2,1,0:T(8,128)(2,1)S(1)} %get-tuple-element.49.key_part, bf16[1,128,1792]{2,1,0:T(8,128)(2,1)S(1)} %collective-permute-done.6.key_sent, bf16[1,128,1792]{2,1,0:T(8,128)(2,1)S(1)} %get-tuple-element.51.refs_0_, ...), custom_call_target="tpu_custom_call" | custom-call | bytes 4587520 | tf_op jit(solution)/shard_map/cond/branch_0_fun/pallas_call | solution.py:483
  (6 shorter events, 0.0 us)
Async XLA Ops:
  2.0 14.6 %collective-permute-start = (bf16[1,128,1792]{2,1,0:T(8,128)(2,1)}, bf16[1,128,1792]{2,1,0:T(8,128)(2,1)S(1)}, u32[]{:S(2)}, u32[]{:S(2)}) collective-permute-start(bf16[1,128,1792]{2,1,0:T(8,128)(2,1)} %get-tuple-element.131.q_own.q0.refs_0_), channel_id=1, source_target_pairs={{0,4},{4,0},{8,12},{12,8},{16,20},{20,16},{24,28},{28,24},{1,5},{5... | collective-permute-start | bytes 1376264 | tf_op jit(solution)/shard_map/cond/branch_0_fun/ppermute | solution.py:468
  5.0 14.7 %collective-permute-start.1 = (bf16[1,128,1792]{2,1,0:T(8,128)(2,1)}, bf16[1,128,1792]{2,1,0:T(8,128)(2,1)S(1)}, u32[]{:S(2)}, u32[]{:S(2)}) collective-permute-start(bf16[1,128,1792]{2,1,0:T(8,128)(2,1)} %get-tuple-element.134.k_own.k0.refs_4_), channel_id=1, source_target_pairs={{0,8},{4,12},{8,16},{12,20},{16,24},{20,28},{1,9},{5,13},{9,17},{1... | collective-permute-start | bytes 1376264 | tf_op jit(solution)/shard_map/cond/branch_0_fun/ppermute | solution.py:468
  8.5 17.2 %collective-permute-start.2 = (bf16[1,128,1792]{2,1,0:T(8,128)(2,1)}, bf16[1,128,1792]{2,1,0:T(8,128)(2,1)S(1)}, u32[]{:S(2)}, u32[]{:S(2)}) collective-permute-start(bf16[1,128,1792]{2,1,0:T(8,128)(2,1)} %get-tuple-element.137.o_own), channel_id=1, source_target_pairs={{0,4},{4,0},{8,12},{12,8},{16,20},{20,16},{24,28},{28,24},{1,5},{5... | collective-permute-start | bytes 1376264 | tf_op jit(solution)/shard_map/cond/branch_0_fun/ppermute | solution.py:468
  9.1 20.6 %collective-permute-start.3 = (bf16[1,128,1792]{2,1,0:T(8,128)(2,1)}, bf16[1,128,1792]{2,1,0:T(8,128)(2,1)S(1)}, u32[]{:S(2)}, u32[]{:S(2)}) collective-permute-start(bf16[1,128,1792]{2,1,0:T(8,128)(2,1)} %get-tuple-element.140.v_own), channel_id=1, source_target_pairs={{0,8},{4,12},{8,16},{12,20},{16,24},{20,28},{24,0},{28,4},{1,9},{5... | collective-permute-start | bytes 1376264 | tf_op jit(solution)/shard_map/cond/branch_0_fun/ppermute | solution.py:468
  19.7 6.4 %copy-start = (bf16[1,128,1792]{2,1,0:T(8,128)(2,1)S(1)}, bf16[1,128,1792]{2,1,0:T(8,128)(2,1)}, u32[]{:S(2)}) copy-start(bf16[1,128,1792]{2,1,0:T(8,128)(2,1)} %get-tuple-element.131.q_own.q0.refs_0_) | copy-start | bytes 1376260
  19.7 6.4 %copy-start.3 = (bf16[1,128,1792]{2,1,0:T(8,128)(2,1)S(1)}, bf16[1,128,1792]{2,1,0:T(8,128)(2,1)}, u32[]{:S(2)}) copy-start(bf16[1,128,1792]{2,1,0:T(8,128)(2,1)} %get-tuple-element.134.k_own.k0.refs_4_) | copy-start | bytes 1376260
  22.3 3.8 %collective-permute-start.4 = (f32[32,128]{1,0:T(8,128)S(1)}, f32[32,128]{1,0:T(8,128)S(1)}, u32[]{:S(2)}, u32[]{:S(2)}) collective-permute-start(f32[32,128]{1,0:T(8,128)S(1)} %get-tuple-element.47.refs_0_), channel_id=1, source_target_pairs={{0,4},{4,0},{8,12},{12,8},{16,20},{20,16},{24,28},{28,24},{1,5},{5... | collective-permute-start | bytes 49160 | tf_op jit(solution)/shard_map/cond/branch_0_fun/ppermute | solution.py:468
  28.3 13.4 %collective-permute-start.8 = (bf16[1,128,1792]{2,1,0:T(8,128)(2,1)S(1)}, bf16[1,128,1792]{2,1,0:T(8,128)(2,1)S(1)}, u32[]{:S(2)}, u32[]{:S(2)}) collective-permute-start(bf16[1,128,1792]{2,1,0:T(8,128)(2,1)S(1)} %get-tuple-element.56), channel_id=1, source_target_pairs={{8,0},{12,4},{16,8},{20,12},{24,16},{28,20},{9,1},{13,5},{17,9},{2... | collective-permute-start | bytes 1376264 | tf_op jit(solution)/shard_map/cond/branch_0_fun/ppermute | solution.py:468
  31.7 3.7 %collective-permute-start.5 = (f32[16,128]{1,0:T(8,128)S(1)}, f32[16,128]{1,0:T(8,128)S(1)}, u32[]{:S(2)}, u32[]{:S(2)}) collective-permute-start(f32[16,128]{1,0:T(8,128)S(1)} %branch_0_fun.7.refs_9_), channel_id=1, source_target_pairs={{0,4},{4,0},{8,12},{12,8},{16,20},{20,16},{24,28},{28,24},{1,5},{5... | collective-permute-start | bytes 24584 | tf_op jit(solution)/shard_map/cond/branch_0_fun/ppermute | solution.py:468
  38.6 13.0 %collective-permute-start.6 = (bf16[1,128,1792]{2,1,0:T(8,128)(2,1)S(1)}, bf16[1,128,1792]{2,1,0:T(8,128)(2,1)S(1)}, u32[]{:S(2)}, u32[]{:S(2)}) collective-permute-start(bf16[1,128,1792]{2,1,0:T(8,128)(2,1)S(1)} %get-tuple-element.50), channel_id=1, source_target_pairs={{8,0},{12,4},{16,8},{20,12},{24,16},{28,20},{9,1},{13,5},{17,9},{2... | collective-permute-start | bytes 1376264 | tf_op jit(solution)/shard_map/cond/branch_0_fun/ppermute | solution.py:468
  39.9 11.7 %collective-permute-start.7 = (bf16[1,128,1792]{2,1,0:T(8,128)(2,1)S(1)}, bf16[1,128,1792]{2,1,0:T(8,128)(2,1)S(1)}, u32[]{:S(2)}, u32[]{:S(2)}) collective-permute-start(bf16[1,128,1792]{2,1,0:T(8,128)(2,1)S(1)} %get-tuple-element.52), channel_id=1, source_target_pairs={{0,4},{4,0},{8,12},{12,8},{16,20},{20,16},{24,28},{28,24},{1,5},{5... | collective-permute-start | bytes 1376264 | tf_op jit(solution)/shard_map/cond/branch_0_fun/ppermute | solution.py:468

commit v5 on v4

--- a/solution.py
+++ b/solution.py
@@ -371,8 +371,9 @@
 def dots_kernel(merge, heads, scaling, power, place_ref, lengths_ref, *refs):
     queries, keys, refs = split_refs(refs)
     if merge:
-        *stats, dots_ref, shift_ref = refs
+        *stats, bundle_ref, dots_ref, shift_ref = refs
         merge_groups(scaling, shift_ref, stats)
+        bundle_ref[: 4 * GROUP] = stats[0][...]
     else:
         shift_ref, dots_ref = refs
     rows, me, step = keys[0][0].shape[1], place_ref[0], pl.program_id(0)
@@ -385,6 +386,8 @@
             dots = jnp.sum(weight * grads, axis=0, keepdims=True)
             for number, slot in enumerate(query_slots):
                 dots_ref[row_of(slot, 1, 0, at), :] = lane_cut(dots, number, rows)
+                if merge:
+                    bundle_ref[row_of(4 + slot, 1, 0, at), :] = lane_cut(dots, number, rows)
 
 
 def keys_kernel(third, heads, scaling, power, place_ref, lengths_ref, *refs):
@@ -413,10 +416,10 @@
 
 def third_kernel(
     third, heads, scaling, power, place_ref, lengths_ref, q_third, o_third, k_back, v_back, value_part,
-    stats, even_stats, odd_stats, even_dots, odd_dots, value_out, key_out, query_out, dots_ref, shift_ref,
+    stats, even, odd, value_out, key_out, query_out, dots_ref, shift_ref,
 ):
     rows, me, step = k_back.shape[1], place_ref[0], pl.program_id(0)
-    parts = [stats[...], part_of(even_stats, 2, 0), part_of(odd_stats, 2, 1)]
+    parts = [stats[...], part_of(even, 2, 0), part_of(odd, 2, 1)]
     shift_ref[...] = merge_stats(scaling, parts)
     slots, keys, mask = third_tile(third, lengths_ref, rows, me)
     queries, keys = (None, None, (q_third, o_third)), (None, (k_back, v_back))
@@ -428,7 +431,7 @@
         weight = jnp.where(mask, jnp.exp2((raw - shift_ref[pl.ds(at, 1), :]) * power), 0.0)
         dots = jnp.sum(weight * grads, axis=0, keepdims=True)
         dots_ref[pl.ds(at, 1), :] = dots
-        total = dots + even_dots[row_of(0, 1, 0, at), :] + odd_dots[row_of(1, 1, 0, at), :]
+        total = dots + even[row_of(4, 1, 0, at), :] + odd[row_of(5, 1, 0, at), :]
         slope = (weight * (grads - total) * scaling).astype(jnp.bfloat16)
         out.emit(head, "v", matmul(weight.astype(jnp.bfloat16), o * keep, NN))
         out.emit(head, "k", matmul(slope, q * keep, NN))
@@ -519,20 +522,20 @@
         base = []
     else:
         query_third = send(query_mate, relay)
-        even_stats, odd_stats = send(stats, from_even), send(stats, relay)
-        held, odd_stats, stats_mate = lax.optimization_barrier((grad_mate, odd_stats, stats_mate))
+        held, stats_mate = lax.optimization_barrier((grad_mate, stats_mate))
         grad_third = send(held, relay)
-        query_third, even_stats, _ = lax.optimization_barrier((query_third, even_stats, value_back))
+        query_third, _ = lax.optimization_barrier((query_third, value_back))
         (third_stats,) = call(
             functools.partial(third_stats_kernel, third, heads, power), 1, [query_third, key_back], [],
             0, [(1, 2)],
         )
         stats_in = [(2, 2, stats), (2, 2, stats_mate)]
         stats_in += [(1, 2, send(third_stats, to_even)), (1, 2, send(third_stats, to_odd))]
-        dots, shift = call(
-            functools.partial(dots_kernel, True, *constants), 2, tensors, stats_in, 0, [(2, 1), (2, 1)]
-        )
-        even_dots, odd_dots, dots_mate = (send(dots, pairs) for pairs in (from_even, relay, mates))
+        bundle, dots, shift = call(
+            functools.partial(dots_kernel, True, *constants), 2, tensors, stats_in, 0,
+            [(2, 3), (2, 1), (2, 1)],
+        )
+        even, odd, dots_mate = send(bundle, from_even), send(bundle, relay), send(dots, mates)
         value_part, value_back_part = call(
             functools.partial(values_kernel, False, *constants), 2, rows_in + [key_vectors, key_back],
             [(2, 1, shift)], 2, [],
@@ -541,7 +544,7 @@
         value_sent, key_third, query_extra, third_dots = call(
             functools.partial(third_kernel, third, *constants), 2,
             [query_third, grad_third, key_back, value_back, value_back_part],
-            [(1, 2, third_stats), (2, 2, even_stats), (2, 2, odd_stats), (2, 1, even_dots), (2, 1, odd_dots)],
+            [(1, 2, third_stats), (2, 3, even), (2, 3, odd)],
             3, [(1, 1)], scratch=[1],
         )
         dots_in = [(2, 1, shift), (2, 1, dots), (2, 1, dots_mate)]

time: 52.9 us -> 75.4 us (1.43)
  the two profiles are of different devices: /device:TPU:0 before, /device:TPU:20 now
where the time goes in v5:
time: 75.4 us; the launch traced here: 75 us
  waiting for transfers between devices  31.6 us (42%)
  starting transfers between devices  25.3 us (34%)
  Pallas kernels  16.2 us (21%)
  other arithmetic  0.87 us (1%)
    ppermute x18, waiting for transfers between devices, send(): return lax.ppermute(value, 'seq', pairs)  31.6 us
    ppermute x18, starting transfers between devices, send(): return lax.ppermute(value, 'seq', pairs)  25.3 us
    pallas_call x7, Pallas kernels, call(): pl.pallas_call(kernel, grid=(steps,), in_specs=[smem] * len(lead) + [wide...  14.9 us
  transfers between devices with their start and end apart: 18, of which 11 were waited for; matrix products, arithmetic and copies ran while one was open for 1% of the time, Pallas kernels for 15%

profile of v5, /device:TPU:20, one launch (start us, length us, event | category | flops | bytes accessed | tf_op | source)
XLA Modules:
  0.0 75.0 jit_solution(1889138533349579105)
XLA Ops:
  2.0 73.0 %conditional.4 = (bf16[1,128,1792]{2,1,0:T(8,128)(2,1)}, bf16[1,128,1792]{2,1,0:T(8,128)(2,1)}, bf16[1,128,1792]{2,1,0:T(8,128)(2,1)}) conditional(s32[]{:T(128)} %bitcast.3, (bf16[1,128,1792]{2,1,0:T(8,128)(2,1)}, bf16[1,128,1792]{2,1,0:T(8,128)(2,1)}, s32[9]{0:T(128)S(1)}, bf16[1,128,1792]{2,1,0:T(8,128)(2,1)}, ...), branch_computations={%region_0.0_spmd, %region_1.0_spmd, %region_2.0_spmd} | conditional | flops 4228775936 | bytes 55903040
  2.0 1.6 %collective-permute-start.9 = (bf16[1,128,1792]{2,1,0:T(8,128)(2,1)}, bf16[1,128,1792]{2,1,0:T(8,128)(2,1)S(1)}, u32[]{:S(2)}, u32[]{:S(2)}) collective-permute-start(bf16[1,128,1792]{2,1,0:T(8,128)(2,1)} %get-tuple-element.130.q_own.refs_0_.q0), channel_id=1, source_target_pairs={{0,4},{4,0},{8,12},{12,8},{16,20},{20,16},{24,28},{28,24},{1,5},{5... | collective-permute-start | bytes 1376264 | tf_op jit(solution)/shard_map/cond/branch_1_fun/ppermute | solution.py:471
  3.5 3.5 %collective-permute-start.10 = (bf16[1,128,1792]{2,1,0:T(8,128)(2,1)}, bf16[1,128,1792]{2,1,0:T(8,128)(2,1)S(1)}, u32[]{:S(2)}, u32[]{:S(2)}) collective-permute-start(bf16[1,128,1792]{2,1,0:T(8,128)(2,1)} %get-tuple-element.133.k_own.refs_4_.k0), channel_id=1, source_target_pairs={{0,8},{4,12},{8,16},{12,20},{16,24},{20,28},{1,9},{5,13},{9,17},{1... | collective-permute-start | bytes 1376264 | tf_op jit(solution)/shard_map/cond/branch_1_fun/ppermute | solution.py:471
  7.6 1.9 %collective-permute-start.12 = (bf16[1,128,1792]{2,1,0:T(8,128)(2,1)}, bf16[1,128,1792]{2,1,0:T(8,128)(2,1)S(1)}, u32[]{:S(2)}, u32[]{:S(2)}) collective-permute-start(bf16[1,128,1792]{2,1,0:T(8,128)(2,1)} %get-tuple-element.139.v_own), channel_id=1, source_target_pairs={{0,8},{4,12},{8,16},{12,20},{16,24},{20,28},{1,9},{5,13},{9,17},{1... | collective-permute-start | bytes 1376264 | tf_op jit(solution)/shard_map/cond/branch_1_fun/ppermute | solution.py:471
  9.5 6.1 %collective-permute-done.9.q_mate.refs_2_.q1 = bf16[1,128,1792]{2,1,0:T(8,128)(2,1)S(1)} collective-permute-done((bf16[1,128,1792]{2,1,0:T(8,128)(2,1)}, bf16[1,128,1792]{2,1,0:T(8,128)(2,1)S(1)}, u32[]{:S(2)}, u32[]{:S(2)}) %collective-permute-start.9) | collective-permute-done | bytes 458784 | tf_op jit(solution)/shard_map/cond/branch_1_fun/ppermute | solution.py:471
  16.4 2.7 %collective-permute-done.10.k_back.refs_6_.k1 = bf16[1,128,1792]{2,1,0:T(8,128)(2,1)S(1)} collective-permute-done((bf16[1,128,1792]{2,1,0:T(8,128)(2,1)}, bf16[1,128,1792]{2,1,0:T(8,128)(2,1)S(1)}, u32[]{:S(2)}, u32[]{:S(2)}) %collective-permute-start.10) | collective-permute-done | bytes 458784 | tf_op jit(solution)/shard_map/cond/branch_1_fun/ppermute | solution.py:471
  19.1 2.5 %branch_1_fun.7 = (bf16[1,128,1792]{2,1,0:T(8,128)(2,1)S(1)}, bf16[1,128,1792]{2,1,0:T(8,128)(2,1)S(1)}, f32[32,128]{1,0:T(8,128)S(1)}) custom-call(s32[1]{0:T(128)} %bitcast.1.place_ref, s32[9]{0:T(128)S(1)} %get-tuple-element.57.lengths_ref, bf16[1,128,1792]{2,1,0:T(8,128)(2,1)} %get-tuple-element.130.q_own.refs_0_.q0, ...), custom_call_target="tpu_custom_call" | custom-call | flops 352321536 | bytes 4587520 | tf_op jit(solution)/shard_map/cond/branch_1_fun/pallas_call | solution.py:486
  22.2 2.3 %collective-permute-done.11.refs_3_.o1 = bf16[1,128,1792]{2,1,0:T(8,128)(2,1)S(1)} collective-permute-done((bf16[1,128,1792]{2,1,0:T(8,128)(2,1)}, bf16[1,128,1792]{2,1,0:T(8,128)(2,1)S(1)}, u32[]{:S(2)}, u32[]{:S(2)}) %collective-permute-start.11) | collective-permute-done | bytes 458784 | tf_op jit(solution)/shard_map/cond/branch_1_fun/ppermute | solution.py:471
  26.1 1.3 %collective-permute-done.12.refs_7_.v_back = bf16[1,128,1792]{2,1,0:T(8,128)(2,1)S(1)} collective-permute-done((bf16[1,128,1792]{2,1,0:T(8,128)(2,1)}, bf16[1,128,1792]{2,1,0:T(8,128)(2,1)S(1)}, u32[]{:S(2)}, u32[]{:S(2)}) %collective-permute-start.12) | collective-permute-done | bytes 458784 | tf_op jit(solution)/shard_map/cond/branch_1_fun/ppermute | solution.py:471
  28.7 1.3 %collective-permute-start.16 = (f32[16,128]{1,0:T(8,128)S(1)}, f32[16,128]{1,0:T(8,128)S(1)}, u32[]{:S(2)}, u32[]{:S(2)}) collective-permute-start(f32[16,128]{1,0:T(8,128)S(1)} %branch_1_fun.8.stats), channel_id=1, source_target_pairs={{12,16},{13,17},{14,18},{15,19}} | collective-permute-start | bytes 24584 | tf_op jit(solution)/shard_map/cond/branch_1_fun/ppermute | solution.py:471
  30.7 4.5 %collective-permute-done.16.refs_10_ = f32[16,128]{1,0:T(8,128)S(1)} collective-permute-done((f32[16,128]{1,0:T(8,128)S(1)}, f32[16,128]{1,0:T(8,128)S(1)}, u32[]{:S(2)}, u32[]{:S(2)}) %collective-permute-start.16) | collective-permute-done | bytes 8224 | tf_op jit(solution)/shard_map/cond/branch_1_fun/ppermute | solution.py:471
  35.1 2.1 %branch_1_fun.9 = (f32[48,128]{1,0:T(8,128)S(1)}, f32[16,128]{1,0:T(8,128)S(1)}, f32[16,128]{1,0:T(8,128)S(1)}) custom-call(s32[1]{0:T(128)} %bitcast.1.place_ref, s32[9]{0:T(128)S(1)} %get-tuple-element.57.lengths_ref, bf16[1,128,1792]{2,1,0:T(8,128)(2,1)S(1)} %copy-done.1, bf16[1,128,1792]{2,1,0:T(8,128)(2,1)S(1)} %get-tuple-element.62.refs_1_.o0, ...), custom_call_target="tpu_custom_call" | custom-call | flops 704643072 | bytes 4587520 | tf_op jit(solution)/shard_map/cond/branch_1_fun/pallas_call | solution.py:486
  37.3 2.9 %collective-permute-start.19 = (f32[48,128]{1,0:T(8,128)S(1)}, f32[48,128]{1,0:T(8,128)S(1)}, u32[]{:S(2)}, u32[]{:S(2)}) collective-permute-start(f32[48,128]{1,0:T(8,128)S(1)} %get-tuple-element.72), channel_id=1, source_target_pairs={{16,12},{17,13},{18,14},{19,15}} | collective-permute-start | bytes 73736 | tf_op jit(solution)/shard_map/cond/branch_1_fun/ppermute | solution.py:471
  42.1 2.2 %branch_1_fun.10 = (bf16[1,128,1792]{2,1,0:T(8,128)(2,1)S(1)}, bf16[1,128,1792]{2,1,0:T(8,128)(2,1)S(1)}) custom-call(s32[1]{0:T(128)} %bitcast.1.place_ref, s32[9]{0:T(128)S(1)} %get-tuple-element.57.lengths_ref, bf16[1,128,1792]{2,1,0:T(8,128)(2,1)S(1)} %copy-done.1, bf16[1,128,1792]{2,1,0:T(8,128)(2,1)S(1)} %get-tuple-element.62.refs_1_.o0, ...), custom_call_target="tpu_custom_call" | custom-call | flops 704643072 | bytes 4587520 | tf_op jit(solution)/shard_map/cond/branch_1_fun/pallas_call | solution.py:486
  44.6 2.5 %branch_1_fun.11 = (bf16[1,128,1792]{2,1,0:T(8,128)(2,1)S(1)}, bf16[1,128,1792]{2,1,0:T(8,128)(2,1)S(1)}, bf16[1,128,1792]{2,1,0:T(8,128)(2,1)S(1)}, f32[8,128]{1,0:T(8,128)S(1)}) custom-call(s32[1]{0:T(128)} %bitcast.1.place_ref, s32[9]{0:T(128)S(1)} %get-tuple-element.57.lengths_ref, bf16[1,128,1792]{2,1,0:T(8,128)(2,1)S(1)} %collective-permute-done.13.q_third, ...), custom_call_target="tpu_custom_call" | custom-call | flops 704643072 | bytes 4587520 | tf_op jit(solution)/shard_map/cond/branch_1_fun/pallas_call | solution.py:486
  47.1 1.9 %collective-permute-start.26 = (bf16[1,128,1792]{2,1,0:T(8,128)(2,1)S(1)}, bf16[1,128,1792]{2,1,0:T(8,128)(2,1)S(1)}, u32[]{:S(2)}, u32[]{:S(2)}) collective-permute-start(bf16[1,128,1792]{2,1,0:T(8,128)(2,1)S(1)} %get-tuple-element.84), channel_id=1, source_target_pairs={{8,0},{12,4},{16,8},{20,12},{24,16},{28,20},{9,1},{13,5},{17,9},{2... | collective-permute-start | bytes 1376264 | tf_op jit(solution)/shard_map/cond/branch_1_fun/ppermute | solution.py:471
  49.0 1.3 %collective-permute-start.21 = (f32[8,128]{1,0:T(8,128)S(1)}, f32[8,128]{1,0:T(8,128)S(1)}, u32[]{:S(2)}, u32[]{:S(2)}) collective-permute-start(f32[8,128]{1,0:T(8,128)S(1)} %get-tuple-element.75), channel_id=1, source_target_pairs={{12,16},{13,17},{14,18},{15,19}} | collective-permute-start | bytes 12296 | tf_op jit(solution)/shard_map/cond/branch_1_fun/ppermute | solution.py:471
  51.0 1.3 %collective-permute-start.25 = (bf16[1,128,1792]{2,1,0:T(8,128)(2,1)S(1)}, bf16[1,128,1792]{2,1,0:T(8,128)(2,1)S(1)}, u32[]{:S(2)}, u32[]{:S(2)}) collective-permute-start(bf16[1,128,1792]{2,1,0:T(8,128)(2,1)S(1)} %get-tuple-element.80), channel_id=1, source_target_pairs={{12,16},{13,17},{14,18},{15,19}} | collective-permute-start | bytes 1376264 | tf_op jit(solution)/shard_map/cond/branch_1_fun/ppermute | solution.py:471
  52.3 3.2 %collective-permute-done.21.refs_12_ = f32[8,128]{1,0:T(8,128)S(1)} collective-permute-done((f32[8,128]{1,0:T(8,128)S(1)}, f32[8,128]{1,0:T(8,128)S(1)}, u32[]{:S(2)}, u32[]{:S(2)}) %collective-permute-start.21) | collective-permute-done | bytes 4128 | tf_op jit(solution)/shard_map/cond/branch_1_fun/ppermute | solution.py:471
  55.5 3.2 %branch_1_fun.12 = (bf16[1,128,1792]{2,1,0:T(8,128)(2,1)S(1)}, bf16[1,128,1792]{2,1,0:T(8,128)(2,1)S(1)}, bf16[1,128,1792]{2,1,0:T(8,128)(2,1)S(1)}, bf16[1,128,1792]{2,1,0:T(8,128)(2,1)S(1)}) custom-call(s32[1]{0:T(128)} %bitcast.1.place_ref, s32[9]{0:T(128)S(1)} %get-tuple-element.57.lengths_ref, bf16[1,128,1792]{2,1,0:T(8,128)(2,1)S(1)} %copy-done.1, ...), custom_call_target="tpu_custom_call" | custom-call | flops 1409286144 | bytes 4587520 | tf_op jit(solution)/shard_map/cond/branch_1_fun/pallas_call | solution.py:486
  58.7 1.9 %collective-permute-start.23 = (bf16[1,128,1792]{2,1,0:T(8,128)(2,1)S(1)}, bf16[1,128,1792]{2,1,0:T(8,128)(2,1)S(1)}, u32[]{:S(2)}, u32[]{:S(2)}) collective-permute-start(bf16[1,128,1792]{2,1,0:T(8,128)(2,1)S(1)} %get-tuple-element.77), channel_id=1, source_target_pairs={{8,0},{12,4},{16,8},{20,12},{24,16},{28,20},{9,1},{13,5},{17,9},{2... | collective-permute-start | bytes 1376264 | tf_op jit(solution)/shard_map/cond/branch_1_fun/ppermute | solution.py:471
  60.6 1.9 %collective-permute-start.24 = (bf16[1,128,1792]{2,1,0:T(8,128)(2,1)S(1)}, bf16[1,128,1792]{2,1,0:T(8,128)(2,1)S(1)}, u32[]{:S(2)}, u32[]{:S(2)}) collective-permute-start(bf16[1,128,1792]{2,1,0:T(8,128)(2,1)S(1)} %get-tuple-element.79), channel_id=1, source_target_pairs={{0,4},{4,0},{8,12},{12,8},{16,20},{20,16},{24,28},{28,24},{1,5},{5... | collective-permute-start | bytes 1376264 | tf_op jit(solution)/shard_map/cond/branch_1_fun/ppermute | solution.py:471
  64.0 5.0 %collective-permute-done.23.key_sent = bf16[1,128,1792]{2,1,0:T(8,128)(2,1)S(1)} collective-permute-done((bf16[1,128,1792]{2,1,0:T(8,128)(2,1)S(1)}, bf16[1,128,1792]{2,1,0:T(8,128)(2,1)S(1)}, u32[]{:S(2)}, u32[]{:S(2)}) %collective-permute-start.23) | collective-permute-done | bytes 458784 | tf_op jit(solution)/shard_map/cond/branch_1_fun/ppermute | solution.py:471
  69.0 4.7 %collective-permute-done.24.refs_1_ = bf16[1,128,1792]{2,1,0:T(8,128)(2,1)S(1)} collective-permute-done((bf16[1,128,1792]{2,1,0:T(8,128)(2,1)S(1)}, bf16[1,128,1792]{2,1,0:T(8,128)(2,1)S(1)}, u32[]{:S(2)}, u32[]{:S(2)}) %collective-permute-start.24) | collective-permute-done | bytes 458784 | tf_op jit(solution)/shard_map/cond/branch_1_fun/ppermute | solution.py:471
  (26 shorter events, 12.2 us)
Async XLA Ops:
  2.0 13.7 %collective-permute-start.9 = (bf16[1,128,1792]{2,1,0:T(8,128)(2,1)}, bf16[1,128,1792]{2,1,0:T(8,128)(2,1)S(1)}, u32[]{:S(2)}, u32[]{:S(2)}) collective-permute-start(bf16[1,128,1792]{2,1,0:T(8,128)(2,1)} %get-tuple-element.130.q_own.refs_0_.q0), channel_id=1, source_target_pairs={{0,4},{4,0},{8,12},{12,8},{16,20},{20,16},{24,28},{28,24},{1,5},{5... | collective-permute-start | bytes 1376264 | tf_op jit(solution)/shard_map/cond/branch_1_fun/ppermute | solution.py:471
  3.5 15.5 %collective-permute-start.10 = (bf16[1,128,1792]{2,1,0:T(8,128)(2,1)}, bf16[1,128,1792]{2,1,0:T(8,128)(2,1)S(1)}, u32[]{:S(2)}, u32[]{:S(2)}) collective-permute-start(bf16[1,128,1792]{2,1,0:T(8,128)(2,1)} %get-tuple-element.133.k_own.refs_4_.k0), channel_id=1, source_target_pairs={{0,8},{4,12},{8,16},{12,20},{16,24},{20,28},{1,9},{5,13},{9,17},{1... | collective-permute-start | bytes 1376264 | tf_op jit(solution)/shard_map/cond/branch_1_fun/ppermute | solution.py:471
  7.0 17.5 %collective-permute-start.11 = (bf16[1,128,1792]{2,1,0:T(8,128)(2,1)}, bf16[1,128,1792]{2,1,0:T(8,128)(2,1)S(1)}, u32[]{:S(2)}, u32[]{:S(2)}) collective-permute-start(bf16[1,128,1792]{2,1,0:T(8,128)(2,1)} %get-tuple-element.136.o_own), channel_id=1, source_target_pairs={{0,4},{4,0},{8,12},{12,8},{16,20},{20,16},{24,28},{28,24},{1,5},{5... | collective-permute-start | bytes 1376264 | tf_op jit(solution)/shard_map/cond/branch_1_fun/ppermute | solution.py:471
  7.6 19.8 %collective-permute-start.12 = (bf16[1,128,1792]{2,1,0:T(8,128)(2,1)}, bf16[1,128,1792]{2,1,0:T(8,128)(2,1)S(1)}, u32[]{:S(2)}, u32[]{:S(2)}) collective-permute-start(bf16[1,128,1792]{2,1,0:T(8,128)(2,1)} %get-tuple-element.139.v_own), channel_id=1, source_target_pairs={{0,8},{4,12},{8,16},{12,20},{16,24},{20,28},{1,9},{5,13},{9,17},{1... | collective-permute-start | bytes 1376264 | tf_op jit(solution)/shard_map/cond/branch_1_fun/ppermute | solution.py:471
  15.7 11.8 %collective-permute-start.13 = (bf16[1,128,1792]{2,1,0:T(8,128)(2,1)S(1)}, bf16[1,128,1792]{2,1,0:T(8,128)(2,1)S(1)}, u32[]{:S(2)}, u32[]{:S(2)}) collective-permute-start(bf16[1,128,1792]{2,1,0:T(8,128)(2,1)S(1)} %collective-permute-done.9.q_mate.refs_2_.q1), channel_id=1, source_target_pairs={{20,12},{21,13},{22,14},{23,15}} | collective-permute-start | bytes 1376264 | tf_op jit(solution)/shard_map/cond/branch_1_fun/ppermute | solution.py:471
  21.6 13.5 %copy-start.1 = (bf16[1,128,1792]{2,1,0:T(8,128)(2,1)S(1)}, bf16[1,128,1792]{2,1,0:T(8,128)(2,1)}, u32[]{:S(2)}) copy-start(bf16[1,128,1792]{2,1,0:T(8,128)(2,1)} %get-tuple-element.130.q_own.refs_0_.q0) | copy-start | bytes 1376260
  21.6 13.5 %copy-start.4 = (bf16[1,128,1792]{2,1,0:T(8,128)(2,1)S(1)}, bf16[1,128,1792]{2,1,0:T(8,128)(2,1)}, u32[]{:S(2)}) copy-start(bf16[1,128,1792]{2,1,0:T(8,128)(2,1)} %get-tuple-element.133.k_own.refs_4_.k0) | copy-start | bytes 1376260
  21.6 3.8 %collective-permute-start.14 = (f32[32,128]{1,0:T(8,128)S(1)}, f32[32,128]{1,0:T(8,128)S(1)}, u32[]{:S(2)}, u32[]{:S(2)}) collective-permute-start(f32[32,128]{1,0:T(8,128)S(1)} %get-tuple-element.65.refs_8_), channel_id=1, source_target_pairs={{0,4},{4,0},{8,12},{12,8},{16,20},{20,16},{24,28},{28,24},{1,5},{5... | collective-permute-start | bytes 49160 | tf_op jit(solution)/shard_map/cond/branch_1_fun/ppermute | solution.py:471
  25.4 19.1 %collective-permute-start.15 = (bf16[1,128,1792]{2,1,0:T(8,128)(2,1)S(1)}, bf16[1,128,1792]{2,1,0:T(8,128)(2,1)S(1)}, u32[]{:S(2)}, u32[]{:S(2)}) collective-permute-start(bf16[1,128,1792]{2,1,0:T(8,128)(2,1)S(1)} %collective-permute-done.11.refs_3_.o1), channel_id=1, source_target_pairs={{20,12},{21,13},{22,14},{23,15}} | collective-permute-start | bytes 1376264 | tf_op jit(solution)/shard_map/cond/branch_1_fun/ppermute | solution.py:471
  28.7 6.4 %collective-permute-start.16 = (f32[16,128]{1,0:T(8,128)S(1)}, f32[16,128]{1,0:T(8,128)S(1)}, u32[]{:S(2)}, u32[]{:S(2)}) collective-permute-start(f32[16,128]{1,0:T(8,128)S(1)} %branch_1_fun.8.stats), channel_id=1, source_target_pairs={{12,16},{13,17},{14,18},{15,19}} | collective-permute-start | bytes 24584 | tf_op jit(solution)/shard_map/cond/branch_1_fun/ppermute | solution.py:471
  30.0 5.1 %collective-permute-start.17 = (f32[16,128]{1,0:T(8,128)S(1)}, f32[16,128]{1,0:T(8,128)S(1)}, u32[]{:S(2)}, u32[]{:S(2)}) collective-permute-start(f32[16,128]{1,0:T(8,128)S(1)} %branch_1_fun.8.stats), channel_id=1, source_target_pairs={{12,20},{13,21},{14,22},{15,23}} | collective-permute-start | bytes 24584 | tf_op jit(solution)/shard_map/cond/branch_1_fun/ppermute | solution.py:471
  37.3 7.3 %collective-permute-start.19 = (f32[48,128]{1,0:T(8,128)S(1)}, f32[48,128]{1,0:T(8,128)S(1)}, u32[]{:S(2)}, u32[]{:S(2)}) collective-permute-start(f32[48,128]{1,0:T(8,128)S(1)} %get-tuple-element.72), channel_id=1, source_target_pairs={{16,12},{17,13},{18,14},{19,15}} | collective-permute-start | bytes 73736 | tf_op jit(solution)/shard_map/cond/branch_1_fun/ppermute | solution.py:471
  40.2 4.4 %collective-permute-start.20 = (f32[48,128]{1,0:T(8,128)S(1)}, f32[48,128]{1,0:T(8,128)S(1)}, u32[]{:S(2)}, u32[]{:S(2)}) collective-permute-start(f32[48,128]{1,0:T(8,128)S(1)} %get-tuple-element.72), channel_id=1, source_target_pairs={{20,12},{21,13},{22,14},{23,15}} | collective-permute-start | bytes 73736 | tf_op jit(solution)/shard_map/cond/branch_1_fun/ppermute | solution.py:471
  40.8 3.7 %collective-permute-start.18 = (f32[16,128]{1,0:T(8,128)S(1)}, f32[16,128]{1,0:T(8,128)S(1)}, u32[]{:S(2)}, u32[]{:S(2)}) collective-permute-start(f32[16,128]{1,0:T(8,128)S(1)} %get-tuple-element.70.refs_10_), channel_id=1, source_target_pairs={{0,4},{4,0},{8,12},{12,8},{16,20},{20,16},{24,28},{28,24},{1,5},{5... | collective-permute-start | bytes 24584 | tf_op jit(solution)/shard_map/cond/branch_1_fun/ppermute | solution.py:471
  47.1 15.5 %collective-permute-start.26 = (bf16[1,128,1792]{2,1,0:T(8,128)(2,1)S(1)}, bf16[1,128,1792]{2,1,0:T(8,128)(2,1)S(1)}, u32[]{:S(2)}, u32[]{:S(2)}) collective-permute-start(bf16[1,128,1792]{2,1,0:T(8,128)(2,1)S(1)} %get-tuple-element.84), channel_id=1, source_target_pairs={{8,0},{12,4},{16,8},{20,12},{24,16},{28,20},{9,1},{13,5},{17,9},{2... | collective-permute-start | bytes 1376264 | tf_op jit(solution)/shard_map/cond/branch_1_fun/ppermute | solution.py:471
  49.0 6.5 %collective-permute-start.21 = (f32[8,128]{1,0:T(8,128)S(1)}, f32[8,128]{1,0:T(8,128)S(1)}, u32[]{:S(2)}, u32[]{:S(2)}) collective-permute-start(f32[8,128]{1,0:T(8,128)S(1)} %get-tuple-element.75), channel_id=1, source_target_pairs={{12,16},{13,17},{14,18},{15,19}} | collective-permute-start | bytes 12296 | tf_op jit(solution)/shard_map/cond/branch_1_fun/ppermute | solution.py:471
  50.3 5.2 %collective-permute-start.22 = (f32[8,128]{1,0:T(8,128)S(1)}, f32[8,128]{1,0:T(8,128)S(1)}, u32[]{:S(2)}, u32[]{:S(2)}) collective-permute-start(f32[8,128]{1,0:T(8,128)S(1)} %get-tuple-element.75), channel_id=1, source_target_pairs={{12,20},{13,21},{14,22},{15,23}} | collective-permute-start | bytes 12296 | tf_op jit(solution)/shard_map/cond/branch_1_fun/ppermute | solution.py:471
  51.0 13.1 %collective-permute-start.25 = (bf16[1,128,1792]{2,1,0:T(8,128)(2,1)S(1)}, bf16[1,128,1792]{2,1,0:T(8,128)(2,1)S(1)}, u32[]{:S(2)}, u32[]{:S(2)}) collective-permute-start(bf16[1,128,1792]{2,1,0:T(8,128)(2,1)S(1)} %get-tuple-element.80), channel_id=1, source_target_pairs={{12,16},{13,17},{14,18},{15,19}} | collective-permute-start | bytes 1376264 | tf_op jit(solution)/shard_map/cond/branch_1_fun/ppermute | solution.py:471
  58.7 10.4 %collective-permute-start.23 = (bf16[1,128,1792]{2,1,0:T(8,128)(2,1)S(1)}, bf16[1,128,1792]{2,1,0:T(8,128)(2,1)S(1)}, u32[]{:S(2)}, u32[]{:S(2)}) collective-permute-start(bf16[1,128,1792]{2,1,0:T(8,128)(2,1)S(1)} %get-tuple-element.77), channel_id=1, source_target_pairs={{8,0},{12,4},{16,8},{20,12},{24,16},{28,20},{9,1},{13,5},{17,9},{2... | collective-permute-start | bytes 1376264 | tf_op jit(solution)/shard_map/cond/branch_1_fun/ppermute | solution.py:471
  60.6 13.2 %collective-permute-start.24 = (bf16[1,128,1792]{2,1,0:T(8,128)(2,1)S(1)}, bf16[1,128,1792]{2,1,0:T(8,128)(2,1)S(1)}, u32[]{:S(2)}, u32[]{:S(2)}) collective-permute-start(bf16[1,128,1792]{2,1,0:T(8,128)(2,1)S(1)} %get-tuple-element.79), channel_id=1, source_target_pairs={{0,4},{4,0},{8,12},{12,8},{16,20},{20,16},{24,28},{28,24},{1,5},{5... | collective-permute-start | bytes 1376264 | tf_op jit(solution)/shard_map/cond/branch_1_fun/ppermute | solution.py:471
